TPU v7x, 32 devices: a whole 2x2x4 slice. The times are simulated.
32 devices in a mesh: seq: 16 (over z, x, core), head: 2 (over y).
Axes of the slice: x: 2, y: 2, z: 4, core: 2. Of those that a mesh axis runs over, the one named last changes fastest.
Arguments:
- query_states: bfloat16 [2048, 2048], P('seq', 'head'), may hold values from -24.5 to 24.5
- key_states: bfloat16 [2048, 512], P('seq', 'head'), may hold values from -10.5 to 10.5
- value_states: bfloat16 [2048, 512], P('seq', 'head'), may hold values from -6 to 6
- out_weight: bfloat16 [2048, 4096], P('head'), may hold values from -0.125 to 0.125
- block_docs: int32 [16], replicated, may hold values from 0 to 7, never falling along the last dimension, each value on 1 to 4 neighbouring positions
Outputs:
- mixed: bfloat16 [2048, 4096], P('seq', 'head')
Inputs may be any that keep to these rules, and one draw needn't show every extreme that they name: `block_docs`: A document spans at most 4 blocks.
All inputs are finite; a program needn't handle non-finite values.
Results may differ from a plain program's by a relative error of at most 0.0095.
Values may be sent and summed in bfloat16 or wider, within the bound.
No kernel may reach another device: no remote copies, remote signals or barrier semaphores. Data moves between devices by JAX's collectives and lax.ppermute only.
A program may use at most 64 MiB of HBM per device.

v0:
```python
import jax
import jax.numpy as jnp
from jax import lax
from jax.sharding import PartitionSpec as P

HD = 128
QH = 16
KH = 4
BLK = 128
DOC_BLK = 32


def passed_along(value, axis, steps):
    count = lax.axis_size(axis)
    initial, last = (max(0, -steps), min(count, count - steps))
    return lax.ppermute(value, axis, [(source, source + steps) for source in range(initial, last)])


def local(query_states, key_states, value_states, out_weight, block_docs):
    tokens_here = query_states.shape[0]
    kv_local = key_states.shape[1] // HD
    group_size = QH // KH
    block_count = block_docs.shape[0]
    blocks_here = tokens_here // BLK
    longest = min(DOC_BLK, block_count // 4)
    reach = (longest - 1 + blocks_here - 1) // blocks_here
    position = lax.axis_index("seq")
    score_scale = 1.0 / HD**0.5
    token_docs = jnp.repeat(block_docs, BLK, total_repeat_length=block_count * BLK)
    my_docs = lax.dynamic_slice_in_dim(token_docs, position * tokens_here, tokens_here, 0)
    query_blocks = query_states.reshape(tokens_here, kv_local, group_size, HD)
    query_pos = position * tokens_here + jnp.arange(tokens_here, dtype=jnp.int32)

    def absorb(state_now, offset, key_shard, value_shard):
        source = position - offset
        key_docs = lax.dynamic_slice_in_dim(
            token_docs, jnp.maximum(source, 0) * tokens_here, tokens_here, 0
        )
        key_pos = source * tokens_here + jnp.arange(tokens_here, dtype=jnp.int32)
        allowed = (
            (my_docs[:, None] == key_docs[None, :])
            & (key_pos[None, :] <= query_pos[:, None])
            & (source >= 0)
        )
        running_max, total, accumulated = state_now
        scores = (
            jnp.einsum(
                "xknv,jkv->knxj",
                query_blocks,
                key_shard.reshape(tokens_here, kv_local, HD),
                preferred_element_type=jnp.float32,
            )
            * score_scale
        )
        scores = jnp.where(allowed, scores, jnp.float32(-1e30))
        new_max = jnp.maximum(running_max, jnp.max(scores, axis=-1))
        weights = jnp.where(allowed, jnp.exp(scores - new_max[..., None]), jnp.float32(0.0))
        factor = jnp.exp(running_max - new_max)
        total = total * factor + jnp.sum(weights, axis=-1)
        product = jnp.einsum(
            "qnuh,hqm->qnum",
            weights.astype(jnp.bfloat16),
            value_shard.reshape(tokens_here, kv_local, HD),
            preferred_element_type=jnp.float32,
        )
        accumulated = accumulated * factor[..., None] + product
        return (new_max, total, accumulated)

    initial = (
        jnp.full((kv_local, group_size, tokens_here), -1e30, jnp.float32),
        jnp.zeros((kv_local, group_size, tokens_here), jnp.float32),
        jnp.zeros((kv_local, group_size, tokens_here, HD), jnp.float32),
    )
    state_now = absorb(initial, 0, key_states, value_states)
    kv_pair = jnp.stack([key_states, value_states])
    plan_steps = []
    have_count = 1
    while have_count < reach + 1:
        send_count = min(have_count, reach + 1 - have_count)
        plan_steps.append((have_count, send_count))
        have_count = have_count + send_count
    held = kv_pair[None]
    for have_count, send_count in plan_steps:
        arrived = passed_along(held, "seq", have_count)
        held = jnp.concatenate([arrived, held], axis=0)

    def absorb_held(index, current):
        pair_now = lax.dynamic_index_in_dim(held, index, 0, keepdims=False)
        return absorb(current, reach - index, pair_now[0], pair_now[1])

    state_now = lax.fori_loop(0, reach, absorb_held, state_now)
    running_max, total, accumulated = state_now
    attended = (accumulated / total[..., None]).astype(jnp.bfloat16)
    attended = attended.transpose(2, 0, 1, 3).reshape(tokens_here, kv_local * group_size * HD)
    partial_terms = jnp.dot(attended, out_weight, preferred_element_type=jnp.float32)
    return lax.psum_scatter(
        partial_terms.astype(jnp.bfloat16), "head", scatter_dimension=1, tiled=True
    )


def solution(mesh):
    return jax.shard_map(
        local,
        mesh=mesh,
        in_specs=(P("seq", "head"), P("seq", "head"), P("seq", "head"), P("head", None), P()),
        out_specs=P("seq", "head"),
        check_vma=False,
    )
```

profile of v0, /device:TPU:0, one launch (start us, length us, event | category | flops | bytes accessed | tf_op | source)
XLA Modules:
  0.0 75.2 jit_solution(16518024142042043830)
XLA Ops:
  6.5 0.0 reduce-scatter.2.cloned.1.call-start
  6.5 0.9 %copy.18 = bf16[128,256]{0,1:T(8,128)(2,1)S(1)} copy(bf16[128,256]{1,0:T(8,128)(2,1)} %param.10) | data formatting | bytes 131072 | tf_op args[1]
  7.5 1.0 %copy.19 = bf16[128,256]{0,1:T(8,128)(2,1)S(1)} copy(bf16[128,256]{1,0:T(8,128)(2,1)} %param.11) | data formatting | bytes 131072 | tf_op args[2]
  8.5 2.4 %collective-permute-start = (bf16[1,2,128,256]{2,3,1,0:T(8,128)(2,1)S(1)}, bf16[1,2,128,256]{2,3,1,0:T(8,128)(2,1)S(1)}, u32[]{:S(2)}, u32[]{:S(2)}) collective-permute-start(bf16[1,2,128,256]{2,3,1,0:T(8,128)(2,1)S(1)} %maximum_bitcast_fusion), channel_id=1, source_target_pairs={{0,2},{2,4},{4,6},{6,8},{8,10},{10,12},{12,14},{14,16},{16,18},{18... | collective-permute-start | bytes 393224 | tf_op jit(solution)/shard_map/ppermute | solution.py:16
  10.9 0.9 %reshape.123 = bf16[128,2,128]{2,1,0:T(2,128)(2,1)S(1)} reshape(bf16[128,256]{1,0:T(8,128)(2,1)} %param.10) | data formatting | bytes 131072 | tf_op jit(solution)/shard_map/reshape | solution.py:50
  11.8 1.9 %fusion.27 = (s32[1]{0:T(128)}, s32[1]{0:T(128)}, s32[1]{0:T(128)}, s32[1]{0:T(128)}, s32[1]{0:T(128)}, /*index=5*/s32[1]{0:T(128)}, s32[1]{0:T(128)}, s32[1]{0:...) fusion(s32[16]{0:T(128)} %param.13), kind=kLoop, calls=%fused_computation.65 | loop fusion | bytes 128 | tf_op jit(solution)/shard_map/jit(_take)/gather | solution.py:29
  13.7 4.3 %compare_select_fusion.1 = (s32[2048,1]{0,1:T(1,128)S(1)}, s32[2048,1]{0,1:T(1,128)S(1)}) fusion(s32[]{:T(128)} %bitcast.13, s32[]{:T(128)} %bitcast.14, s32[]{:T(128)} %bitcast.15, s32[]{:T(128)} %bitcast.16, s32[]{:T(128)} %bitcast.17, s32[]{:T(128)} %bitcast.19, s32[]{:T(128)} %bitcast.18, s32[2048,1]{0,1:T(1,128)S(1)} %bitcast.106, ...), kind=kLoop, calls=%fused_computation.47 | loop fusion | flops 28672 | bytes 32796 | tf_op jit(solution)/shard_map/jit(_take)/gather | solution.py:29
  18.1 0.2 compare_reduce_fusion.8
  18.3 1.1 %copy.13 = bf16[128,1024]{0,1:T(8,128)(2,1)S(1)} copy(bf16[128,1024]{1,0:T(8,128)(2,1)} %param.9) | data formatting | bytes 524288 | tf_op args[0]
  19.4 5.6 %select_select_fusion = s32[2048]{0:T(1024)S(1)} fusion(pred[2048]{0:T(1024)(128)(4,1)S(1)} %get-tuple-element.230, pred[2048]{0:T(1024)(128)(4,1)S(1)} %get-tuple-element.229, pred[2048]{0:T(1024)(128)(4,1)S(1)} %get-tuple-element.228, pred[2048]{0:T(1024)(128)(4,1)S(1)} %get-tuple-element.227, pred[2048]{0:T(1024)(128)(4,1)S(1)} %get-tuple-element.226, ...), kind=kLoop, calls=%fused_computation.54 | loop fusion | flops 36864 | bytes 34852 | tf_op jit(solution)/shard_map/jit(_take)/select_n | solution.py:29
  25.0 0.1 fusion.26
  25.1 0.1 and_and_fusion.1
  25.2 0.2 fusion.28
  25.5 0.1 fusion.14
  25.6 0.0 collective-permute-done
  25.6 4.4 %collective-permute-start.1 = (bf16[2,2,128,256]{2,3,1,0:T(8,128)(2,1)S(1)}, bf16[2,2,128,256]{2,3,1,0:T(8,128)(2,1)S(1)}, u32[]{:S(2)}, u32[]{:S(2)}) collective-permute-start(bf16[2,2,128,256]{2,3,1,0:T(8,128)(2,1)S(1)} %pad_maximum_fusion.1), channel_id=1, source_target_pairs={{0,4},{2,6},{4,8},{6,10},{8,12},{10,14},{12,16},{14,18},{16,20},{1... | collective-permute-start | bytes 786440 | tf_op jit(solution)/shard_map/ppermute | solution.py:16
  30.1 0.9 %reshape.125 = bf16[128,2,128]{2,1,0:T(2,128)(2,1)S(1)} reshape(bf16[128,256]{1,0:T(8,128)(2,1)} %param.11) | data formatting | bytes 131072 | tf_op jit(solution)/shard_map/reshape | solution.py:63
  31.0 0.2 copy.20
  31.1 0.3 convolution_add_fusion.1
  31.5 4.6 %collective-permute-done.1 = bf16[2,2,128,256]{2,3,1,0:T(8,128)(2,1)S(1)} collective-permute-done((bf16[2,2,128,256]{2,3,1,0:T(8,128)(2,1)S(1)}, bf16[2,2,128,256]{2,3,1,0:T(8,128)(2,1)S(1)}, u32[]{:S(2)}, u32[]{:S(2)}) %collective-permute-start.1) | collective-permute-done | bytes 262176 | tf_op jit(solution)/shard_map/ppermute | solution.py:16
  36.1 0.1 pad_maximum_fusion
  36.2 3.5 %while.19 = (s32[]{:T(128)}, f32[2,4,128]{2,1,0:T(4,128)S(1)}, f32[2,4,128]{2,1,0:T(4,128)S(1)}, f32[2,4,128,128]{3,2,1,0:T(8,128)S(1)}, s32[128]{0:T(128)S(1)},...) while((s32[]{:T(128)}, f32[2,4,128]{2,1,0:T(4,128)S(1)}, ...), condition=%wide.region_5.6_spmd.clone, body=%wide.region_2.5_spmd.clone.sunk | while | flops 68618512 | bytes 3412261 | solution.py:91
  36.2 0.1 dynamic_slice.28
  36.3 0.1 and_and_fusion.3
  36.4 0.3 fusion.45
  36.7 0.1 fusion.46
  36.8 0.5 convolution_add_fusion.3
  37.3 0.1 dynamic_slice.28
  37.4 0.1 and_and_fusion.3
  37.6 0.3 fusion.45
  37.9 0.1 fusion.46
  38.0 0.5 convolution_add_fusion.3
  38.5 0.1 dynamic_slice.28
  38.6 0.1 and_and_fusion.3
  38.7 0.3 fusion.45
  39.0 0.1 fusion.46
  39.2 0.5 convolution_add_fusion.3
  39.6 0.2 copy.21
  39.8 0.1 divide_convert_fusion
  39.9 5.7 %convolution_convert_fusion = bf16[128,4096]{1,0:T(8,128)(2,1)} fusion(bf16[128,1024]{0,1:T(8,128)(2,1)S(1)} %bitcast.94, bf16[1024,4096]{1,0:T(8,128)(2,1)} %param.12), kind=kOutput, calls=%fused_computation.19 | convolution fusion | flops 1074266112 | bytes 9699328 | tf_op jit(solution)/shard_map/dot_general | solution.py:95
  45.6 0.0 reduce-scatter.2.cloned.1.call-update
  45.6 22.8 %reduce-scatter.2.cloned.1.call-done = bf16[128,2048]{1,0:T(8,128)(2,1)} async-done(((bf16[128,4096]{1,0:T(8,128)(2,1)}), bf16[128,2048]{1,0:T(8,128)(2,1)}) %reduce-scatter.2.cloned.1.call-update) | async-done | bytes 524304 | tf_op jit(solution)/shard_map/reduce_scatter | solution.py:96
  (22 shorter events, 0.2 us)
Async XLA Ops:
  6.5 61.9 %reduce-scatter.2.cloned.1.call-start = ((), (), s32[]{:S(2)}) async-start(), calls=%async_computation.1 | async-start | bytes 1572864 | tf_op jit(solution)/shard_map/reduce_scatter | solution.py:96
  8.5 17.1 %collective-permute-start = (bf16[1,2,128,256]{2,3,1,0:T(8,128)(2,1)S(1)}, bf16[1,2,128,256]{2,3,1,0:T(8,128)(2,1)S(1)}, u32[]{:S(2)}, u32[]{:S(2)}) collective-permute-start(bf16[1,2,128,256]{2,3,1,0:T(8,128)(2,1)S(1)} %maximum_bitcast_fusion), channel_id=1, source_target_pairs={{0,2},{2,4},{4,6},{6,8},{8,10},{10,12},{12,14},{14,16},{16,18},{18... | collective-permute-start | bytes 393224 | tf_op jit(solution)/shard_map/ppermute | solution.py:16
  25.6 10.5 %collective-permute-start.1 = (bf16[2,2,128,256]{2,3,1,0:T(8,128)(2,1)S(1)}, bf16[2,2,128,256]{2,3,1,0:T(8,128)(2,1)S(1)}, u32[]{:S(2)}, u32[]{:S(2)}) collective-permute-start(bf16[2,2,128,256]{2,3,1,0:T(8,128)(2,1)S(1)} %pad_maximum_fusion.1), channel_id=1, source_target_pairs={{0,4},{2,6},{4,8},{6,10},{8,12},{10,14},{12,16},{14,18},{16,20},{1... | collective-permute-start | bytes 786440 | tf_op jit(solution)/shard_map/ppermute | solution.py:16
Sparse Core Ops, SparseCore 0:
  45.7 22.6 reduce-scatter.1
where the time goes:
time: 75.8 us; the launch traced here: 75.2 us
  waiting for transfers between devices  27.5 us (36%)
  between operations  13.6 us (18%)
  other arithmetic  11.3 us (15%)
  matrix products  8.47 us (11%)
  local copies, waits for them, and re-layouts  7.45 us (10%)
  starting transfers between devices  6.78 us (9%)
    reduce_scatter x1, waiting for transfers between devices, local(): lax.psum_scatter(partial_terms.astype(jnp.bfloat16), 'head', scatter_dime...  22.8 us
    ppermute x2, starting transfers between devices, passed_along(): lax.ppermute(value, axis, [(source, source + steps) for source in range(i...  6.78 us
    dot_general x1, matrix products, local(): jnp.dot(attended, out_weight, preferred_element_type=jnp.float32)  5.67 us
    select_n x1, other arithmetic, local(): jnp.repeat(block_docs, BLK, total_repeat_length=block_count * BLK)  5.64 us
    ppermute x2, waiting for transfers between devices, passed_along(): lax.ppermute(value, axis, [(source, source + steps) for source in range(i...  4.64 us
    gather x2, other arithmetic, local(): jnp.repeat(block_docs, BLK, total_repeat_length=block_count * BLK)  4.55 us
    unnamed x4, local copies, waits for them, and re-layouts  3.2 us
    gather x1, local copies, waits for them, and re-layouts, local(): jnp.repeat(block_docs, BLK, total_repeat_length=block_count * BLK)  1.95 us
  transfers between devices with their start and end apart: 3, of which 2 were waited for; matrix products, arithmetic and copies ran while one was open for 21% of the time, Pallas kernels for 0%

commit v1 on v0

v1 whole, which is shorter than its diff:
```python
import functools
import jax
import jax.numpy as jnp
from jax import lax
from jax.experimental import pallas as pl
from jax.experimental.pallas import tpu as pltpu
from jax.sharding import PartitionSpec as P

HD = 128
QH = 16
KH = 4
BLK = 128
DOC_BLK = 32
PARTS = 4
ROUND = 4
LOG2E = 1.4426950408889634
MIB = 1024 * 1024
VMEM = pl.BlockSpec(memory_space=pltpu.VMEM)
SMEM = pl.BlockSpec(memory_space=pltpu.SMEM)
ANY = pl.BlockSpec(memory_space=pl.ANY)


def cost(flops, bytes_accessed):
    return pl.CostEstimate(flops=flops, bytes_accessed=bytes_accessed, transcendentals=0)


def turned(value, axis, steps):
    count = lax.axis_size(axis)
    return lax.ppermute(value, axis, [(source, (source + steps) % count) for source in range(count)])


def stage_kernel(q_ref, w_ref, q_out, w_out, sems):
    groups, _, columns = w_out.shape
    group = lax.axis_index("head")
    copies = [pltpu.make_async_copy(q_ref, q_out, sems.at[groups])]
    for step in range(groups):
        target = lax.rem(group + step, groups)
        columns_of = pl.ds(pl.multiple_of(target * columns, 128), columns)
        copies.append(pltpu.make_async_copy(w_ref.at[:, columns_of], w_out.at[step], sems.at[step]))
    for copy in copies:
        copy.start()
    for copy in copies:
        copy.wait()


def stage(query_states, out_weight, groups):
    rows, columns = out_weight.shape
    return pl.pallas_call(
        stage_kernel,
        out_shape=(
            jax.ShapeDtypeStruct(query_states.shape, jnp.bfloat16),
            jax.ShapeDtypeStruct((groups, rows, columns // groups), jnp.bfloat16),
        ),
        in_specs=[ANY, ANY],
        out_specs=(VMEM, VMEM),
        scratch_shapes=[pltpu.SemaphoreType.DMA((groups + 1,))],
        compiler_params=pltpu.CompilerParams(vmem_limit_bytes=24 * MIB),
        cost_estimate=cost(0, 2 * out_weight.size * 2),
    )(query_states, out_weight)


def attend_kernel(blocks, kv_local, group_size, docs_ref, q_ref, *refs):
    kv_refs, w_ref, out_ref, part_ref = refs[:blocks], refs[blocks], refs[blocks + 1], refs[blocks + 2]
    width = kv_local * HD
    scale = jnp.float32(LOG2E / HD**0.5)
    position = lax.axis_index("seq")
    doc = docs_ref[position]
    near = [None]
    for offset in range(1, blocks):
        source = jnp.maximum(position - offset, 0)
        near.append((docs_ref[source] == doc) & (position >= offset))
    row = lax.broadcasted_iota(jnp.int32, (BLK, BLK), 0)
    column = lax.broadcasted_iota(jnp.int32, (BLK, BLK), 1)
    causal = jnp.concatenate([column <= row] * group_size, axis=0)
    for kv_head in range(kv_local):
        first = kv_head * group_size
        queries = jnp.concatenate(
            [q_ref[:, (first + g) * HD : (first + g + 1) * HD] for g in range(group_size)], axis=0
        )
        top = total = summed = None
        for start in range(0, blocks, ROUND):
            offsets = range(start, min(start + ROUND, blocks))
            scores = []
            for offset in offsets:
                keys = kv_refs[offset][:, kv_head * HD : (kv_head + 1) * HD]
                part = lax.dot_general(
                    queries, keys, (((1,), (1,)), ((), ())), preferred_element_type=jnp.float32
                )
                allowed = causal if offset == 0 else near[offset]
                scores.append(jnp.where(allowed, part, jnp.float32(-1e30)))
            largest = functools.reduce(jnp.maximum, scores)
            new_top = jnp.max(largest, axis=1, keepdims=True)
            if start:
                new_top = jnp.maximum(top, new_top)
            weights = [jnp.exp2((part - new_top) * scale) for part in scores]
            new_total = jnp.sum(functools.reduce(jnp.add, weights), axis=1, keepdims=True)
            values = jnp.concatenate(
                [
                    kv_refs[offset][:, width + kv_head * HD : width + (kv_head + 1) * HD]
                    for offset in offsets
                ],
                axis=0,
            )
            product = jnp.dot(
                jnp.concatenate([w.astype(jnp.bfloat16) for w in weights], axis=1),
                values,
                preferred_element_type=jnp.float32,
            )
            if start:
                factor = jnp.exp2((top - new_top) * scale)
                new_total = new_total + total * factor
                product = product + summed * factor
            top, total, summed = new_top, new_total, product
        attended = (summed / total).astype(jnp.bfloat16)
        for g in range(group_size):
            out_ref[:, (first + g) * HD : (first + g + 1) * HD] = attended[g * BLK : (g + 1) * BLK]
    width = part_ref.shape[1]
    part_ref[...] = jnp.dot(
        out_ref[...], w_ref[min(1, w_ref.shape[0] - 1), :, :width], preferred_element_type=jnp.float32
    ).astype(jnp.bfloat16)


def attend(docs, query_states, kv_blocks, weights, kv_local, group_size, width):
    return pl.pallas_call(
        functools.partial(attend_kernel, len(kv_blocks), kv_local, group_size),
        out_shape=(
            jax.ShapeDtypeStruct(query_states.shape, jnp.bfloat16),
            jax.ShapeDtypeStruct((BLK, width), jnp.bfloat16),
        ),
        in_specs=[SMEM] + [VMEM] * (2 + len(kv_blocks)),
        out_specs=(VMEM, VMEM),
        compiler_params=pltpu.CompilerParams(vmem_limit_bytes=32 * MIB),
        cost_estimate=cost(600_000_000, 2_000_000),
    )(docs, query_states, *kv_blocks, weights)


def project_kernel(step, width, a_ref, w_ref, *out_refs):
    first = w_ref.shape[2] - width * len(out_refs)
    for i, out_ref in enumerate(out_refs):
        out_ref[...] = jnp.dot(
            a_ref[...],
            w_ref[step, :, first + i * width : first + (i + 1) * width],
            preferred_element_type=jnp.float32,
        ).astype(jnp.bfloat16)


def project(attended, weights, step, width, count):
    return pl.pallas_call(
        functools.partial(project_kernel, step, width),
        out_shape=[jax.ShapeDtypeStruct((BLK, width), jnp.bfloat16)] * count,
        in_specs=[VMEM, VMEM],
        out_specs=[VMEM] * count,
        compiler_params=pltpu.CompilerParams(vmem_limit_bytes=24 * MIB),
        cost_estimate=cost(2 * BLK * width * count * attended.shape[1], 1_000_000),
    )(attended, weights)


def local(query_states, key_states, value_states, out_weight, block_docs):
    tokens_here = query_states.shape[0]
    kv_local = key_states.shape[1] // HD
    group_size = QH // KH
    block_count = block_docs.shape[0]
    groups = lax.axis_size("head")
    assert tokens_here == BLK and block_count == lax.axis_size("seq")
    reach = min(DOC_BLK, block_count // 4) - 1

    kv = jnp.concatenate([key_states, value_states], axis=1)
    if reach <= 3:
        kv_blocks = [kv] + [turned(kv, "seq", offset) for offset in range(reach, 0, -1)][::-1]
    else:
        kv_blocks = [kv]
        while len(kv_blocks) < reach + 1:
            have = len(kv_blocks)
            send = min(have, reach + 1 - have)
            arrived = turned(jnp.stack(kv_blocks[:send]), "seq", have)
            kv_blocks = kv_blocks + [arrived[i] for i in range(send)]

    queries, weights = stage(query_states, out_weight, groups)
    width = out_weight.shape[1] // groups // PARTS
    attended, first = attend(block_docs, queries, kv_blocks, weights, kv_local, group_size, width)

    received = []
    for step in range(1, groups):
        if step == 1:
            row = [first] + list(project(attended, weights, 1, width, PARTS - 1))
        else:
            row = list(project(attended, weights, step, width, PARTS))
        received.append([turned(partial, "head", step) for partial in row])
    mine = project(attended, weights, 0, width, PARTS)
    outs = []
    for i in range(PARTS):
        total = mine[i].astype(jnp.float32)
        for row in received:
            total = total + row[i].astype(jnp.float32)
        outs.append(total.astype(jnp.bfloat16))
    return jnp.concatenate(outs, axis=1)


def solution(mesh):
    return jax.shard_map(
        local,
        mesh=mesh,
        in_specs=(P("seq", "head"), P("seq", "head"), P("seq", "head"), P("head", None), P()),
        out_specs=P("seq", "head"),
        check_vma=False,
    )
```

time: 75.8 us -> 30.1 us (0.40)
  waiting for transfers between devices: 27.5 us -> 8.62 us
  between operations: 13.6 us -> 0.1 us
  other arithmetic: 11.3 us -> 0.98 us
  matrix products: 8.47 us -> 0 us
  Pallas kernels: 0 us -> 4.45 us
  starting transfers between devices: 6.78 us -> 9.59 us
  local copies, waits for them, and re-layouts: 7.45 us -> 6.04 us
    reduce_scatter x1 -> x0, waiting for transfers between devices: 22.8 us -> none  [local(): lax.psum_scatter(partial_terms.astype(jnp.bfloat16), 'head', scatter_dime...]
    dot_general x9 -> x0, matrix products: 8.47 us -> none  [the longest x1 5.67 us: local(): jnp.dot(attended, out_weight, preferred_element_type=jnp.float32)]
    select_n x1 -> x0, other arithmetic: 5.64 us -> none  [local(): jnp.repeat(block_docs, BLK, total_repeat_length=block_count * BLK)]
    gather x2 -> x0, other arithmetic: 4.55 us -> none  [local(): jnp.repeat(block_docs, BLK, total_repeat_length=block_count * BLK)]
    pallas_call x0 -> x4, Pallas kernels: none -> 4.45 us  [the longest x1 2 us: attend(): pl.pallas_call(functools.partial(attend_kernel, len(kv_blocks), kv_local,...]
    ppermute x2 -> x7, waiting for transfers between devices: 4.64 us -> 8.62 us  [turned(): lax.ppermute(value, axis, [(source, (source + steps) % count) for source...]
    ppermute x2 -> x7, starting transfers between devices: 6.78 us -> 9.59 us  [turned(): lax.ppermute(value, axis, [(source, (source + steps) % count) for source...]
    unnamed x4 -> x7, local copies, waits for them, and re-layouts: 3.2 us -> 5.19 us
  transfers between devices with their start and end apart: 3 -> 7, of which waited for: 2 -> 3; matrix products, arithmetic and copies ran while one was open for 21% -> 0% of each run, Pallas kernels for 0% -> 8%
where the time goes in v1:
time: 30.1 us; the launch traced here: 29.8 us
  starting transfers between devices  9.59 us (32%)
  waiting for transfers between devices  8.62 us (29%)
  local copies, waits for them, and re-layouts  6.04 us (20%)
  Pallas kernels  4.45 us (15%)
  other arithmetic  0.98 us (3%)
    ppermute x7, starting transfers between devices, turned(): lax.ppermute(value, axis, [(source, (source + steps) % count) for source...  9.59 us
    ppermute x7, waiting for transfers between devices, turned(): lax.ppermute(value, axis, [(source, (source + steps) % count) for source...  8.62 us
    unnamed x7, local copies, waits for them, and re-layouts  5.19 us
    pallas_call x1, Pallas kernels, attend(): pl.pallas_call(functools.partial(attend_kernel, len(kv_blocks), kv_local,...  2 us
    pallas_call x2, Pallas kernels, project(): pl.pallas_call(functools.partial(project_kernel, step, width), out_shape=...  1.32 us
    pallas_call x1, Pallas kernels, stage(): pl.pallas_call(stage_kernel, out_shape=(jax.ShapeDtypeStruct(query_states...  1.14 us
    concatenate x1, other arithmetic, local(): return jnp.concatenate(outs, axis=1)  0.85 us
    concatenate x1, local copies, waits for them, and re-layouts, local(): kv = jnp.concatenate([key_states, value_states], axis=1)  0.84 us
  transfers between devices with their start and end apart: 7, of which 3 were waited for; matrix products, arithmetic and copies ran while one was open for 0% of the time, Pallas kernels for 8%

profile of v1, /device:TPU:0, one launch (start us, length us, event | category | flops | bytes accessed | tf_op | source)
XLA Modules:
  0.0 29.8 jit_solution(8945209240651289506)
XLA Ops:
  0.0 0.0 copy-start.2
  0.0 0.9 %constant_dynamic-update-slice_fusion.1 = bf16[128,512]{1,0:T(8,128)(2,1)S(1)} fusion(bf16[128,256]{1,0:T(8,128)(2,1)} %param.6), kind=kLoop, calls=%fused_computation.6 | loop fusion | bytes 131072
  0.9 0.8 %constant_dynamic-update-slice_fusion.refs_0_ = bf16[128,512]{1,0:T(8,128)(2,1)S(1)} fusion(bf16[128,512]{1,0:T(8,128)(2,1)S(1)} %constant_dynamic-update-slice_fusion.1, bf16[128,256]{1,0:T(8,128)(2,1)} %param.7), kind=kLoop, calls=%fused_computation.5 | loop fusion | bytes 131072 | tf_op jit(solution)/shard_map/concatenate | solution.py:167
  1.7 0.5 %collective-permute-start = (bf16[128,512]{1,0:T(8,128)(2,1)S(1)}, bf16[128,512]{1,0:T(8,128)(2,1)S(1)}, u32[]{:S(2)}, u32[]{:S(2)}) collective-permute-start(bf16[128,512]{1,0:T(8,128)(2,1)S(1)} %constant_dynamic-update-slice_fusion.refs_0_), channel_id=1, source_target_pairs={{0,2},{2,4},{4,6},{6,8},{8,10},{10,12},{12,14},{14,16},{16,18},{18... | collective-permute-start | bytes 393224 | tf_op jit(solution)/shard_map/ppermute | solution.py:29
  2.2 2.5 %collective-permute-start.1 = (bf16[128,512]{1,0:T(8,128)(2,1)S(1)}, bf16[128,512]{1,0:T(8,128)(2,1)S(1)}, u32[]{:S(2)}, u32[]{:S(2)}) collective-permute-start(bf16[128,512]{1,0:T(8,128)(2,1)S(1)} %constant_dynamic-update-slice_fusion.refs_0_), channel_id=1, source_target_pairs={{0,4},{2,6},{4,8},{6,10},{8,12},{10,14},{12,16},{14,18},{16,20},{1... | collective-permute-start | bytes 393224 | tf_op jit(solution)/shard_map/ppermute | solution.py:29
  4.7 2.4 %collective-permute-start.2 = (bf16[128,512]{1,0:T(8,128)(2,1)S(1)}, bf16[128,512]{1,0:T(8,128)(2,1)S(1)}, u32[]{:S(2)}, u32[]{:S(2)}) collective-permute-start(bf16[128,512]{1,0:T(8,128)(2,1)S(1)} %constant_dynamic-update-slice_fusion.refs_0_), channel_id=1, source_target_pairs={{0,6},{2,8},{4,10},{6,12},{8,14},{10,16},{12,18},{14,20},{16,22},{... | collective-permute-start | bytes 393224 | tf_op jit(solution)/shard_map/ppermute | solution.py:29
  7.1 0.0 copy-start
  7.1 3.4 %copy-done = bf16[1024,4096]{1,0:T(8,128)(2,1)S(1)} copy-done((bf16[1024,4096]{1,0:T(8,128)(2,1)S(1)}, bf16[1024,4096]{1,0:T(8,128)(2,1)}, u32[]{:S(2)}) %copy-start) | copy-done | bytes 8388632
  10.5 0.0 copy-start.1
  10.5 0.9 %copy-done.1 = bf16[128,1024]{1,0:T(8,128)(2,1)S(1)} copy-done((bf16[128,1024]{1,0:T(8,128)(2,1)S(1)}, bf16[128,1024]{1,0:T(8,128)(2,1)}, u32[]{:S(2)}) %copy-start.1) | copy-done | bytes 262168
  11.5 1.1 %shard_map.55 = (bf16[128,1024]{1,0:T(8,128)(2,1)S(1)}, bf16[2,1024,2048]{2,1,0:T(8,128)(2,1)S(1)}) custom-call(bf16[128,1024]{1,0:T(8,128)(2,1)S(1)} %copy-done.1, bf16[1024,4096]{1,0:T(8,128)(2,1)S(1)} %copy-done), custom_call_target="tpu_custom_call" | custom-call | bytes 16777216 | tf_op jit(solution)/shard_map/pallas_call | solution.py:48
  12.6 0.0 collective-permute-done.refs_1_
  12.6 0.0 collective-permute-done.1.refs_2_
  12.6 0.0 collective-permute-done.2.refs_3_
  12.6 0.0 copy-done.2
  12.6 2.0 %shard_map.56 = (bf16[128,1024]{1,0:T(8,128)(2,1)S(1)}, bf16[128,512]{1,0:T(8,128)(2,1)S(1)}) custom-call(s32[16]{0:T(128)S(1)} %copy-done.2, bf16[128,1024]{1,0:T(8,128)(2,1)S(1)} %get-tuple-element.16.q_ref, bf16[128,512]{1,0:T(8,128)(2,1)S(1)} %constant_dynamic-update-slice_fusion.refs_0_, bf16[128,512]{1,0:T(8,128)(2,1)S(1)} %collective-permute-done.refs_1_, ...), custom_call_target="tpu_custom_call" | custom-call | flops 600000000 | bytes 2000000 | tf_op jit(solution)/shard_map/pallas_call | solution.py:124
  14.6 1.6 %collective-permute-start.3 = (bf16[128,512]{1,0:T(8,128)(2,1)S(1)}, bf16[128,512]{1,0:T(8,128)(2,1)S(1)}, u32[]{:S(2)}, u32[]{:S(2)}) collective-permute-start(bf16[128,512]{1,0:T(8,128)(2,1)S(1)} %get-tuple-element.20), channel_id=1, source_target_pairs={{0,1},{1,0},{2,3},{3,2},{4,5},{5,4},{6,7},{7,6},{8,9},{9,8},{10,11... | collective-permute-start | bytes 393224 | tf_op jit(solution)/shard_map/ppermute | solution.py:29
  16.2 0.6 %shard_map.58 = (bf16[128,512]{1,0:T(8,128)(2,1)S(1)}, bf16[128,512]{1,0:T(8,128)(2,1)S(1)}, bf16[128,512]{1,0:T(8,128)(2,1)S(1)}) custom-call(bf16[128,1024]{1,0:T(8,128)(2,1)S(1)} %get-tuple-element.18.a_ref, bf16[2,1024,2048]{2,1,0:T(8,128)(2,1)S(1)} %get-tuple-element.17.refs_4_.w_ref), custom_call_target="tpu_custom_call" | custom-call | flops 402653184 | bytes 1000000 | tf_op jit(solution)/shard_map/pallas_call | solution.py:148
  16.8 0.6 %collective-permute-start.4 = (bf16[128,512]{1,0:T(8,128)(2,1)S(1)}, bf16[128,512]{1,0:T(8,128)(2,1)S(1)}, u32[]{:S(2)}, u32[]{:S(2)}) collective-permute-start(bf16[128,512]{1,0:T(8,128)(2,1)S(1)} %get-tuple-element.22), channel_id=1, source_target_pairs={{0,1},{1,0},{2,3},{3,2},{4,5},{5,4},{6,7},{7,6},{8,9},{9,8},{10,11... | collective-permute-start | bytes 393224 | tf_op jit(solution)/shard_map/ppermute | solution.py:29
  17.4 1.5 %collective-permute-start.5 = (bf16[128,512]{1,0:T(8,128)(2,1)S(1)}, bf16[128,512]{1,0:T(8,128)(2,1)S(1)}, u32[]{:S(2)}, u32[]{:S(2)}) collective-permute-start(bf16[128,512]{1,0:T(8,128)(2,1)S(1)} %get-tuple-element.24), channel_id=1, source_target_pairs={{0,1},{1,0},{2,3},{3,2},{4,5},{5,4},{6,7},{7,6},{8,9},{9,8},{10,11... | collective-permute-start | bytes 393224 | tf_op jit(solution)/shard_map/ppermute | solution.py:29
  18.9 0.5 %collective-permute-start.6 = (bf16[128,512]{1,0:T(8,128)(2,1)S(1)}, bf16[128,512]{1,0:T(8,128)(2,1)S(1)}, u32[]{:S(2)}, u32[]{:S(2)}) collective-permute-start(bf16[128,512]{1,0:T(8,128)(2,1)S(1)} %get-tuple-element.26), channel_id=1, source_target_pairs={{0,1},{1,0},{2,3},{3,2},{4,5},{5,4},{6,7},{7,6},{8,9},{9,8},{10,11... | collective-permute-start | bytes 393224 | tf_op jit(solution)/shard_map/ppermute | solution.py:29
  19.4 0.7 %shard_map.57 = (bf16[128,512]{1,0:T(8,128)(2,1)S(1)}, bf16[128,512]{1,0:T(8,128)(2,1)S(1)}, bf16[128,512]{1,0:T(8,128)(2,1)S(1)}, bf16[128,512]{1,0:T(8,128)(2,1)S(1)}) custom-call(bf16[128,1024]{1,0:T(8,128)(2,1)S(1)} %get-tuple-element.18.a_ref, bf16[2,1024,2048]{2,1,0:T(8,128)(2,1)S(1)} %get-tuple-element.17.refs_4_.w_ref), custom_call_target="tpu_custom_call" | custom-call | flops 536870912 | bytes 1000000 | tf_op jit(solution)/shard_map/pallas_call | solution.py:148
  20.2 0.0 collective-permute-done.3
  20.2 3.1 %collective-permute-done.4 = bf16[128,512]{1,0:T(8,128)(2,1)S(1)} collective-permute-done((bf16[128,512]{1,0:T(8,128)(2,1)S(1)}, bf16[128,512]{1,0:T(8,128)(2,1)S(1)}, u32[]{:S(2)}, u32[]{:S(2)}) %collective-permute-start.4) | collective-permute-done | bytes 131104 | tf_op jit(solution)/shard_map/ppermute | solution.py:29
  23.3 2.8 %collective-permute-done.5 = bf16[128,512]{1,0:T(8,128)(2,1)S(1)} collective-permute-done((bf16[128,512]{1,0:T(8,128)(2,1)S(1)}, bf16[128,512]{1,0:T(8,128)(2,1)S(1)}, u32[]{:S(2)}, u32[]{:S(2)}) %collective-permute-start.5) | collective-permute-done | bytes 131104 | tf_op jit(solution)/shard_map/ppermute | solution.py:29
  26.1 2.8 %collective-permute-done.6 = bf16[128,512]{1,0:T(8,128)(2,1)S(1)} collective-permute-done((bf16[128,512]{1,0:T(8,128)(2,1)S(1)}, bf16[128,512]{1,0:T(8,128)(2,1)S(1)}, u32[]{:S(2)}, u32[]{:S(2)}) %collective-permute-start.6) | collective-permute-done | bytes 131104 | tf_op jit(solution)/shard_map/ppermute | solution.py:29
  28.9 0.8 %pad_maximum_fusion = bf16[128,2048]{1,0:T(8,128)(2,1)} fusion(bf16[128,512]{1,0:T(8,128)(2,1)S(1)} %add_convert_fusion, bf16[128,512]{1,0:T(8,128)(2,1)S(1)} %add_convert_fusion.1, bf16[128,512]{1,0:T(8,128)(2,1)S(1)} %add_convert_fusion.2, bf16[128,512]{1,0:T(8,128)(2,1)S(1)} %add_convert_fusion.3), kind=kLoop, calls=%fused_computation | loop fusion | flops 2097152 | bytes 1048576 | tf_op jit(solution)/shard_map/concatenate | solution.py:196
  (4 shorter events, 0.1 us)
Async XLA Ops:
  0.0 12.6 %copy-start.2 = (s32[16]{0:T(128)S(1)}, s32[16]{0:T(128)}, u32[]{:S(2)}) copy-start(s32[16]{0:T(128)} %docs_ref.1) | copy-start | bytes 196
  1.7 10.9 %collective-permute-start = (bf16[128,512]{1,0:T(8,128)(2,1)S(1)}, bf16[128,512]{1,0:T(8,128)(2,1)S(1)}, u32[]{:S(2)}, u32[]{:S(2)}) collective-permute-start(bf16[128,512]{1,0:T(8,128)(2,1)S(1)} %constant_dynamic-update-slice_fusion.refs_0_), channel_id=1, source_target_pairs={{0,2},{2,4},{4,6},{6,8},{8,10},{10,12},{12,14},{14,16},{16,18},{18... | collective-permute-start | bytes 393224 | tf_op jit(solution)/shard_map/ppermute | solution.py:29
  2.2 10.5 %collective-permute-start.1 = (bf16[128,512]{1,0:T(8,128)(2,1)S(1)}, bf16[128,512]{1,0:T(8,128)(2,1)S(1)}, u32[]{:S(2)}, u32[]{:S(2)}) collective-permute-start(bf16[128,512]{1,0:T(8,128)(2,1)S(1)} %constant_dynamic-update-slice_fusion.refs_0_), channel_id=1, source_target_pairs={{0,4},{2,6},{4,8},{6,10},{8,12},{10,14},{12,16},{14,18},{16,20},{1... | collective-permute-start | bytes 393224 | tf_op jit(solution)/shard_map/ppermute | solution.py:29
  4.7 7.9 %collective-permute-start.2 = (bf16[128,512]{1,0:T(8,128)(2,1)S(1)}, bf16[128,512]{1,0:T(8,128)(2,1)S(1)}, u32[]{:S(2)}, u32[]{:S(2)}) collective-permute-start(bf16[128,512]{1,0:T(8,128)(2,1)S(1)} %constant_dynamic-update-slice_fusion.refs_0_), channel_id=1, source_target_pairs={{0,6},{2,8},{4,10},{6,12},{8,14},{10,16},{12,18},{14,20},{16,22},{... | collective-permute-start | bytes 393224 | tf_op jit(solution)/shard_map/ppermute | solution.py:29
  7.1 3.4 %copy-start = (bf16[1024,4096]{1,0:T(8,128)(2,1)S(1)}, bf16[1024,4096]{1,0:T(8,128)(2,1)}, u32[]{:S(2)}) copy-start(bf16[1024,4096]{1,0:T(8,128)(2,1)} %w_ref.1) | copy-start | bytes 25165828
  10.5 0.9 %copy-start.1 = (bf16[128,1024]{1,0:T(8,128)(2,1)S(1)}, bf16[128,1024]{1,0:T(8,128)(2,1)}, u32[]{:S(2)}) copy-start(bf16[128,1024]{1,0:T(8,128)(2,1)} %q_ref.1) | copy-start | bytes 786436
  14.6 5.5 %collective-permute-start.3 = (bf16[128,512]{1,0:T(8,128)(2,1)S(1)}, bf16[128,512]{1,0:T(8,128)(2,1)S(1)}, u32[]{:S(2)}, u32[]{:S(2)}) collective-permute-start(bf16[128,512]{1,0:T(8,128)(2,1)S(1)} %get-tuple-element.20), channel_id=1, source_target_pairs={{0,1},{1,0},{2,3},{3,2},{4,5},{5,4},{6,7},{7,6},{8,9},{9,8},{10,11... | collective-permute-start | bytes 393224 | tf_op jit(solution)/shard_map/ppermute | solution.py:29
  16.8 6.5 %collective-permute-start.4 = (bf16[128,512]{1,0:T(8,128)(2,1)S(1)}, bf16[128,512]{1,0:T(8,128)(2,1)S(1)}, u32[]{:S(2)}, u32[]{:S(2)}) collective-permute-start(bf16[128,512]{1,0:T(8,128)(2,1)S(1)} %get-tuple-element.22), channel_id=1, source_target_pairs={{0,1},{1,0},{2,3},{3,2},{4,5},{5,4},{6,7},{7,6},{8,9},{9,8},{10,11... | collective-permute-start | bytes 393224 | tf_op jit(solution)/shard_map/ppermute | solution.py:29
  17.4 8.7 %collective-permute-start.5 = (bf16[128,512]{1,0:T(8,128)(2,1)S(1)}, bf16[128,512]{1,0:T(8,128)(2,1)S(1)}, u32[]{:S(2)}, u32[]{:S(2)}) collective-permute-start(bf16[128,512]{1,0:T(8,128)(2,1)S(1)} %get-tuple-element.24), channel_id=1, source_target_pairs={{0,1},{1,0},{2,3},{3,2},{4,5},{5,4},{6,7},{7,6},{8,9},{9,8},{10,11... | collective-permute-start | bytes 393224 | tf_op jit(solution)/shard_map/ppermute | solution.py:29
  18.9 10.0 %collective-permute-start.6 = (bf16[128,512]{1,0:T(8,128)(2,1)S(1)}, bf16[128,512]{1,0:T(8,128)(2,1)S(1)}, u32[]{:S(2)}, u32[]{:S(2)}) collective-permute-start(bf16[128,512]{1,0:T(8,128)(2,1)S(1)} %get-tuple-element.26), channel_id=1, source_target_pairs={{0,1},{1,0},{2,3},{3,2},{4,5},{5,4},{6,7},{7,6},{8,9},{9,8},{10,11... | collective-permute-start | bytes 393224 | tf_op jit(solution)/shard_map/ppermute | solution.py:29

commit v2 on v0

v2 whole, which is shorter than its diff:
```python
import functools
import jax
import jax.numpy as jnp
from jax import lax
from jax.experimental import pallas as pl
from jax.experimental.pallas import tpu as pltpu
from jax.sharding import PartitionSpec as P

HD = 128
QH = 16
KH = 4
BLK = 128
DOC_BLK = 32
PARTS = 4
ROUND = 4
LOG2E = 1.4426950408889634
MIB = 1024 * 1024
FAR = -1e30
VMEM = pl.BlockSpec(memory_space=pltpu.VMEM)
SMEM = pl.BlockSpec(memory_space=pltpu.SMEM)
HBM = pl.BlockSpec(memory_space=pltpu.HBM)
RINGS = (
    (2, 0, 3, 1, 5, 8, 7, 9, 10, 4, 6, 14, 13, 12, 15, 11),
    (1, 3, 4, 6, 0, 7, 8, 2, 5, 11, 12, 13, 14, 9, 15, 10),
    (1, 4, 3, 5, 6, 0, 2, 10, 9, 12, 11, 7, 8, 15, 13, 14),
)


def cost(flops, bytes_accessed):
    return pl.CostEstimate(flops=flops, bytes_accessed=bytes_accessed, transcendentals=0)


def turned(value, axis, steps):
    count = lax.axis_size(axis)
    return lax.ppermute(value, axis, [(source, (source + steps) % count) for source in range(count)])


def ring_table():
    gaps, carrier, seen = [0] * len(RINGS), 0, set()
    for at, ring in enumerate(RINGS):
        for source, target in enumerate(ring):
            gap = target - source
            wanted = gap == 2 or gap == (3 if source % 2 else 1)
            if wanted and (source, target) not in seen:
                seen.add((source, target))
                gaps[at] |= gap << 2 * target
                if gap == 2:
                    carrier |= at << 2 * target
    assert len(seen) == 5 * len(RINGS[0]) // 2 - 12
    return gaps, carrier


def pick(packed, position):
    signed = packed - (1 << 32) if packed >= 1 << 31 else packed
    return lax.shift_right_logical(jnp.int32(signed), 2 * position) & 3


def hold_kernel(kv_in, kv_out):
    pass


def hold(kv):
    return pl.pallas_call(
        hold_kernel,
        out_shape=jax.ShapeDtypeStruct(kv.shape, kv.dtype),
        in_specs=[VMEM],
        out_specs=VMEM,
        input_output_aliases={0: 0},
        compiler_params=pltpu.CompilerParams(vmem_limit_bytes=2 * MIB),
        cost_estimate=cost(10_000_000_000, 0),
    )(kv)


def choose_kernel(carrier, *refs):
    *arrived_refs, _, out_ref = refs
    holder = pick(carrier, lax.axis_index("seq"))
    for at, ref in enumerate(arrived_refs):

        @pl.when(holder == at)
        def _():
            out_ref[...] = ref[...]


def choose(carrier, arrived, after):
    return pl.pallas_call(
        functools.partial(choose_kernel, carrier),
        out_shape=jax.ShapeDtypeStruct(arrived[0].shape, arrived[0].dtype),
        in_specs=[VMEM] * (len(arrived) + 1),
        out_specs=VMEM,
        compiler_params=pltpu.CompilerParams(vmem_limit_bytes=4 * MIB),
        cost_estimate=cost(0, 300_000),
    )(*arrived, after)


def opening_kernel(gaps, kv_local, group_size, docs_ref, q_ref, kv_ref, *refs):
    *state_refs, bias_ref = refs
    position = lax.axis_index("seq")
    doc = docs_ref[position]
    for at, gap in enumerate(gaps):
        gap = gap(position)
        source = jnp.maximum(position - gap, 0)
        near = (docs_ref[source] == doc) & (position >= gap) & (gap > 0)
        bias_ref[at] = jnp.full(bias_ref.shape[1:], jnp.where(near, 0.0, FAR), jnp.float32)
    attend_kernel(1, True, kv_local, group_size, False, False, q_ref, kv_ref, *state_refs)


def opening(docs, queries, kv, weights, gaps, kv_local, group_size):
    rows = group_size * BLK
    state = [jax.ShapeDtypeStruct((kv_local, n, rows), jnp.float32) for n in (1, 1, HD)]
    bias = jax.ShapeDtypeStruct((len(gaps), 1, rows), jnp.float32)
    *state, bias = pl.pallas_call(
        functools.partial(opening_kernel, gaps, kv_local, group_size),
        out_shape=[*state, bias],
        in_specs=[SMEM, VMEM, VMEM],
        out_specs=[VMEM] * 4,
        compiler_params=pltpu.CompilerParams(vmem_limit_bytes=20 * MIB),
        cost_estimate=cost(500_000_000, 1_000_000),
    )(docs, queries, kv)
    return state, bias


def heads_of(kv_head, group_size):
    return range(kv_head * group_size, (kv_head + 1) * group_size)


def attend_kernel(blocks, own, kv_local, group_size, resume, finish, q_ref, *refs):
    refs = list(refs)
    kv_refs = [refs.pop(0) for _ in range(blocks)]
    bias_refs = [refs.pop(0) for _ in range(blocks - own)]
    state_in = [refs.pop(0) for _ in range(3)] if resume else None
    w_ref = refs.pop(0) if finish else None
    width = kv_local * HD
    scale = jnp.float32(LOG2E / HD**0.5)
    if own:
        row = lax.broadcasted_iota(jnp.int32, (BLK, BLK), 0)
        column = lax.broadcasted_iota(jnp.int32, (BLK, BLK), 1)
        causal = jnp.concatenate([row <= column] * group_size, axis=1)
    states = [[ref[kv_head] for ref in state_in] if resume else None for kv_head in range(kv_local)]
    queries = [
        jnp.concatenate([q_ref[:, h * HD : (h + 1) * HD] for h in heads_of(kv_head, group_size)], axis=0)
        for kv_head in range(kv_local)
    ]
    for start in range(0, blocks, ROUND):
        picked = range(start, min(start + ROUND, blocks))
        scores = [
            [
                lax.dot_general(
                    kv_refs[at][:, kv_head * HD : (kv_head + 1) * HD],
                    queries[kv_head],
                    (((1,), (1,)), ((), ())),
                    preferred_element_type=jnp.float32,
                )
                for at in picked
            ]
            for kv_head in range(kv_local)
        ]
        for kv_head in range(kv_local):
            parts = [
                jnp.where(causal, part, FAR) if own and at == 0 else part + bias_refs[at - own][...]
                for at, part in zip(picked, scores[kv_head])
            ]
            state = states[kv_head]
            top = jnp.max(functools.reduce(jnp.maximum, parts), axis=0, keepdims=True)
            if state:
                top = jnp.maximum(state[0], top)
            weights = [jnp.exp2((part - top) * scale) for part in parts]
            total = jnp.sum(functools.reduce(jnp.add, weights), axis=0, keepdims=True)
            values = [
                kv_refs[at][:, width + kv_head * HD : width + (kv_head + 1) * HD] for at in picked
            ]
            summed = lax.dot_general(
                jnp.concatenate(values, axis=0),
                jnp.concatenate([w.astype(jnp.bfloat16) for w in weights], axis=0),
                (((0,), (0,)), ((), ())),
                preferred_element_type=jnp.float32,
            )
            if state:
                factor = jnp.exp2((state[0] - top) * scale)
                total = total + state[1] * factor
                summed = summed + state[2] * factor
            states[kv_head] = [top, total, summed]
    for kv_head, state in enumerate(states):
        if finish:
            attended = state[2] * (1.0 / state[1])
            for g, h in enumerate(heads_of(kv_head, group_size)):
                turned_back = attended[:, g * BLK : (g + 1) * BLK].T
                refs[0][:, h * HD : (h + 1) * HD] = turned_back.astype(jnp.bfloat16)
        else:
            for ref, value in zip(refs, state):
                ref[kv_head] = value
    if finish:
        out_ref, part_ref = refs
        part_ref[...] = project_part(out_ref, w_ref, 1, 0, part_ref.shape[1])


def first_column(columns, step):
    groups = lax.axis_size("head")
    target = lax.rem(lax.axis_index("head") + step, groups)
    return pl.multiple_of(target * (columns // groups), 128)


def attend(queries, kv_blocks, biases, kv_local, group_size, state, weights=None, width=0):
    rows = group_size * BLK
    if width:
        out_shape = [
            jax.ShapeDtypeStruct(queries.shape, jnp.bfloat16),
            jax.ShapeDtypeStruct((BLK, width), jnp.bfloat16),
        ]
    else:
        out_shape = [jax.ShapeDtypeStruct((kv_local, n, rows), jnp.float32) for n in (1, 1, HD)]
    operands = [queries, *kv_blocks, *biases, *state] + ([weights] if width else [])
    blocks = len(kv_blocks)
    return pl.pallas_call(
        functools.partial(
            attend_kernel, blocks, len(biases) < blocks, kv_local, group_size, bool(state), bool(width)
        ),
        out_shape=out_shape,
        in_specs=[VMEM] * len(operands),
        out_specs=[VMEM] * len(out_shape),
        compiler_params=pltpu.CompilerParams(vmem_limit_bytes=20 * MIB),
        cost_estimate=cost(1_000_000_000, 2_000_000),
    )(*operands)


def project_part(a_ref, w_ref, step, part, width):
    begin = pl.multiple_of(first_column(w_ref.shape[1], step) + part * width, 128)
    return jnp.dot(
        a_ref[...], w_ref[:, pl.ds(begin, width)], preferred_element_type=jnp.float32
    ).astype(jnp.bfloat16)


def project_kernel(step, parts, a_ref, w_ref, *out_refs):
    for part, out_ref in zip(parts, out_refs):
        out_ref[...] = project_part(a_ref, w_ref, step, part, out_ref.shape[1])


def project(attended, weights, step, parts, width):
    return pl.pallas_call(
        functools.partial(project_kernel, step, parts),
        out_shape=[jax.ShapeDtypeStruct((BLK, width), jnp.bfloat16)] * len(parts),
        in_specs=[VMEM, VMEM],
        out_specs=[VMEM] * len(parts),
        compiler_params=pltpu.CompilerParams(vmem_limit_bytes=20 * MIB),
        cost_estimate=cost(2 * BLK * width * len(parts) * attended.shape[1], 1_000_000),
    )(attended, weights)


def mask_kernel(docs_ref, bias_ref):
    position = lax.axis_index("seq")
    doc = docs_ref[position]
    for at in range(bias_ref.shape[0]):
        near = (docs_ref[jnp.maximum(position - at - 1, 0)] == doc) & (position > at)
        bias_ref[at] = jnp.full(bias_ref.shape[1:], jnp.where(near, 0.0, FAR), jnp.float32)


def mask(docs, reach, rows):
    return pl.pallas_call(
        mask_kernel,
        out_shape=jax.ShapeDtypeStruct((reach, 1, rows), jnp.float32),
        in_specs=[SMEM],
        out_specs=VMEM,
    )(docs)


def side_by_side(left, right):
    low = jnp.array(-jnp.inf, left.dtype)
    first = lax.pad(left, low, ((0, 0, 0), (0, right.shape[1], 0)))
    return jnp.maximum(first, lax.pad(right, low, ((0, 0, 0), (left.shape[1], 0, 0))))


def local(query_states, key_states, value_states, out_weight, block_docs):
    tokens_here = query_states.shape[0]
    kv_local = key_states.shape[1] // HD
    group_size = QH // KH
    count = lax.axis_size("seq")
    groups = lax.axis_size("head")
    assert tokens_here == BLK and block_docs.shape[0] == count
    reach = min(DOC_BLK, count // 4) - 1
    width = out_weight.shape[1] // groups // PARTS
    sizes = (kv_local, group_size)

    kv = hold(side_by_side(key_states, value_states))
    if reach == 3 and count == len(RINGS[0]):
        packed, carrier = ring_table()
        arrived = [lax.ppermute(kv, "seq", list(enumerate(ring))) for ring in RINGS]
        gaps = [functools.partial(pick, word) for word in packed]
        gaps.append(lambda position: 1 + 2 * (position & 1))
        state, bias = opening(block_docs, query_states, kv, out_weight, gaps, *sizes)
        second = choose(carrier, arrived, state[0])
        late = lax.ppermute(second, "seq", [(i, i ^ 1) for i in range(count)])
        biases = [bias[at] for at in range(len(gaps))]
        state = attend(query_states, arrived, biases[:-1], *sizes, state)
        attended, first = attend(query_states, [late], biases[-1:], *sizes, state, out_weight, width)
    else:
        blocks = [kv]
        while len(blocks) < reach + 1:
            have = len(blocks)
            send = min(have, reach + 1 - have)
            passed = turned(jnp.stack(blocks[:send]), "seq", have)
            blocks = blocks + [passed[i] for i in range(send)]
        bias = mask(block_docs, reach, group_size * BLK)
        biases = [bias[at] for at in range(reach)]
        attended, first = attend(query_states, blocks, biases, *sizes, (), out_weight, width)

    received = []
    for step in range(1, groups):
        if step == 1:
            row = [first] + list(project(attended, out_weight, 1, range(1, PARTS), width))
        else:
            row = project(attended, out_weight, step, range(PARTS), width)
        received.append([turned(partial, "head", step) for partial in row])
    mine = project(attended, out_weight, 0, range(PARTS), width)
    outs = []
    for i in range(PARTS):
        total = mine[i].astype(jnp.float32)
        for row in received:
            total = total + row[i].astype(jnp.float32)
        outs.append(total.astype(jnp.bfloat16))
    return jnp.concatenate(outs, axis=1)


def solution(mesh):
    return jax.shard_map(
        local,
        mesh=mesh,
        in_specs=(P("seq", "head"), P("seq", "head"), P("seq", "head"), P("head", None), P()),
        out_specs=P("seq", "head"),
        check_vma=False,
    )
```

time: 75.8 us -> 28 us (0.37)
  waiting for transfers between devices: 27.5 us -> 11 us
  between operations: 13.6 us -> 0.15 us
  other arithmetic: 11.3 us -> 2.02 us
  matrix products: 8.47 us -> 0 us
  local copies, waits for them, and re-layouts: 7.45 us -> 0.03 us
  Pallas kernels: 0 us -> 4.43 us
  starting transfers between devices: 6.78 us -> 10.2 us
    reduce_scatter x1 -> x0, waiting for transfers between devices: 22.8 us -> none  [local(): lax.psum_scatter(partial_terms.astype(jnp.bfloat16), 'head', scatter_dime...]
    dot_general x9 -> x0, matrix products: 8.47 us -> none  [the longest x1 5.67 us: local(): jnp.dot(attended, out_weight, preferred_element_type=jnp.float32)]
    ppermute x2 -> x8, waiting for transfers between devices: 4.64 us -> 11 us  [the longest x4 9.26 us: turned(): lax.ppermute(value, axis, [(source, (source + steps) % count) for source...]
    select_n x1 -> x0, other arithmetic: 5.64 us -> none  [local(): jnp.repeat(block_docs, BLK, total_repeat_length=block_count * BLK)]
    gather x2 -> x0, other arithmetic: 4.55 us -> none  [local(): jnp.repeat(block_docs, BLK, total_repeat_length=block_count * BLK)]
    pallas_call x0 -> x7, Pallas kernels: none -> 4.43 us  [the longest x2 2.02 us: attend(): pl.pallas_call(functools.partial(attend_kernel, blocks, len(biases) < blo...]
    ppermute x2 -> x8, starting transfers between devices: 6.78 us -> 10.2 us  [the longest x3 6.04 us: local(): arrived = [lax.ppermute(kv, 'seq', list(enumerate(ring))) for ring in RINGS]]
    unnamed x4 -> x8, local copies, waits for them, and re-layouts: 3.2 us -> 0.02 us
  transfers between devices with their start and end apart: 3 -> 8, of which waited for: 2 -> 5; matrix products, arithmetic and copies ran while one was open for 21% -> 0% of each run, Pallas kernels for 0% -> 10%
where the time goes in v2:
time: 28 us; the launch traced here: 27.8 us
  waiting for transfers between devices  11 us (39%)
  starting transfers between devices  10.2 us (36%)
  Pallas kernels  4.43 us (16%)
  other arithmetic  2.02 us (7%)
    ppermute x4, waiting for transfers between devices, turned(): lax.ppermute(value, axis, [(source, (source + steps) % count) for source...  9.26 us
    ppermute x3, starting transfers between devices, local(): arrived = [lax.ppermute(kv, 'seq', list(enumerate(ring))) for ring in RINGS]  6.04 us
    ppermute x4, starting transfers between devices, turned(): lax.ppermute(value, axis, [(source, (source + steps) % count) for source...  4.12 us
    pallas_call x2, Pallas kernels, attend(): pl.pallas_call(functools.partial(attend_kernel, blocks, len(biases) < blo...  2.02 us
    ppermute x3, waiting for transfers between devices, local(): arrived = [lax.ppermute(kv, 'seq', list(enumerate(ring))) for ring in RINGS]  1.46 us
    pallas_call x2, Pallas kernels, project(): pl.pallas_call(functools.partial(project_kernel, step, parts), out_shape=...  1.35 us
    pallas_call x1, Pallas kernels, opening(): pl.pallas_call(functools.partial(opening_kernel, gaps, kv_local, group_si...  1.05 us
    max x1, other arithmetic, side_by_side(): jnp.maximum(first, lax.pad(right, low, ((0, 0, 0), (left.shape[1], 0, 0))))  1.03 us
  transfers between devices with their start and end apart: 8, of which 5 were waited for; matrix products, arithmetic and copies ran while one was open for 0% of the time, Pallas kernels for 10%

profile of v2, /device:TPU:0, one launch (start us, length us, event | category | flops | bytes accessed | tf_op | source)
XLA Modules:
  0.0 27.8 jit_solution(8501018860373436215)
XLA Ops:
  0.0 0.0 slice-start
  0.0 1.0 %pad_maximum_fusion.1.kv_in = bf16[128,512]{1,0:T(8,128)(2,1)S(1)} fusion(bf16[128,256]{1,0:T(8,128)(2,1)} %param.7, bf16[128,256]{1,0:T(8,128)(2,1)} %param.6), kind=kLoop, calls=%fused_computation.5 | loop fusion | flops 262144 | bytes 262144 | tf_op jit(solution)/shard_map/max | solution.py:268
  1.0 0.0 copy-start
  1.0 0.0 copy-start.1
  1.1 0.0 slice-start.1
  1.1 0.5 %collective-permute-start.2 = (bf16[128,512]{1,0:T(8,128)(2,1)S(1)}, bf16[128,512]{1,0:T(8,128)(2,1)S(1)}, u32[]{:S(2)}, u32[]{:S(2)}) collective-permute-start(bf16[128,512]{1,0:T(8,128)(2,1)S(1)} %shard_map.55.kv_ref), channel_id=1, source_target_pairs={{0,2},{2,8},{4,6},{6,10},{8,12},{10,0},{12,4},{14,20},{16,18},{18,... | collective-permute-start | bytes 393224 | tf_op jit(solution)/shard_map/ppermute | solution.py:285
  1.6 2.7 %collective-permute-start.1 = (bf16[128,512]{1,0:T(8,128)(2,1)S(1)}, bf16[128,512]{1,0:T(8,128)(2,1)S(1)}, u32[]{:S(2)}, u32[]{:S(2)}) collective-permute-start(bf16[128,512]{1,0:T(8,128)(2,1)S(1)} %shard_map.55.kv_ref), channel_id=1, source_target_pairs={{0,2},{2,6},{4,8},{6,12},{8,0},{10,14},{12,16},{14,4},{16,10},{18,... | collective-permute-start | bytes 393224 | tf_op jit(solution)/shard_map/ppermute | solution.py:285
  4.3 2.8 %collective-permute-start = (bf16[128,512]{1,0:T(8,128)(2,1)S(1)}, bf16[128,512]{1,0:T(8,128)(2,1)S(1)}, u32[]{:S(2)}, u32[]{:S(2)}) collective-permute-start(bf16[128,512]{1,0:T(8,128)(2,1)S(1)} %shard_map.55.kv_ref), channel_id=1, source_target_pairs={{0,4},{2,0},{4,6},{6,2},{8,10},{10,16},{12,14},{14,18},{16,20},{18... | collective-permute-start | bytes 393224 | tf_op jit(solution)/shard_map/ppermute | solution.py:285
  7.1 0.0 copy-done
  7.1 0.0 copy-done.1
  7.1 1.0 %shard_map.56 = (f32[2,1,512]{2,1,0:T(1,128)S(1)}, f32[2,1,512]{2,1,0:T(1,128)S(1)}, f32[2,128,512]{2,1,0:T(8,128)S(1)}, f32[4,1,512]{2,1,0:T(1,128)S(1)}) custom-call(s32[16]{0:T(128)S(1)} %copy-done.1, bf16[128,1024]{1,0:T(8,128)(2,1)S(1)} %copy-done, bf16[128,512]{1,0:T(8,128)(2,1)S(1)} %shard_map.55.kv_ref), custom_call_target="tpu_custom_call" | custom-call | flops 500000000 | bytes 1000000 | tf_op jit(solution)/shard_map/pallas_call | solution.py:111
  8.2 0.0 collective-permute-done.2.refs_2_
  8.2 0.4 %collective-permute-done.1.refs_1_ = bf16[128,512]{1,0:T(8,128)(2,1)S(1)} collective-permute-done((bf16[128,512]{1,0:T(8,128)(2,1)S(1)}, bf16[128,512]{1,0:T(8,128)(2,1)S(1)}, u32[]{:S(2)}, u32[]{:S(2)}) %collective-permute-start.1) | collective-permute-done | bytes 131104 | tf_op jit(solution)/shard_map/ppermute | solution.py:285
  8.6 1.0 %collective-permute-done.refs_0_ = bf16[128,512]{1,0:T(8,128)(2,1)S(1)} collective-permute-done((bf16[128,512]{1,0:T(8,128)(2,1)S(1)}, bf16[128,512]{1,0:T(8,128)(2,1)S(1)}, u32[]{:S(2)}, u32[]{:S(2)}) %collective-permute-start) | collective-permute-done | bytes 131104 | tf_op jit(solution)/shard_map/ppermute | solution.py:285
  9.7 0.1 collective-permute-start.3
  9.8 1.1 %shard_map.58 = (f32[2,1,512]{2,1,0:T(1,128)S(1)}, f32[2,1,512]{2,1,0:T(1,128)S(1)}, f32[2,128,512]{2,1,0:T(8,128)S(1)}) custom-call(bf16[128,1024]{1,0:T(8,128)(2,1)S(1)} %copy-done, bf16[128,512]{1,0:T(8,128)(2,1)S(1)} %collective-permute-done.refs_0_, bf16[128,512]{1,0:T(8,128)(2,1)S(1)} %collective-permute-done.1.refs_1_, ...), custom_call_target="tpu_custom_call" | custom-call | flops 1000000000 | bytes 2000000 | tf_op jit(solution)/shard_map/pallas_call | solution.py:213
  10.8 0.2 collective-permute-done.3.refs_0_
  11.1 0.0 slice-done
  11.1 0.0 slice-done.1
  11.1 0.9 %shard_map.59 = (bf16[128,1024]{1,0:T(8,128)(2,1)S(1)}, bf16[128,512]{1,0:T(8,128)(2,1)S(1)}) custom-call(bf16[128,1024]{1,0:T(8,128)(2,1)S(1)} %copy-done, bf16[128,512]{1,0:T(8,128)(2,1)S(1)} %collective-permute-done.3.refs_0_, f32[1,512]{1,0:T(1,128)S(1)} %get-tuple-element.40.refs_1_, f32[2,1,512]{2,1,0:T(1,128)S(1)} %get-tuple-element.25.refs_2_, ...), custom_call_target="tpu_custom_call" | custom-call | flops 1000000000 | bytes 2000000 | tf_op jit(solution)/shard_map/pallas_call | solution.py:213
  12.0 0.6 %shard_map.61 = (bf16[128,512]{1,0:T(8,128)(2,1)S(1)}, bf16[128,512]{1,0:T(8,128)(2,1)S(1)}, bf16[128,512]{1,0:T(8,128)(2,1)S(1)}) custom-call(bf16[128,1024]{1,0:T(8,128)(2,1)S(1)} %get-tuple-element.28.a_ref, bf16[1024,4096]{1,0:T(8,128)(2,1)S(1)} %bitcast.9), custom_call_target="tpu_custom_call" | custom-call | flops 402653184 | bytes 1000000 | tf_op jit(solution)/shard_map/pallas_call | solution.py:238
  12.7 1.6 %collective-permute-start.7 = (bf16[128,512]{1,0:T(8,128)(2,1)S(1)}, bf16[128,512]{1,0:T(8,128)(2,1)S(1)}, u32[]{:S(2)}, u32[]{:S(2)}) collective-permute-start(bf16[128,512]{1,0:T(8,128)(2,1)S(1)} %get-tuple-element.36), channel_id=1, source_target_pairs={{0,1},{1,0},{2,3},{3,2},{4,5},{5,4},{6,7},{7,6},{8,9},{9,8},{10,11... | collective-permute-start | bytes 393224 | tf_op jit(solution)/shard_map/ppermute | solution.py:35
  14.2 0.5 %collective-permute-start.4 = (bf16[128,512]{1,0:T(8,128)(2,1)S(1)}, bf16[128,512]{1,0:T(8,128)(2,1)S(1)}, u32[]{:S(2)}, u32[]{:S(2)}) collective-permute-start(bf16[128,512]{1,0:T(8,128)(2,1)S(1)} %get-tuple-element.30), channel_id=1, source_target_pairs={{0,1},{1,0},{2,3},{3,2},{4,5},{5,4},{6,7},{7,6},{8,9},{9,8},{10,11... | collective-permute-start | bytes 393224 | tf_op jit(solution)/shard_map/ppermute | solution.py:35
  14.7 1.5 %collective-permute-start.5 = (bf16[128,512]{1,0:T(8,128)(2,1)S(1)}, bf16[128,512]{1,0:T(8,128)(2,1)S(1)}, u32[]{:S(2)}, u32[]{:S(2)}) collective-permute-start(bf16[128,512]{1,0:T(8,128)(2,1)S(1)} %get-tuple-element.32), channel_id=1, source_target_pairs={{0,1},{1,0},{2,3},{3,2},{4,5},{5,4},{6,7},{7,6},{8,9},{9,8},{10,11... | collective-permute-start | bytes 393224 | tf_op jit(solution)/shard_map/ppermute | solution.py:35
  16.3 0.5 %collective-permute-start.6 = (bf16[128,512]{1,0:T(8,128)(2,1)S(1)}, bf16[128,512]{1,0:T(8,128)(2,1)S(1)}, u32[]{:S(2)}, u32[]{:S(2)}) collective-permute-start(bf16[128,512]{1,0:T(8,128)(2,1)S(1)} %get-tuple-element.34), channel_id=1, source_target_pairs={{0,1},{1,0},{2,3},{3,2},{4,5},{5,4},{6,7},{7,6},{8,9},{9,8},{10,11... | collective-permute-start | bytes 393224 | tf_op jit(solution)/shard_map/ppermute | solution.py:35
  16.8 0.7 %shard_map.60 = (bf16[128,512]{1,0:T(8,128)(2,1)S(1)}, bf16[128,512]{1,0:T(8,128)(2,1)S(1)}, bf16[128,512]{1,0:T(8,128)(2,1)S(1)}, bf16[128,512]{1,0:T(8,128)(2,1)S(1)}) custom-call(bf16[128,1024]{1,0:T(8,128)(2,1)S(1)} %get-tuple-element.28.a_ref, bf16[1024,4096]{1,0:T(8,128)(2,1)S(1)} %bitcast.9), custom_call_target="tpu_custom_call" | custom-call | flops 536870912 | bytes 1000000 | tf_op jit(solution)/shard_map/pallas_call | solution.py:238
  17.5 1.5 %collective-permute-done.7 = bf16[128,512]{1,0:T(8,128)(2,1)S(1)} collective-permute-done((bf16[128,512]{1,0:T(8,128)(2,1)S(1)}, bf16[128,512]{1,0:T(8,128)(2,1)S(1)}, u32[]{:S(2)}, u32[]{:S(2)}) %collective-permute-start.7) | collective-permute-done | bytes 131104 | tf_op jit(solution)/shard_map/ppermute | solution.py:35
  19.1 7.7 %collective-permute-done.6 = bf16[128,512]{1,0:T(8,128)(2,1)S(1)} collective-permute-done((bf16[128,512]{1,0:T(8,128)(2,1)S(1)}, bf16[128,512]{1,0:T(8,128)(2,1)S(1)}, u32[]{:S(2)}, u32[]{:S(2)}) %collective-permute-start.6) | collective-permute-done | bytes 131104 | tf_op jit(solution)/shard_map/ppermute | solution.py:35
  26.9 0.0 collective-permute-done.4
  26.9 0.0 collective-permute-done.5
  27.0 0.8 %pad_maximum_fusion = bf16[128,2048]{1,0:T(8,128)(2,1)} fusion(bf16[128,512]{1,0:T(8,128)(2,1)S(1)} %add_convert_fusion, bf16[128,512]{1,0:T(8,128)(2,1)S(1)} %add_convert_fusion.1, bf16[128,512]{1,0:T(8,128)(2,1)S(1)} %add_convert_fusion.2, bf16[128,512]{1,0:T(8,128)(2,1)S(1)} %add_convert_fusion.3), kind=kLoop, calls=%fused_computation | loop fusion | flops 2097152 | bytes 1048576 | tf_op jit(solution)/shard_map/concatenate | solution.py:319
  (8 shorter events, 0.2 us)
Async XLA Ops:
  0.0 11.1 %slice-start = ((s8[8388608]{0:T(1024)(128)(4,1)}), s8[4194304]{0:T(1024)(128)(4,1)S(1)}, s32[]{:S(2)}) async-start(s8[8388608]{0:T(1024)(128)(4,1)} %bitcast.8), calls=%async_computation | async-start | bytes 8388608
  1.0 6.1 %copy-start = (bf16[128,1024]{1,0:T(8,128)(2,1)S(1)}, bf16[128,1024]{1,0:T(8,128)(2,1)}, u32[]{:S(2)}) copy-start(bf16[128,1024]{1,0:T(8,128)(2,1)} %q_ref.5) | copy-start | bytes 786436
  1.0 6.1 %copy-start.1 = (s32[16]{0:T(128)S(1)}, s32[16]{0:T(128)}, u32[]{:S(2)}) copy-start(s32[16]{0:T(128)} %docs_ref.1) | copy-start | bytes 196
  1.1 10.0 %slice-start.1 = ((s8[8388608]{0:T(1024)(128)(4,1)}), s8[4194304]{0:T(1024)(128)(4,1)S(1)}, s32[]{:S(2)}) async-start(s8[8388608]{0:T(1024)(128)(4,1)} %bitcast.8), calls=%async_computation.1 | async-start | bytes 8388608
  1.1 7.1 %collective-permute-start.2 = (bf16[128,512]{1,0:T(8,128)(2,1)S(1)}, bf16[128,512]{1,0:T(8,128)(2,1)S(1)}, u32[]{:S(2)}, u32[]{:S(2)}) collective-permute-start(bf16[128,512]{1,0:T(8,128)(2,1)S(1)} %shard_map.55.kv_ref), channel_id=1, source_target_pairs={{0,2},{2,8},{4,6},{6,10},{8,12},{10,0},{12,4},{14,20},{16,18},{18,... | collective-permute-start | bytes 393224 | tf_op jit(solution)/shard_map/ppermute | solution.py:285
  1.6 7.0 %collective-permute-start.1 = (bf16[128,512]{1,0:T(8,128)(2,1)S(1)}, bf16[128,512]{1,0:T(8,128)(2,1)S(1)}, u32[]{:S(2)}, u32[]{:S(2)}) collective-permute-start(bf16[128,512]{1,0:T(8,128)(2,1)S(1)} %shard_map.55.kv_ref), channel_id=1, source_target_pairs={{0,2},{2,6},{4,8},{6,12},{8,0},{10,14},{12,16},{14,4},{16,10},{18,... | collective-permute-start | bytes 393224 | tf_op jit(solution)/shard_map/ppermute | solution.py:285
  4.3 5.4 %collective-permute-start = (bf16[128,512]{1,0:T(8,128)(2,1)S(1)}, bf16[128,512]{1,0:T(8,128)(2,1)S(1)}, u32[]{:S(2)}, u32[]{:S(2)}) collective-permute-start(bf16[128,512]{1,0:T(8,128)(2,1)S(1)} %shard_map.55.kv_ref), channel_id=1, source_target_pairs={{0,4},{2,0},{4,6},{6,2},{8,10},{10,16},{12,14},{14,18},{16,20},{18... | collective-permute-start | bytes 393224 | tf_op jit(solution)/shard_map/ppermute | solution.py:285
  9.7 1.4 %collective-permute-start.3 = (bf16[128,512]{1,0:T(8,128)(2,1)S(1)}, bf16[128,512]{1,0:T(8,128)(2,1)S(1)}, u32[]{:S(2)}, u32[]{:S(2)}) collective-permute-start(bf16[128,512]{1,0:T(8,128)(2,1)S(1)} %shard_map.57), channel_id=1, source_target_pairs={{0,2},{2,0},{4,6},{6,4},{8,10},{10,8},{12,14},{14,12},{16,18},{18,... | collective-permute-start | bytes 393224 | tf_op jit(solution)/shard_map/ppermute | solution.py:290
  12.7 6.4 %collective-permute-start.7 = (bf16[128,512]{1,0:T(8,128)(2,1)S(1)}, bf16[128,512]{1,0:T(8,128)(2,1)S(1)}, u32[]{:S(2)}, u32[]{:S(2)}) collective-permute-start(bf16[128,512]{1,0:T(8,128)(2,1)S(1)} %get-tuple-element.36), channel_id=1, source_target_pairs={{0,1},{1,0},{2,3},{3,2},{4,5},{5,4},{6,7},{7,6},{8,9},{9,8},{10,11... | collective-permute-start | bytes 393224 | tf_op jit(solution)/shard_map/ppermute | solution.py:35
  14.2 12.6 %collective-permute-start.4 = (bf16[128,512]{1,0:T(8,128)(2,1)S(1)}, bf16[128,512]{1,0:T(8,128)(2,1)S(1)}, u32[]{:S(2)}, u32[]{:S(2)}) collective-permute-start(bf16[128,512]{1,0:T(8,128)(2,1)S(1)} %get-tuple-element.30), channel_id=1, source_target_pairs={{0,1},{1,0},{2,3},{3,2},{4,5},{5,4},{6,7},{7,6},{8,9},{9,8},{10,11... | collective-permute-start | bytes 393224 | tf_op jit(solution)/shard_map/ppermute | solution.py:35
  14.7 12.2 %collective-permute-start.5 = (bf16[128,512]{1,0:T(8,128)(2,1)S(1)}, bf16[128,512]{1,0:T(8,128)(2,1)S(1)}, u32[]{:S(2)}, u32[]{:S(2)}) collective-permute-start(bf16[128,512]{1,0:T(8,128)(2,1)S(1)} %get-tuple-element.32), channel_id=1, source_target_pairs={{0,1},{1,0},{2,3},{3,2},{4,5},{5,4},{6,7},{7,6},{8,9},{9,8},{10,11... | collective-permute-start | bytes 393224 | tf_op jit(solution)/shard_map/ppermute | solution.py:35
  16.3 10.6 %collective-permute-start.6 = (bf16[128,512]{1,0:T(8,128)(2,1)S(1)}, bf16[128,512]{1,0:T(8,128)(2,1)S(1)}, u32[]{:S(2)}, u32[]{:S(2)}) collective-permute-start(bf16[128,512]{1,0:T(8,128)(2,1)S(1)} %get-tuple-element.34), channel_id=1, source_target_pairs={{0,1},{1,0},{2,3},{3,2},{4,5},{5,4},{6,7},{7,6},{8,9},{9,8},{10,11... | collective-permute-start | bytes 393224 | tf_op jit(solution)/shard_map/ppermute | solution.py:35

commit v3 on v2

--- a/solution.py
+++ b/solution.py
@@ -20,9 +20,9 @@
 SMEM = pl.BlockSpec(memory_space=pltpu.SMEM)
 HBM = pl.BlockSpec(memory_space=pltpu.HBM)
 RINGS = (
-    (2, 0, 3, 1, 5, 8, 7, 9, 10, 4, 6, 14, 13, 12, 15, 11),
-    (1, 3, 4, 6, 0, 7, 8, 2, 5, 11, 12, 13, 14, 9, 15, 10),
-    (1, 4, 3, 5, 6, 0, 2, 10, 9, 12, 11, 7, 8, 15, 13, 14),
+    (1, 4, 3, 6, 5, 0, 2, 10, 9, 12, 7, 14, 13, 8, 15, 11),
+    (1, 0, 3, 5, 6, 7, 8, 2, 10, 4, 11, 13, 14, 9, 15, 12),
+    (2, 3, 4, 0, 1, 8, 7, 9, 5, 11, 12, 6, 13, 15, 10, 14),
 )
 
 
@@ -45,7 +45,7 @@
                 seen.add((source, target))
                 gaps[at] |= gap << 2 * target
                 if gap == 2:
-                    carrier |= at << 2 * target
+                    carrier |= (at - 1) << 2 * target
     assert len(seen) == 5 * len(RINGS[0]) // 2 - 12
     return gaps, carrier
 
@@ -93,7 +93,8 @@
 
 
 def opening_kernel(gaps, kv_local, group_size, docs_ref, q_ref, kv_ref, *refs):
-    *state_refs, bias_ref = refs
+    *state_refs, bias_ref, kv_out = refs
+    kv_out[...] = kv_ref[...]
     position = lax.axis_index("seq")
     doc = docs_ref[position]
     for at, gap in enumerate(gaps):
@@ -108,15 +109,15 @@
     rows = group_size * BLK
     state = [jax.ShapeDtypeStruct((kv_local, n, rows), jnp.float32) for n in (1, 1, HD)]
     bias = jax.ShapeDtypeStruct((len(gaps), 1, rows), jnp.float32)
-    *state, bias = pl.pallas_call(
+    *state, bias, kv = pl.pallas_call(
         functools.partial(opening_kernel, gaps, kv_local, group_size),
-        out_shape=[*state, bias],
+        out_shape=[*state, bias, jax.ShapeDtypeStruct(kv.shape, kv.dtype)],
         in_specs=[SMEM, VMEM, VMEM],
-        out_specs=[VMEM] * 4,
+        out_specs=[VMEM] * 5,
         compiler_params=pltpu.CompilerParams(vmem_limit_bytes=20 * MIB),
         cost_estimate=cost(500_000_000, 1_000_000),
     )(docs, queries, kv)
-    return state, bias
+    return state, bias, kv
 
 
 def heads_of(kv_head, group_size):
@@ -190,7 +191,7 @@
                 ref[kv_head] = value
     if finish:
         out_ref, part_ref = refs
-        part_ref[...] = project_part(out_ref, w_ref, 1, 0, part_ref.shape[1])
+        part_ref[...] = project_part(out_ref, w_ref, 1, PARTS - 1, part_ref.shape[1])
 
 
 def first_column(columns, step):
@@ -245,6 +246,46 @@
     )(attended, weights)
 
 
+def close_kernel(parts, each, resume, *refs):
+    refs = list(refs)
+    mine_refs = [refs.pop(0) for _ in parts]
+    other_refs = [[refs.pop(0) for _ in range(each)] for _ in parts]
+    if resume:
+        refs.pop(0)
+    out_ref, sums, sems = refs
+    width = mine_refs[0].shape[1]
+    copies = []
+    for at, part in enumerate(parts):
+        total = mine_refs[at][...].astype(jnp.float32)
+        for ref in other_refs[at]:
+            total = total + ref[...].astype(jnp.float32)
+        sums[at] = total.astype(sums.dtype)
+        columns = slice(part * width, (part + 1) * width)
+        copies.append(pltpu.make_async_copy(sums.at[at], out_ref.at[:, columns], sems.at[at]))
+        copies[-1].start()
+    for copy in copies:
+        copy.wait()
+
+
+def close(parts, mine, received, columns, out=None):
+    rows, width = mine[0].shape
+    others = [row[part] for part in parts for row in received]
+    operands = [mine[part] for part in parts] + others + ([] if out is None else [out])
+    return pl.pallas_call(
+        functools.partial(close_kernel, tuple(parts), len(received), out is not None),
+        out_shape=jax.ShapeDtypeStruct((rows, columns), mine[0].dtype),
+        in_specs=[VMEM] * (len(parts) + len(others)) + ([] if out is None else [HBM]),
+        out_specs=HBM,
+        scratch_shapes=[
+            pltpu.VMEM((len(parts), rows, width), mine[0].dtype),
+            pltpu.SemaphoreType.DMA((len(parts),)),
+        ],
+        input_output_aliases={} if out is None else {len(operands) - 1: 0},
+        compiler_params=pltpu.CompilerParams(vmem_limit_bytes=8 * MIB),
+        cost_estimate=cost(1_000_000, 1_000_000),
+    )(*operands)
+
+
 def mask_kernel(docs_ref, bias_ref):
     position = lax.axis_index("seq")
     doc = docs_ref[position]
@@ -282,15 +323,18 @@
     kv = hold(side_by_side(key_states, value_states))
     if reach == 3 and count == len(RINGS[0]):
         packed, carrier = ring_table()
-        arrived = [lax.ppermute(kv, "seq", list(enumerate(ring))) for ring in RINGS]
+        arrived = [lax.ppermute(kv, "seq", list(enumerate(ring))) for ring in RINGS[1:]]
         gaps = [functools.partial(pick, word) for word in packed]
         gaps.append(lambda position: 1 + 2 * (position & 1))
-        state, bias = opening(block_docs, query_states, kv, out_weight, gaps, *sizes)
-        second = choose(carrier, arrived, state[0])
+        state, bias, kv = opening(block_docs, query_states, kv, out_weight, gaps, *sizes)
+        arrived = [lax.ppermute(kv, "seq", list(enumerate(RINGS[0])))] + arrived
+        second = choose(carrier, arrived[1:], state[0])
         late = lax.ppermute(second, "seq", [(i, i ^ 1) for i in range(count)])
         biases = [bias[at] for at in range(len(gaps))]
-        state = attend(query_states, arrived, biases[:-1], *sizes, state)
-        attended, first = attend(query_states, [late], biases[-1:], *sizes, state, out_weight, width)
+        state = attend(query_states, arrived[1:], biases[1:3], *sizes, state)
+        attended, last = attend(
+            query_states, [arrived[0], late], [biases[0], biases[3]], *sizes, state, out_weight, width
+        )
     else:
         blocks = [kv]
         while len(blocks) < reach + 1:
@@ -300,23 +344,19 @@
             blocks = blocks + [passed[i] for i in range(send)]
         bias = mask(block_docs, reach, group_size * BLK)
         biases = [bias[at] for at in range(reach)]
-        attended, first = attend(query_states, blocks, biases, *sizes, (), out_weight, width)
+        attended, last = attend(query_states, blocks, biases, *sizes, (), out_weight, width)
 
     received = []
     for step in range(1, groups):
         if step == 1:
-            row = [first] + list(project(attended, out_weight, 1, range(1, PARTS), width))
+            row = list(project(attended, out_weight, 1, range(PARTS - 1), width)) + [last]
         else:
             row = project(attended, out_weight, step, range(PARTS), width)
         received.append([turned(partial, "head", step) for partial in row])
     mine = project(attended, out_weight, 0, range(PARTS), width)
-    outs = []
-    for i in range(PARTS):
-        total = mine[i].astype(jnp.float32)
-        for row in received:
-            total = total + row[i].astype(jnp.float32)
-        outs.append(total.astype(jnp.bfloat16))
-    return jnp.concatenate(outs, axis=1)
+    columns = out_weight.shape[1] // groups
+    out = close([PARTS - 1, *range(PARTS - 2)], mine, received, columns)
+    return close([PARTS - 2], mine, received, columns, out)
 
 
 def solution(mesh):

time: 28 us -> 25.8 us (0.921)
  the two profiles are of different devices: /device:TPU:0 before, /device:TPU:24 now
where the time goes in v3:
time: 25.8 us; the launch traced here: 25.6 us
  waiting for transfers between devices  12.2 us (47%)
  starting transfers between devices  6.42 us (25%)
  Pallas kernels  5.84 us (23%)
  other arithmetic  1.03 us (4%)
    ppermute x4, waiting for transfers between devices, turned(): lax.ppermute(value, axis, [(source, (source + steps) % count) for source...  7.7 us
    ppermute x4, starting transfers between devices, turned(): lax.ppermute(value, axis, [(source, (source + steps) % count) for source...  4.18 us
    ppermute x2, waiting for transfers between devices, local(): lax.ppermute(kv, 'seq', list(enumerate(ring)))  4.13 us
    ppermute x2, starting transfers between devices, local(): lax.ppermute(kv, 'seq', list(enumerate(ring)))  1.99 us
    pallas_call x2, Pallas kernels, attend(): pl.pallas_call(functools.partial(attend_kernel, blocks, len(biases) < blo...  1.95 us
    pallas_call x2, Pallas kernels, close(): pl.pallas_call(functools.partial(close_kernel, tuple(parts), len(received...  1.49 us
    pallas_call x2, Pallas kernels, project(): pl.pallas_call(functools.partial(project_kernel, step, parts), out_shape=...  1.33 us
    pallas_call x1, Pallas kernels, opening(): pl.pallas_call(functools.partial(opening_kernel, gaps, kv_local, group_si...  1.05 us
  transfers between devices with their start and end apart: 8, of which 6 were waited for; matrix products, arithmetic and copies ran while one was open for 0% of the time, Pallas kernels for 16%

profile of v3, /device:TPU:24, one launch (start us, length us, event | category | flops | bytes accessed | tf_op | source)
XLA Modules:
  0.0 25.6 jit_solution(4331314547039827700)
XLA Ops:
  0.0 0.0 slice-start
  0.0 1.0 %pad_maximum_fusion.kv_in = bf16[128,512]{1,0:T(8,128)(2,1)S(1)} fusion(bf16[128,256]{1,0:T(8,128)(2,1)} %param.7, bf16[128,256]{1,0:T(8,128)(2,1)} %param.6), kind=kLoop, calls=%fused_computation | loop fusion | flops 262144 | bytes 262144 | tf_op jit(solution)/shard_map/max | solution.py:309
  1.0 0.0 copy-start
  1.0 0.0 copy-start.1
  1.1 0.0 slice-start.1
  1.1 0.1 collective-permute-start.2
  1.2 1.9 %collective-permute-start.1 = (bf16[128,512]{1,0:T(8,128)(2,1)S(1)}, bf16[128,512]{1,0:T(8,128)(2,1)S(1)}, u32[]{:S(2)}, u32[]{:S(2)}) collective-permute-start(bf16[128,512]{1,0:T(8,128)(2,1)S(1)} %shard_map.55.kv_ref), channel_id=1, source_target_pairs={{0,2},{2,0},{4,6},{6,10},{8,12},{10,14},{12,16},{14,4},{16,20},{18... | collective-permute-start | bytes 393224 | tf_op jit(solution)/shard_map/ppermute | solution.py:326
  3.1 0.0 copy-done
  3.1 0.0 copy-done.1
  3.1 1.1 %shard_map.56 = (f32[2,1,512]{2,1,0:T(1,128)S(1)}, f32[2,1,512]{2,1,0:T(1,128)S(1)}, f32[2,128,512]{2,1,0:T(8,128)S(1)}, f32[4,1,512]{2,1,0:T(1,128)S(1)}, bf16[128,512]{1,0:T(8,128)(2,1)S(1)}) custom-call(s32[16]{0:T(128)S(1)} %copy-done.1, bf16[128,1024]{1,0:T(8,128)(2,1)S(1)} %copy-done, bf16[128,512]{1,0:T(8,128)(2,1)S(1)} %shard_map.55.kv_ref), custom_call_target="tpu_custom_call" | custom-call | flops 500000000 | bytes 1000000 | tf_op jit(solution)/shard_map/pallas_call | solution.py:112
  4.1 0.1 collective-permute-start
  4.2 4.1 %collective-permute-done.2.refs_1_ = bf16[128,512]{1,0:T(8,128)(2,1)S(1)} collective-permute-done((bf16[128,512]{1,0:T(8,128)(2,1)S(1)}, bf16[128,512]{1,0:T(8,128)(2,1)S(1)}, u32[]{:S(2)}, u32[]{:S(2)}) %collective-permute-start.2) | collective-permute-done | bytes 131104 | tf_op jit(solution)/shard_map/ppermute | solution.py:326
  8.3 0.0 collective-permute-done.1.refs_0_
  8.4 0.2 collective-permute-start.3
  8.5 0.8 %shard_map.58 = (f32[2,1,512]{2,1,0:T(1,128)S(1)}, f32[2,1,512]{2,1,0:T(1,128)S(1)}, f32[2,128,512]{2,1,0:T(8,128)S(1)}) custom-call(bf16[128,1024]{1,0:T(8,128)(2,1)S(1)} %copy-done, bf16[128,512]{1,0:T(8,128)(2,1)S(1)} %collective-permute-done.1.refs_0_, bf16[128,512]{1,0:T(8,128)(2,1)S(1)} %collective-permute-done.2.refs_1_, ...), custom_call_target="tpu_custom_call" | custom-call | flops 1000000000 | bytes 2000000 | tf_op jit(solution)/shard_map/pallas_call | solution.py:214
  9.4 0.0 collective-permute-done.refs_0_
  9.4 0.4 %collective-permute-done.3.refs_1_ = bf16[128,512]{1,0:T(8,128)(2,1)S(1)} collective-permute-done((bf16[128,512]{1,0:T(8,128)(2,1)S(1)}, bf16[128,512]{1,0:T(8,128)(2,1)S(1)}, u32[]{:S(2)}, u32[]{:S(2)}) %collective-permute-start.3) | collective-permute-done | bytes 131104 | tf_op jit(solution)/shard_map/ppermute | solution.py:332
  9.8 0.0 slice-done
  9.8 0.0 slice-done.1
  9.8 1.1 %shard_map.59 = (bf16[128,1024]{1,0:T(8,128)(2,1)S(1)}, bf16[128,512]{1,0:T(8,128)(2,1)S(1)}) custom-call(bf16[128,1024]{1,0:T(8,128)(2,1)S(1)} %copy-done, bf16[128,512]{1,0:T(8,128)(2,1)S(1)} %collective-permute-done.refs_0_, bf16[128,512]{1,0:T(8,128)(2,1)S(1)} %collective-permute-done.3.refs_1_, f32[1,512]{1,0:T(1,128)S(1)} %get-tuple-element.42.refs_2_, ...), custom_call_target="tpu_custom_call" | custom-call | flops 1000000000 | bytes 2000000 | tf_op jit(solution)/shard_map/pallas_call | solution.py:214
  10.9 1.6 %collective-permute-start.5 = (bf16[128,512]{1,0:T(8,128)(2,1)S(1)}, bf16[128,512]{1,0:T(8,128)(2,1)S(1)}, u32[]{:S(2)}, u32[]{:S(2)}) collective-permute-start(bf16[128,512]{1,0:T(8,128)(2,1)S(1)} %get-tuple-element.36), channel_id=1, source_target_pairs={{0,1},{1,0},{2,3},{3,2},{4,5},{5,4},{6,7},{7,6},{8,9},{9,8},{10,11... | collective-permute-start | bytes 393224 | tf_op jit(solution)/shard_map/ppermute | solution.py:35
  12.5 0.6 %shard_map.61 = (bf16[128,512]{1,0:T(8,128)(2,1)S(1)}, bf16[128,512]{1,0:T(8,128)(2,1)S(1)}, bf16[128,512]{1,0:T(8,128)(2,1)S(1)}) custom-call(bf16[128,1024]{1,0:T(8,128)(2,1)S(1)} %get-tuple-element.30.a_ref, bf16[1024,4096]{1,0:T(8,128)(2,1)S(1)} %bitcast.9), custom_call_target="tpu_custom_call" | custom-call | flops 402653184 | bytes 1000000 | tf_op jit(solution)/shard_map/pallas_call | solution.py:239
  13.1 0.6 %collective-permute-start.6 = (bf16[128,512]{1,0:T(8,128)(2,1)S(1)}, bf16[128,512]{1,0:T(8,128)(2,1)S(1)}, u32[]{:S(2)}, u32[]{:S(2)}) collective-permute-start(bf16[128,512]{1,0:T(8,128)(2,1)S(1)} %get-tuple-element.37), channel_id=1, source_target_pairs={{0,1},{1,0},{2,3},{3,2},{4,5},{5,4},{6,7},{7,6},{8,9},{9,8},{10,11... | collective-permute-start | bytes 393224 | tf_op jit(solution)/shard_map/ppermute | solution.py:35
  13.7 1.5 %collective-permute-start.7 = (bf16[128,512]{1,0:T(8,128)(2,1)S(1)}, bf16[128,512]{1,0:T(8,128)(2,1)S(1)}, u32[]{:S(2)}, u32[]{:S(2)}) collective-permute-start(bf16[128,512]{1,0:T(8,128)(2,1)S(1)} %get-tuple-element.38), channel_id=1, source_target_pairs={{0,1},{1,0},{2,3},{3,2},{4,5},{5,4},{6,7},{7,6},{8,9},{9,8},{10,11... | collective-permute-start | bytes 393224 | tf_op jit(solution)/shard_map/ppermute | solution.py:35
  15.2 0.5 %collective-permute-start.4 = (bf16[128,512]{1,0:T(8,128)(2,1)S(1)}, bf16[128,512]{1,0:T(8,128)(2,1)S(1)}, u32[]{:S(2)}, u32[]{:S(2)}) collective-permute-start(bf16[128,512]{1,0:T(8,128)(2,1)S(1)} %get-tuple-element.32), channel_id=1, source_target_pairs={{0,1},{1,0},{2,3},{3,2},{4,5},{5,4},{6,7},{7,6},{8,9},{9,8},{10,11... | collective-permute-start | bytes 393224 | tf_op jit(solution)/shard_map/ppermute | solution.py:35
  15.7 0.7 %shard_map.60 = (bf16[128,512]{1,0:T(8,128)(2,1)S(1)}, bf16[128,512]{1,0:T(8,128)(2,1)S(1)}, bf16[128,512]{1,0:T(8,128)(2,1)S(1)}, bf16[128,512]{1,0:T(8,128)(2,1)S(1)}) custom-call(bf16[128,1024]{1,0:T(8,128)(2,1)S(1)} %get-tuple-element.30.a_ref, bf16[1024,4096]{1,0:T(8,128)(2,1)S(1)} %bitcast.9), custom_call_target="tpu_custom_call" | custom-call | flops 536870912 | bytes 1000000 | tf_op jit(solution)/shard_map/pallas_call | solution.py:239
  16.4 0.9 %collective-permute-done.5.refs_3_ = bf16[128,512]{1,0:T(8,128)(2,1)S(1)} collective-permute-done((bf16[128,512]{1,0:T(8,128)(2,1)S(1)}, bf16[128,512]{1,0:T(8,128)(2,1)S(1)}, u32[]{:S(2)}, u32[]{:S(2)}) %collective-permute-start.5) | collective-permute-done | bytes 131104 | tf_op jit(solution)/shard_map/ppermute | solution.py:35
  17.3 2.8 %collective-permute-done.6.refs_4_ = bf16[128,512]{1,0:T(8,128)(2,1)S(1)} collective-permute-done((bf16[128,512]{1,0:T(8,128)(2,1)S(1)}, bf16[128,512]{1,0:T(8,128)(2,1)S(1)}, u32[]{:S(2)}, u32[]{:S(2)}) %collective-permute-start.6) | collective-permute-done | bytes 131104 | tf_op jit(solution)/shard_map/ppermute | solution.py:35
  20.1 2.8 %collective-permute-done.7.refs_5_ = bf16[128,512]{1,0:T(8,128)(2,1)S(1)} collective-permute-done((bf16[128,512]{1,0:T(8,128)(2,1)S(1)}, bf16[128,512]{1,0:T(8,128)(2,1)S(1)}, u32[]{:S(2)}, u32[]{:S(2)}) %collective-permute-start.7) | collective-permute-done | bytes 131104 | tf_op jit(solution)/shard_map/ppermute | solution.py:35
  22.9 0.8 %shard_map.62.refs_2_ = bf16[128,2048]{1,0:T(8,128)(2,1)} custom-call(bf16[128,512]{1,0:T(8,128)(2,1)S(1)} %get-tuple-element.33.refs_0_, bf16[128,512]{1,0:T(8,128)(2,1)S(1)} %get-tuple-element.34.refs_1_, bf16[128,512]{1,0:T(8,128)(2,1)S(1)} %get-tuple-element.35.refs_2_, bf16[128,512]{1,0:T(8,128)(2,1)S(1)} %collective-permute-done.5.refs_3_, ...), custom_call_target="tpu_custom_call" | custom-call | flops 1000000 | bytes 1000000 | tf_op jit(solution)/shard_map/pallas_call | solution.py:274
  23.7 1.2 %collective-permute-done.4.refs_1_ = bf16[128,512]{1,0:T(8,128)(2,1)S(1)} collective-permute-done((bf16[128,512]{1,0:T(8,128)(2,1)S(1)}, bf16[128,512]{1,0:T(8,128)(2,1)S(1)}, u32[]{:S(2)}, u32[]{:S(2)}) %collective-permute-start.4) | collective-permute-done | bytes 131104 | tf_op jit(solution)/shard_map/ppermute | solution.py:35
  24.9 0.7 %shard_map.63 = bf16[128,2048]{1,0:T(8,128)(2,1)} custom-call(bf16[128,512]{1,0:T(8,128)(2,1)S(1)} %get-tuple-element.31.refs_0_, bf16[128,512]{1,0:T(8,128)(2,1)S(1)} %collective-permute-done.4.refs_1_, bf16[128,2048]{1,0:T(8,128)(2,1)} %shard_map.62.refs_2_), custom_call_target="tpu_custom_call", output_to_operand_aliasing={{}: (2, {})} | custom-call | flops 1000000 | bytes 1000000 | tf_op jit(solution)/shard_map/pallas_call | solution.py:274
  (4 shorter events, 0.0 us)
Async XLA Ops:
  0.0 9.8 %slice-start = ((s8[8388608]{0:T(1024)(128)(4,1)}), s8[4194304]{0:T(1024)(128)(4,1)S(1)}, s32[]{:S(2)}) async-start(s8[8388608]{0:T(1024)(128)(4,1)} %bitcast.8), calls=%async_computation | async-start | bytes 8388608
  1.0 2.1 %copy-start = (bf16[128,1024]{1,0:T(8,128)(2,1)S(1)}, bf16[128,1024]{1,0:T(8,128)(2,1)}, u32[]{:S(2)}) copy-start(bf16[128,1024]{1,0:T(8,128)(2,1)} %q_ref.5) | copy-start | bytes 786436
  1.0 2.0 %copy-start.1 = (s32[16]{0:T(128)S(1)}, s32[16]{0:T(128)}, u32[]{:S(2)}) copy-start(s32[16]{0:T(128)} %docs_ref.1) | copy-start | bytes 196
  1.1 8.7 %slice-start.1 = ((s8[8388608]{0:T(1024)(128)(4,1)}), s8[4194304]{0:T(1024)(128)(4,1)S(1)}, s32[]{:S(2)}) async-start(s8[8388608]{0:T(1024)(128)(4,1)} %bitcast.8), calls=%async_computation.1 | async-start | bytes 8388608
  1.1 7.3 %collective-permute-start.2 = (bf16[128,512]{1,0:T(8,128)(2,1)S(1)}, bf16[128,512]{1,0:T(8,128)(2,1)S(1)}, u32[]{:S(2)}, u32[]{:S(2)}) collective-permute-start(bf16[128,512]{1,0:T(8,128)(2,1)S(1)} %shard_map.55.kv_ref), channel_id=1, source_target_pairs={{0,4},{2,6},{4,8},{6,0},{8,2},{10,16},{12,14},{14,18},{16,10},{18,... | collective-permute-start | bytes 393224 | tf_op jit(solution)/shard_map/ppermute | solution.py:326
  1.2 7.2 %collective-permute-start.1 = (bf16[128,512]{1,0:T(8,128)(2,1)S(1)}, bf16[128,512]{1,0:T(8,128)(2,1)S(1)}, u32[]{:S(2)}, u32[]{:S(2)}) collective-permute-start(bf16[128,512]{1,0:T(8,128)(2,1)S(1)} %shard_map.55.kv_ref), channel_id=1, source_target_pairs={{0,2},{2,0},{4,6},{6,10},{8,12},{10,14},{12,16},{14,4},{16,20},{18... | collective-permute-start | bytes 393224 | tf_op jit(solution)/shard_map/ppermute | solution.py:326
  4.1 5.3 %collective-permute-start = (bf16[128,512]{1,0:T(8,128)(2,1)S(1)}, bf16[128,512]{1,0:T(8,128)(2,1)S(1)}, u32[]{:S(2)}, u32[]{:S(2)}) collective-permute-start(bf16[128,512]{1,0:T(8,128)(2,1)S(1)} %get-tuple-element.22), channel_id=1, source_target_pairs={{0,2},{2,8},{4,6},{6,12},{8,10},{10,0},{12,4},{14,20},{16,18},{18,... | collective-permute-start | bytes 393224 | tf_op jit(solution)/shard_map/ppermute | solution.py:330
  8.4 1.4 %collective-permute-start.3 = (bf16[128,512]{1,0:T(8,128)(2,1)S(1)}, bf16[128,512]{1,0:T(8,128)(2,1)S(1)}, u32[]{:S(2)}, u32[]{:S(2)}) collective-permute-start(bf16[128,512]{1,0:T(8,128)(2,1)S(1)} %shard_map.57), channel_id=1, source_target_pairs={{0,2},{2,0},{4,6},{6,4},{8,10},{10,8},{12,14},{14,12},{16,18},{18,... | collective-permute-start | bytes 393224 | tf_op jit(solution)/shard_map/ppermute | solution.py:332
  10.9 6.4 %collective-permute-start.5 = (bf16[128,512]{1,0:T(8,128)(2,1)S(1)}, bf16[128,512]{1,0:T(8,128)(2,1)S(1)}, u32[]{:S(2)}, u32[]{:S(2)}) collective-permute-start(bf16[128,512]{1,0:T(8,128)(2,1)S(1)} %get-tuple-element.36), channel_id=1, source_target_pairs={{0,1},{1,0},{2,3},{3,2},{4,5},{5,4},{6,7},{7,6},{8,9},{9,8},{10,11... | collective-permute-start | bytes 393224 | tf_op jit(solution)/shard_map/ppermute | solution.py:35
  13.1 7.0 %collective-permute-start.6 = (bf16[128,512]{1,0:T(8,128)(2,1)S(1)}, bf16[128,512]{1,0:T(8,128)(2,1)S(1)}, u32[]{:S(2)}, u32[]{:S(2)}) collective-permute-start(bf16[128,512]{1,0:T(8,128)(2,1)S(1)} %get-tuple-element.37), channel_id=1, source_target_pairs={{0,1},{1,0},{2,3},{3,2},{4,5},{5,4},{6,7},{7,6},{8,9},{9,8},{10,11... | collective-permute-start | bytes 393224 | tf_op jit(solution)/shard_map/ppermute | solution.py:35
  13.7 9.3 %collective-permute-start.7 = (bf16[128,512]{1,0:T(8,128)(2,1)S(1)}, bf16[128,512]{1,0:T(8,128)(2,1)S(1)}, u32[]{:S(2)}, u32[]{:S(2)}) collective-permute-start(bf16[128,512]{1,0:T(8,128)(2,1)S(1)} %get-tuple-element.38), channel_id=1, source_target_pairs={{0,1},{1,0},{2,3},{3,2},{4,5},{5,4},{6,7},{7,6},{8,9},{9,8},{10,11... | collective-permute-start | bytes 393224 | tf_op jit(solution)/shard_map/ppermute | solution.py:35
  15.2 9.8 %collective-permute-start.4 = (bf16[128,512]{1,0:T(8,128)(2,1)S(1)}, bf16[128,512]{1,0:T(8,128)(2,1)S(1)}, u32[]{:S(2)}, u32[]{:S(2)}) collective-permute-start(bf16[128,512]{1,0:T(8,128)(2,1)S(1)} %get-tuple-element.32), channel_id=1, source_target_pairs={{0,1},{1,0},{2,3},{3,2},{4,5},{5,4},{6,7},{7,6},{8,9},{9,8},{10,11... | collective-permute-start | bytes 393224 | tf_op jit(solution)/shard_map/ppermute | solution.py:35

commit v4 on v3

--- a/solution.py
+++ b/solution.py
@@ -11,7 +11,7 @@
 KH = 4
 BLK = 128
 DOC_BLK = 32
-PARTS = 4
+PARTS = (2, 2, 2, 2)
 ROUND = 4
 LOG2E = 1.4426950408889634
 MIB = 1024 * 1024
@@ -67,7 +67,7 @@
         out_specs=VMEM,
         input_output_aliases={0: 0},
         compiler_params=pltpu.CompilerParams(vmem_limit_bytes=2 * MIB),
-        cost_estimate=cost(10_000_000_000, 0),
+        cost_estimate=cost(6_000_000_000, 0),
     )(kv)
 
 
@@ -115,7 +115,7 @@
         in_specs=[SMEM, VMEM, VMEM],
         out_specs=[VMEM] * 5,
         compiler_params=pltpu.CompilerParams(vmem_limit_bytes=20 * MIB),
-        cost_estimate=cost(500_000_000, 1_000_000),
+        cost_estimate=cost(20_000_000_000, 0),
     )(docs, queries, kv)
     return state, bias, kv
 
@@ -191,7 +191,7 @@
                 ref[kv_head] = value
     if finish:
         out_ref, part_ref = refs
-        part_ref[...] = project_part(out_ref, w_ref, 1, PARTS - 1, part_ref.shape[1])
+        part_ref[...] = project_part(out_ref, w_ref, 1, finish)
 
 
 def first_column(columns, step):
@@ -200,20 +200,17 @@
     return pl.multiple_of(target * (columns // groups), 128)
 
 
-def attend(queries, kv_blocks, biases, kv_local, group_size, state, weights=None, width=0):
+def attend(queries, kv_blocks, biases, kv_local, group_size, state, weights=None, part=None):
     rows = group_size * BLK
-    if width:
-        out_shape = [
-            jax.ShapeDtypeStruct(queries.shape, jnp.bfloat16),
-            jax.ShapeDtypeStruct((BLK, width), jnp.bfloat16),
-        ]
+    if part:
+        out_shape = [jax.ShapeDtypeStruct(queries.shape, jnp.bfloat16), part_shape(part)]
     else:
         out_shape = [jax.ShapeDtypeStruct((kv_local, n, rows), jnp.float32) for n in (1, 1, HD)]
-    operands = [queries, *kv_blocks, *biases, *state] + ([weights] if width else [])
+    operands = [queries, *kv_blocks, *biases, *state] + ([weights] if part else [])
     blocks = len(kv_blocks)
     return pl.pallas_call(
         functools.partial(
-            attend_kernel, blocks, len(biases) < blocks, kv_local, group_size, bool(state), bool(width)
+            attend_kernel, blocks, len(biases) < blocks, kv_local, group_size, bool(state), part
         ),
         out_shape=out_shape,
         in_specs=[VMEM] * len(operands),
@@ -223,27 +220,33 @@
     )(*operands)
 
 
-def project_part(a_ref, w_ref, step, part, width):
-    begin = pl.multiple_of(first_column(w_ref.shape[1], step) + part * width, 128)
+def project_part(a_ref, w_ref, step, part):
+    begin = pl.multiple_of(first_column(w_ref.shape[1], step) + part.start, 128)
+    columns = pl.ds(begin, part.stop - part.start)
     return jnp.dot(
-        a_ref[...], w_ref[:, pl.ds(begin, width)], preferred_element_type=jnp.float32
+        a_ref[...], w_ref[:, columns], preferred_element_type=jnp.float32
     ).astype(jnp.bfloat16)
 
 
 def project_kernel(step, parts, a_ref, w_ref, *out_refs):
     for part, out_ref in zip(parts, out_refs):
-        out_ref[...] = project_part(a_ref, w_ref, step, part, out_ref.shape[1])
-
-
-def project(attended, weights, step, parts, width):
+        out_ref[...] = project_part(a_ref, w_ref, step, part)
+
+
+def project(attended, weights, step, parts):
+    width = sum(part.stop - part.start for part in parts)
     return pl.pallas_call(
         functools.partial(project_kernel, step, parts),
-        out_shape=[jax.ShapeDtypeStruct((BLK, width), jnp.bfloat16)] * len(parts),
+        out_shape=[part_shape(part) for part in parts],
         in_specs=[VMEM, VMEM],
         out_specs=[VMEM] * len(parts),
         compiler_params=pltpu.CompilerParams(vmem_limit_bytes=20 * MIB),
-        cost_estimate=cost(2 * BLK * width * len(parts) * attended.shape[1], 1_000_000),
+        cost_estimate=cost(2 * BLK * width * attended.shape[1], 1_000_000),
     )(attended, weights)
+
+
+def part_shape(part):
+    return jax.ShapeDtypeStruct((BLK, part.stop - part.start), jnp.bfloat16)
 
 
 def close_kernel(parts, each, resume, *refs):
@@ -252,33 +255,32 @@
     other_refs = [[refs.pop(0) for _ in range(each)] for _ in parts]
     if resume:
         refs.pop(0)
-    out_ref, sums, sems = refs
-    width = mine_refs[0].shape[1]
+    out_ref, *sum_refs, sems = refs
     copies = []
     for at, part in enumerate(parts):
         total = mine_refs[at][...].astype(jnp.float32)
         for ref in other_refs[at]:
             total = total + ref[...].astype(jnp.float32)
-        sums[at] = total.astype(sums.dtype)
-        columns = slice(part * width, (part + 1) * width)
-        copies.append(pltpu.make_async_copy(sums.at[at], out_ref.at[:, columns], sems.at[at]))
+        sum_refs[at][...] = total.astype(sum_refs[at].dtype)
+        copies.append(pltpu.make_async_copy(sum_refs[at], out_ref.at[:, part], sems.at[at]))
         copies[-1].start()
     for copy in copies:
         copy.wait()
 
 
-def close(parts, mine, received, columns, out=None):
-    rows, width = mine[0].shape
-    others = [row[part] for part in parts for row in received]
-    operands = [mine[part] for part in parts] + others + ([] if out is None else [out])
-    return pl.pallas_call(
-        functools.partial(close_kernel, tuple(parts), len(received), out is not None),
-        out_shape=jax.ShapeDtypeStruct((rows, columns), mine[0].dtype),
-        in_specs=[VMEM] * (len(parts) + len(others)) + ([] if out is None else [HBM]),
+def close(chosen, parts, mine, received, out=None):
+    others = [row[at] for at in chosen for row in received]
+    operands = [mine[at] for at in chosen] + others + ([] if out is None else [out])
+    return pl.pallas_call(
+        functools.partial(
+            close_kernel, [parts[at] for at in chosen], len(received), out is not None
+        ),
+        out_shape=jax.ShapeDtypeStruct((BLK, parts[-1].stop), jnp.bfloat16),
+        in_specs=[VMEM] * (len(chosen) + len(others)) + ([] if out is None else [HBM]),
         out_specs=HBM,
         scratch_shapes=[
-            pltpu.VMEM((len(parts), rows, width), mine[0].dtype),
-            pltpu.SemaphoreType.DMA((len(parts),)),
+            *[pltpu.VMEM((BLK, parts[at].stop - parts[at].start), jnp.bfloat16) for at in chosen],
+            pltpu.SemaphoreType.DMA((len(chosen),)),
         ],
         input_output_aliases={} if out is None else {len(operands) - 1: 0},
         compiler_params=pltpu.CompilerParams(vmem_limit_bytes=8 * MIB),
@@ -317,7 +319,9 @@
     groups = lax.axis_size("head")
     assert tokens_here == BLK and block_docs.shape[0] == count
     reach = min(DOC_BLK, count // 4) - 1
-    width = out_weight.shape[1] // groups // PARTS
+    eighth = out_weight.shape[1] // groups // 8
+    ends = [eighth * sum(PARTS[:at]) for at in range(len(PARTS) + 1)]
+    parts = [slice(begin, end) for begin, end in zip(ends, ends[1:])]
     sizes = (kv_local, group_size)
 
     kv = hold(side_by_side(key_states, value_states))
@@ -333,7 +337,7 @@
         biases = [bias[at] for at in range(len(gaps))]
         state = attend(query_states, arrived[1:], biases[1:3], *sizes, state)
         attended, last = attend(
-            query_states, [arrived[0], late], [biases[0], biases[3]], *sizes, state, out_weight, width
+            query_states, [arrived[0], late], [biases[0], biases[3]], *sizes, state, out_weight, parts[-1]
         )
     else:
         blocks = [kv]
@@ -344,19 +348,20 @@
             blocks = blocks + [passed[i] for i in range(send)]
         bias = mask(block_docs, reach, group_size * BLK)
         biases = [bias[at] for at in range(reach)]
-        attended, last = attend(query_states, blocks, biases, *sizes, (), out_weight, width)
+        attended, last = attend(query_states, blocks, biases, *sizes, (), out_weight, parts[-1])
 
     received = []
     for step in range(1, groups):
         if step == 1:
-            row = list(project(attended, out_weight, 1, range(PARTS - 1), width)) + [last]
+            row = [*project(attended, out_weight, 1, parts[:-1]), last]
         else:
-            row = project(attended, out_weight, step, range(PARTS), width)
+            row = project(attended, out_weight, step, parts)
         received.append([turned(partial, "head", step) for partial in row])
-    mine = project(attended, out_weight, 0, range(PARTS), width)
-    columns = out_weight.shape[1] // groups
-    out = close([PARTS - 1, *range(PARTS - 2)], mine, received, columns)
-    return close([PARTS - 2], mine, received, columns, out)
+    mine = project(attended, out_weight, 0, parts)
+    late = len(parts) - 2
+    early = [at for at in range(len(parts)) if at != late]
+    out = close(early, parts, mine, received)
+    return close([late], parts, mine, received, out)
 
 
 def solution(mesh):

time: 25.8 us -> 25.7 us (level)
  no operation moved by 1% of the time
where the time goes in v4:
time: 25.7 us; the launch traced here: 25.5 us
  waiting for transfers between devices  12.2 us (47%)
  starting transfers between devices  6.41 us (25%)
  Pallas kernels  5.84 us (23%)
  other arithmetic  0.88 us (3%)
    ppermute x4, waiting for transfers between devices, turned(): lax.ppermute(value, axis, [(source, (source + steps) % count) for source...  7.7 us
    ppermute x4, starting transfers between devices, turned(): lax.ppermute(value, axis, [(source, (source + steps) % count) for source...  4.18 us
    ppermute x2, waiting for transfers between devices, local(): lax.ppermute(kv, 'seq', list(enumerate(ring)))  4.13 us
    ppermute x2, starting transfers between devices, local(): lax.ppermute(kv, 'seq', list(enumerate(ring)))  1.99 us
    pallas_call x2, Pallas kernels, attend(): pl.pallas_call(functools.partial(attend_kernel, blocks, len(biases) < blo...  1.95 us
    pallas_call x2, Pallas kernels, close(): pl.pallas_call(functools.partial(close_kernel, [parts[at] for at in chose...  1.49 us
    pallas_call x2, Pallas kernels, project(): pl.pallas_call(functools.partial(project_kernel, step, parts), out_shape=...  1.33 us
    pallas_call x1, Pallas kernels, opening(): pl.pallas_call(functools.partial(opening_kernel, gaps, kv_local, group_si...  1.05 us
  transfers between devices with their start and end apart: 8, of which 6 were waited for; matrix products, arithmetic and copies ran while one was open for 0% of the time, Pallas kernels for 16%

profile of v4, /device:TPU:24, one launch (start us, length us, event | category | flops | bytes accessed | tf_op | source)
XLA Modules:
  0.0 25.5 jit_solution(4755017519743835957)
XLA Ops:
  0.0 0.9 %pad_maximum_fusion.kv_in = bf16[128,512]{1,0:T(8,128)(2,1)S(1)} fusion(bf16[128,256]{1,0:T(8,128)(2,1)} %param.7, bf16[128,256]{1,0:T(8,128)(2,1)} %param.6), kind=kLoop, calls=%fused_computation | loop fusion | flops 262144 | bytes 262144 | tf_op jit(solution)/shard_map/max | solution.py:311
  0.9 0.0 copy-start
  0.9 0.0 copy-start.1
  0.9 0.0 slice-start
  0.9 0.0 slice-start.1
  0.9 0.1 collective-permute-start.2
  1.0 1.9 %collective-permute-start.1 = (bf16[128,512]{1,0:T(8,128)(2,1)S(1)}, bf16[128,512]{1,0:T(8,128)(2,1)S(1)}, u32[]{:S(2)}, u32[]{:S(2)}) collective-permute-start(bf16[128,512]{1,0:T(8,128)(2,1)S(1)} %shard_map.55.kv_ref), channel_id=1, source_target_pairs={{0,2},{2,0},{4,6},{6,10},{8,12},{10,14},{12,16},{14,4},{16,20},{18... | collective-permute-start | bytes 393224 | tf_op jit(solution)/shard_map/ppermute | solution.py:330
  2.9 0.0 copy-done
  2.9 0.0 copy-done.1
  3.0 1.1 %shard_map.56 = (f32[2,1,512]{2,1,0:T(1,128)S(1)}, f32[2,1,512]{2,1,0:T(1,128)S(1)}, f32[2,128,512]{2,1,0:T(8,128)S(1)}, f32[4,1,512]{2,1,0:T(1,128)S(1)}, bf16[128,512]{1,0:T(8,128)(2,1)S(1)}) custom-call(s32[16]{0:T(128)S(1)} %copy-done.1, bf16[128,1024]{1,0:T(8,128)(2,1)S(1)} %copy-done, bf16[128,512]{1,0:T(8,128)(2,1)S(1)} %shard_map.55.kv_ref), custom_call_target="tpu_custom_call" | custom-call | flops 20000000000 | tf_op jit(solution)/shard_map/pallas_call | solution.py:112
  4.0 0.1 collective-permute-start
  4.1 4.1 %collective-permute-done.2.refs_1_ = bf16[128,512]{1,0:T(8,128)(2,1)S(1)} collective-permute-done((bf16[128,512]{1,0:T(8,128)(2,1)S(1)}, bf16[128,512]{1,0:T(8,128)(2,1)S(1)}, u32[]{:S(2)}, u32[]{:S(2)}) %collective-permute-start.2) | collective-permute-done | bytes 131104 | tf_op jit(solution)/shard_map/ppermute | solution.py:330
  8.2 0.0 collective-permute-done.1.refs_0_
  8.2 0.2 collective-permute-start.3
  8.4 0.8 %shard_map.58 = (f32[2,1,512]{2,1,0:T(1,128)S(1)}, f32[2,1,512]{2,1,0:T(1,128)S(1)}, f32[2,128,512]{2,1,0:T(8,128)S(1)}) custom-call(bf16[128,1024]{1,0:T(8,128)(2,1)S(1)} %copy-done, bf16[128,512]{1,0:T(8,128)(2,1)S(1)} %collective-permute-done.1.refs_0_, bf16[128,512]{1,0:T(8,128)(2,1)S(1)} %collective-permute-done.2.refs_1_, ...), custom_call_target="tpu_custom_call" | custom-call | flops 1000000000 | bytes 2000000 | tf_op jit(solution)/shard_map/pallas_call | solution.py:211
  9.3 0.0 collective-permute-done.refs_0_
  9.3 0.4 %collective-permute-done.3.refs_1_ = bf16[128,512]{1,0:T(8,128)(2,1)S(1)} collective-permute-done((bf16[128,512]{1,0:T(8,128)(2,1)S(1)}, bf16[128,512]{1,0:T(8,128)(2,1)S(1)}, u32[]{:S(2)}, u32[]{:S(2)}) %collective-permute-start.3) | collective-permute-done | bytes 131104 | tf_op jit(solution)/shard_map/ppermute | solution.py:336
  9.6 0.0 slice-done
  9.6 0.0 slice-done.1
  9.6 1.1 %shard_map.59 = (bf16[128,1024]{1,0:T(8,128)(2,1)S(1)}, bf16[128,512]{1,0:T(8,128)(2,1)S(1)}) custom-call(bf16[128,1024]{1,0:T(8,128)(2,1)S(1)} %copy-done, bf16[128,512]{1,0:T(8,128)(2,1)S(1)} %collective-permute-done.refs_0_, bf16[128,512]{1,0:T(8,128)(2,1)S(1)} %collective-permute-done.3.refs_1_, f32[1,512]{1,0:T(1,128)S(1)} %get-tuple-element.42.refs_2_, ...), custom_call_target="tpu_custom_call" | custom-call | flops 1000000000 | bytes 2000000 | tf_op jit(solution)/shard_map/pallas_call | solution.py:211
  10.8 1.6 %collective-permute-start.7 = (bf16[128,512]{1,0:T(8,128)(2,1)S(1)}, bf16[128,512]{1,0:T(8,128)(2,1)S(1)}, u32[]{:S(2)}, u32[]{:S(2)}) collective-permute-start(bf16[128,512]{1,0:T(8,128)(2,1)S(1)} %get-tuple-element.38), channel_id=1, source_target_pairs={{0,1},{1,0},{2,3},{3,2},{4,5},{5,4},{6,7},{7,6},{8,9},{9,8},{10,11... | collective-permute-start | bytes 393224 | tf_op jit(solution)/shard_map/ppermute | solution.py:35
  12.3 0.6 %shard_map.61 = (bf16[128,512]{1,0:T(8,128)(2,1)S(1)}, bf16[128,512]{1,0:T(8,128)(2,1)S(1)}, bf16[128,512]{1,0:T(8,128)(2,1)S(1)}) custom-call(bf16[128,1024]{1,0:T(8,128)(2,1)S(1)} %get-tuple-element.30.a_ref, bf16[1024,4096]{1,0:T(8,128)(2,1)S(1)} %bitcast.9), custom_call_target="tpu_custom_call" | custom-call | flops 402653184 | bytes 1000000 | tf_op jit(solution)/shard_map/pallas_call | solution.py:238
  13.0 0.6 %collective-permute-start.5 = (bf16[128,512]{1,0:T(8,128)(2,1)S(1)}, bf16[128,512]{1,0:T(8,128)(2,1)S(1)}, u32[]{:S(2)}, u32[]{:S(2)}) collective-permute-start(bf16[128,512]{1,0:T(8,128)(2,1)S(1)} %get-tuple-element.36), channel_id=1, source_target_pairs={{0,1},{1,0},{2,3},{3,2},{4,5},{5,4},{6,7},{7,6},{8,9},{9,8},{10,11... | collective-permute-start | bytes 393224 | tf_op jit(solution)/shard_map/ppermute | solution.py:35
  13.5 1.5 %collective-permute-start.6 = (bf16[128,512]{1,0:T(8,128)(2,1)S(1)}, bf16[128,512]{1,0:T(8,128)(2,1)S(1)}, u32[]{:S(2)}, u32[]{:S(2)}) collective-permute-start(bf16[128,512]{1,0:T(8,128)(2,1)S(1)} %get-tuple-element.37), channel_id=1, source_target_pairs={{0,1},{1,0},{2,3},{3,2},{4,5},{5,4},{6,7},{7,6},{8,9},{9,8},{10,11... | collective-permute-start | bytes 393224 | tf_op jit(solution)/shard_map/ppermute | solution.py:35
  15.0 0.5 %collective-permute-start.4 = (bf16[128,512]{1,0:T(8,128)(2,1)S(1)}, bf16[128,512]{1,0:T(8,128)(2,1)S(1)}, u32[]{:S(2)}, u32[]{:S(2)}) collective-permute-start(bf16[128,512]{1,0:T(8,128)(2,1)S(1)} %get-tuple-element.32), channel_id=1, source_target_pairs={{0,1},{1,0},{2,3},{3,2},{4,5},{5,4},{6,7},{7,6},{8,9},{9,8},{10,11... | collective-permute-start | bytes 393224 | tf_op jit(solution)/shard_map/ppermute | solution.py:35
  15.6 0.7 %shard_map.60 = (bf16[128,512]{1,0:T(8,128)(2,1)S(1)}, bf16[128,512]{1,0:T(8,128)(2,1)S(1)}, bf16[128,512]{1,0:T(8,128)(2,1)S(1)}, bf16[128,512]{1,0:T(8,128)(2,1)S(1)}) custom-call(bf16[128,1024]{1,0:T(8,128)(2,1)S(1)} %get-tuple-element.30.a_ref, bf16[1024,4096]{1,0:T(8,128)(2,1)S(1)} %bitcast.9), custom_call_target="tpu_custom_call" | custom-call | flops 536870912 | bytes 1000000 | tf_op jit(solution)/shard_map/pallas_call | solution.py:238
  16.3 0.9 %collective-permute-done.7.refs_5_ = bf16[128,512]{1,0:T(8,128)(2,1)S(1)} collective-permute-done((bf16[128,512]{1,0:T(8,128)(2,1)S(1)}, bf16[128,512]{1,0:T(8,128)(2,1)S(1)}, u32[]{:S(2)}, u32[]{:S(2)}) %collective-permute-start.7) | collective-permute-done | bytes 131104 | tf_op jit(solution)/shard_map/ppermute | solution.py:35
  17.2 2.8 %collective-permute-done.5.refs_3_ = bf16[128,512]{1,0:T(8,128)(2,1)S(1)} collective-permute-done((bf16[128,512]{1,0:T(8,128)(2,1)S(1)}, bf16[128,512]{1,0:T(8,128)(2,1)S(1)}, u32[]{:S(2)}, u32[]{:S(2)}) %collective-permute-start.5) | collective-permute-done | bytes 131104 | tf_op jit(solution)/shard_map/ppermute | solution.py:35
  20.0 2.8 %collective-permute-done.6.refs_4_ = bf16[128,512]{1,0:T(8,128)(2,1)S(1)} collective-permute-done((bf16[128,512]{1,0:T(8,128)(2,1)S(1)}, bf16[128,512]{1,0:T(8,128)(2,1)S(1)}, u32[]{:S(2)}, u32[]{:S(2)}) %collective-permute-start.6) | collective-permute-done | bytes 131104 | tf_op jit(solution)/shard_map/ppermute | solution.py:35
  22.8 0.8 %shard_map.62.refs_2_ = bf16[128,2048]{1,0:T(8,128)(2,1)} custom-call(bf16[128,512]{1,0:T(8,128)(2,1)S(1)} %get-tuple-element.33.refs_0_, bf16[128,512]{1,0:T(8,128)(2,1)S(1)} %get-tuple-element.34.refs_1_, bf16[128,512]{1,0:T(8,128)(2,1)S(1)} %get-tuple-element.35.refs_2_, bf16[128,512]{1,0:T(8,128)(2,1)S(1)} %collective-permute-done.5.refs_3_, ...), custom_call_target="tpu_custom_call" | custom-call | flops 1000000 | bytes 1000000 | tf_op jit(solution)/shard_map/pallas_call | solution.py:274
  23.6 1.2 %collective-permute-done.4.refs_1_ = bf16[128,512]{1,0:T(8,128)(2,1)S(1)} collective-permute-done((bf16[128,512]{1,0:T(8,128)(2,1)S(1)}, bf16[128,512]{1,0:T(8,128)(2,1)S(1)}, u32[]{:S(2)}, u32[]{:S(2)}) %collective-permute-start.4) | collective-permute-done | bytes 131104 | tf_op jit(solution)/shard_map/ppermute | solution.py:35
  24.8 0.7 %shard_map.63 = bf16[128,2048]{1,0:T(8,128)(2,1)} custom-call(bf16[128,512]{1,0:T(8,128)(2,1)S(1)} %get-tuple-element.31.refs_0_, bf16[128,512]{1,0:T(8,128)(2,1)S(1)} %collective-permute-done.4.refs_1_, bf16[128,2048]{1,0:T(8,128)(2,1)} %shard_map.62.refs_2_), custom_call_target="tpu_custom_call", output_to_operand_aliasing={{}: (2, {})} | custom-call | flops 1000000 | bytes 1000000 | tf_op jit(solution)/shard_map/pallas_call | solution.py:274
  (4 shorter events, 0.0 us)
Async XLA Ops:
  0.9 2.1 %copy-start = (bf16[128,1024]{1,0:T(8,128)(2,1)S(1)}, bf16[128,1024]{1,0:T(8,128)(2,1)}, u32[]{:S(2)}) copy-start(bf16[128,1024]{1,0:T(8,128)(2,1)} %q_ref.5) | copy-start | bytes 786436
  0.9 2.1 %copy-start.1 = (s32[16]{0:T(128)S(1)}, s32[16]{0:T(128)}, u32[]{:S(2)}) copy-start(s32[16]{0:T(128)} %docs_ref.1) | copy-start | bytes 196
  0.9 8.7 %slice-start = ((s8[8388608]{0:T(1024)(128)(4,1)}), s8[4194304]{0:T(1024)(128)(4,1)S(1)}, s32[]{:S(2)}) async-start(s8[8388608]{0:T(1024)(128)(4,1)} %bitcast.8), calls=%async_computation | async-start | bytes 8388608
  0.9 8.7 %slice-start.1 = ((s8[8388608]{0:T(1024)(128)(4,1)}), s8[4194304]{0:T(1024)(128)(4,1)S(1)}, s32[]{:S(2)}) async-start(s8[8388608]{0:T(1024)(128)(4,1)} %bitcast.8), calls=%async_computation.1 | async-start | bytes 8388608
  0.9 7.3 %collective-permute-start.2 = (bf16[128,512]{1,0:T(8,128)(2,1)S(1)}, bf16[128,512]{1,0:T(8,128)(2,1)S(1)}, u32[]{:S(2)}, u32[]{:S(2)}) collective-permute-start(bf16[128,512]{1,0:T(8,128)(2,1)S(1)} %shard_map.55.kv_ref), channel_id=1, source_target_pairs={{0,4},{2,6},{4,8},{6,0},{8,2},{10,16},{12,14},{14,18},{16,10},{18,... | collective-permute-start | bytes 393224 | tf_op jit(solution)/shard_map/ppermute | solution.py:330
  1.0 7.2 %collective-permute-start.1 = (bf16[128,512]{1,0:T(8,128)(2,1)S(1)}, bf16[128,512]{1,0:T(8,128)(2,1)S(1)}, u32[]{:S(2)}, u32[]{:S(2)}) collective-permute-start(bf16[128,512]{1,0:T(8,128)(2,1)S(1)} %shard_map.55.kv_ref), channel_id=1, source_target_pairs={{0,2},{2,0},{4,6},{6,10},{8,12},{10,14},{12,16},{14,4},{16,20},{18... | collective-permute-start | bytes 393224 | tf_op jit(solution)/shard_map/ppermute | solution.py:330
  4.0 5.2 %collective-permute-start = (bf16[128,512]{1,0:T(8,128)(2,1)S(1)}, bf16[128,512]{1,0:T(8,128)(2,1)S(1)}, u32[]{:S(2)}, u32[]{:S(2)}) collective-permute-start(bf16[128,512]{1,0:T(8,128)(2,1)S(1)} %get-tuple-element.22), channel_id=1, source_target_pairs={{0,2},{2,8},{4,6},{6,12},{8,10},{10,0},{12,4},{14,20},{16,18},{18,... | collective-permute-start | bytes 393224 | tf_op jit(solution)/shard_map/ppermute | solution.py:334
  8.2 1.4 %collective-permute-start.3 = (bf16[128,512]{1,0:T(8,128)(2,1)S(1)}, bf16[128,512]{1,0:T(8,128)(2,1)S(1)}, u32[]{:S(2)}, u32[]{:S(2)}) collective-permute-start(bf16[128,512]{1,0:T(8,128)(2,1)S(1)} %shard_map.57), channel_id=1, source_target_pairs={{0,2},{2,0},{4,6},{6,4},{8,10},{10,8},{12,14},{14,12},{16,18},{18,... | collective-permute-start | bytes 393224 | tf_op jit(solution)/shard_map/ppermute | solution.py:336
  10.8 6.4 %collective-permute-start.7 = (bf16[128,512]{1,0:T(8,128)(2,1)S(1)}, bf16[128,512]{1,0:T(8,128)(2,1)S(1)}, u32[]{:S(2)}, u32[]{:S(2)}) collective-permute-start(bf16[128,512]{1,0:T(8,128)(2,1)S(1)} %get-tuple-element.38), channel_id=1, source_target_pairs={{0,1},{1,0},{2,3},{3,2},{4,5},{5,4},{6,7},{7,6},{8,9},{9,8},{10,11... | collective-permute-start | bytes 393224 | tf_op jit(solution)/shard_map/ppermute | solution.py:35
  13.0 7.0 %collective-permute-start.5 = (bf16[128,512]{1,0:T(8,128)(2,1)S(1)}, bf16[128,512]{1,0:T(8,128)(2,1)S(1)}, u32[]{:S(2)}, u32[]{:S(2)}) collective-permute-start(bf16[128,512]{1,0:T(8,128)(2,1)S(1)} %get-tuple-element.36), channel_id=1, source_target_pairs={{0,1},{1,0},{2,3},{3,2},{4,5},{5,4},{6,7},{7,6},{8,9},{9,8},{10,11... | collective-permute-start | bytes 393224 | tf_op jit(solution)/shard_map/ppermute | solution.py:35
  13.5 9.3 %collective-permute-start.6 = (bf16[128,512]{1,0:T(8,128)(2,1)S(1)}, bf16[128,512]{1,0:T(8,128)(2,1)S(1)}, u32[]{:S(2)}, u32[]{:S(2)}) collective-permute-start(bf16[128,512]{1,0:T(8,128)(2,1)S(1)} %get-tuple-element.37), channel_id=1, source_target_pairs={{0,1},{1,0},{2,3},{3,2},{4,5},{5,4},{6,7},{7,6},{8,9},{9,8},{10,11... | collective-permute-start | bytes 393224 | tf_op jit(solution)/shard_map/ppermute | solution.py:35
  15.0 9.8 %collective-permute-start.4 = (bf16[128,512]{1,0:T(8,128)(2,1)S(1)}, bf16[128,512]{1,0:T(8,128)(2,1)S(1)}, u32[]{:S(2)}, u32[]{:S(2)}) collective-permute-start(bf16[128,512]{1,0:T(8,128)(2,1)S(1)} %get-tuple-element.32), channel_id=1, source_target_pairs={{0,1},{1,0},{2,3},{3,2},{4,5},{5,4},{6,7},{7,6},{8,9},{9,8},{10,11... | collective-permute-start | bytes 393224 | tf_op jit(solution)/shard_map/ppermute | solution.py:35

commit v5 on v4

--- a/solution.py
+++ b/solution.py
@@ -11,7 +11,7 @@
 KH = 4
 BLK = 128
 DOC_BLK = 32
-PARTS = (2, 2, 2, 2)
+PARTS = (2, 4, 2)
 ROUND = 4
 LOG2E = 1.4426950408889634
 MIB = 1024 * 1024
@@ -241,7 +241,7 @@
         in_specs=[VMEM, VMEM],
         out_specs=[VMEM] * len(parts),
         compiler_params=pltpu.CompilerParams(vmem_limit_bytes=20 * MIB),
-        cost_estimate=cost(2 * BLK * width * attended.shape[1], 1_000_000),
+        cost_estimate=cost(4_000_000_000, 0),
     )(attended, weights)
 
 
@@ -336,8 +336,8 @@
         late = lax.ppermute(second, "seq", [(i, i ^ 1) for i in range(count)])
         biases = [bias[at] for at in range(len(gaps))]
         state = attend(query_states, arrived[1:], biases[1:3], *sizes, state)
-        attended, last = attend(
-            query_states, [arrived[0], late], [biases[0], biases[3]], *sizes, state, out_weight, parts[-1]
+        attended, first = attend(
+            query_states, [arrived[0], late], [biases[0], biases[3]], *sizes, state, out_weight, parts[0]
         )
     else:
         blocks = [kv]
@@ -348,17 +348,17 @@
             blocks = blocks + [passed[i] for i in range(send)]
         bias = mask(block_docs, reach, group_size * BLK)
         biases = [bias[at] for at in range(reach)]
-        attended, last = attend(query_states, blocks, biases, *sizes, (), out_weight, parts[-1])
+        attended, first = attend(query_states, blocks, biases, *sizes, (), out_weight, parts[0])
 
     received = []
     for step in range(1, groups):
         if step == 1:
-            row = [*project(attended, out_weight, 1, parts[:-1]), last]
+            row = [first, *project(attended, out_weight, 1, parts[1:])]
         else:
             row = project(attended, out_weight, step, parts)
         received.append([turned(partial, "head", step) for partial in row])
     mine = project(attended, out_weight, 0, parts)
-    late = len(parts) - 2
+    late = 1
     early = [at for at in range(len(parts)) if at != late]
     out = close(early, parts, mine, received)
     return close([late], parts, mine, received, out)

time: 25.7 us -> 25.7 us (level)
  waiting for transfers between devices: 12.2 us -> 12.8 us
  starting transfers between devices: 6.41 us -> 5.91 us
    ppermute x4 -> x3, waiting for transfers between devices: 7.7 us -> 8.25 us  [turned(): lax.ppermute(value, axis, [(source, (source + steps) % count) for source...]
    ppermute x4 -> x3, starting transfers between devices: 4.18 us -> 3.67 us  [turned(): lax.ppermute(value, axis, [(source, (source + steps) % count) for source...]
  transfers between devices with their start and end apart: 8 -> 7, of which waited for: 6 -> 5; matrix products, arithmetic and copies ran while one was open for 0% -> 0% of each run, Pallas kernels for 16% -> 16%
where the time goes in v5:
time: 25.7 us; the launch traced here: 25.6 us
  waiting for transfers between devices  12.8 us (50%)
  starting transfers between devices  5.91 us (23%)
  Pallas kernels  5.88 us (23%)
  other arithmetic  0.88 us (3%)
    ppermute x3, waiting for transfers between devices, turned(): lax.ppermute(value, axis, [(source, (source + steps) % count) for source...  8.25 us
    ppermute x2, waiting for transfers between devices, local(): lax.ppermute(kv, 'seq', list(enumerate(ring)))  4.13 us
    ppermute x3, starting transfers between devices, turned(): lax.ppermute(value, axis, [(source, (source + steps) % count) for source...  3.67 us
    ppermute x2, starting transfers between devices, local(): lax.ppermute(kv, 'seq', list(enumerate(ring)))  1.99 us
    pallas_call x2, Pallas kernels, attend(): pl.pallas_call(functools.partial(attend_kernel, blocks, len(biases) < blo...  1.96 us
    pallas_call x2, Pallas kernels, close(): pl.pallas_call(functools.partial(close_kernel, [parts[at] for at in chose...  1.52 us
    pallas_call x2, Pallas kernels, project(): pl.pallas_call(functools.partial(project_kernel, step, parts), out_shape=...  1.34 us
    pallas_call x1, Pallas kernels, opening(): pl.pallas_call(functools.partial(opening_kernel, gaps, kv_local, group_si...  1.05 us
  transfers between devices with their start and end apart: 7, of which 5 were waited for; matrix products, arithmetic and copies ran while one was open for 0% of the time, Pallas kernels for 16%

profile of v5, /device:TPU:24, one launch (start us, length us, event | category | flops | bytes accessed | tf_op | source)
XLA Modules:
  0.0 25.6 jit_solution(13955723746956768543)
XLA Ops:
  0.0 0.9 %pad_maximum_fusion.kv_in = bf16[128,512]{1,0:T(8,128)(2,1)S(1)} fusion(bf16[128,256]{1,0:T(8,128)(2,1)} %param.7, bf16[128,256]{1,0:T(8,128)(2,1)} %param.6), kind=kLoop, calls=%fused_computation | loop fusion | flops 262144 | bytes 262144 | tf_op jit(solution)/shard_map/max | solution.py:311
  0.9 0.0 copy-start
  0.9 0.0 copy-start.1
  0.9 0.0 slice-start
  0.9 0.0 slice-start.1
  0.9 0.1 collective-permute-start.2
  1.0 1.9 %collective-permute-start.1 = (bf16[128,512]{1,0:T(8,128)(2,1)S(1)}, bf16[128,512]{1,0:T(8,128)(2,1)S(1)}, u32[]{:S(2)}, u32[]{:S(2)}) collective-permute-start(bf16[128,512]{1,0:T(8,128)(2,1)S(1)} %shard_map.55.kv_ref), channel_id=1, source_target_pairs={{0,2},{2,0},{4,6},{6,10},{8,12},{10,14},{12,16},{14,4},{16,20},{18... | collective-permute-start | bytes 393224 | tf_op jit(solution)/shard_map/ppermute | solution.py:330
  2.9 0.0 copy-done
  2.9 0.0 copy-done.1
  3.0 1.1 %shard_map.56 = (f32[2,1,512]{2,1,0:T(1,128)S(1)}, f32[2,1,512]{2,1,0:T(1,128)S(1)}, f32[2,128,512]{2,1,0:T(8,128)S(1)}, f32[4,1,512]{2,1,0:T(1,128)S(1)}, bf16[128,512]{1,0:T(8,128)(2,1)S(1)}) custom-call(s32[16]{0:T(128)S(1)} %copy-done.1, bf16[128,1024]{1,0:T(8,128)(2,1)S(1)} %copy-done, bf16[128,512]{1,0:T(8,128)(2,1)S(1)} %shard_map.55.kv_ref), custom_call_target="tpu_custom_call" | custom-call | flops 20000000000 | tf_op jit(solution)/shard_map/pallas_call | solution.py:112
  4.0 0.1 collective-permute-start
  4.1 4.1 %collective-permute-done.2.refs_1_ = bf16[128,512]{1,0:T(8,128)(2,1)S(1)} collective-permute-done((bf16[128,512]{1,0:T(8,128)(2,1)S(1)}, bf16[128,512]{1,0:T(8,128)(2,1)S(1)}, u32[]{:S(2)}, u32[]{:S(2)}) %collective-permute-start.2) | collective-permute-done | bytes 131104 | tf_op jit(solution)/shard_map/ppermute | solution.py:330
  8.2 0.0 collective-permute-done.1.refs_0_
  8.2 0.2 collective-permute-start.3
  8.4 0.8 %shard_map.58 = (f32[2,1,512]{2,1,0:T(1,128)S(1)}, f32[2,1,512]{2,1,0:T(1,128)S(1)}, f32[2,128,512]{2,1,0:T(8,128)S(1)}) custom-call(bf16[128,1024]{1,0:T(8,128)(2,1)S(1)} %copy-done, bf16[128,512]{1,0:T(8,128)(2,1)S(1)} %collective-permute-done.1.refs_0_, bf16[128,512]{1,0:T(8,128)(2,1)S(1)} %collective-permute-done.2.refs_1_, ...), custom_call_target="tpu_custom_call" | custom-call | flops 1000000000 | bytes 2000000 | tf_op jit(solution)/shard_map/pallas_call | solution.py:211
  9.3 0.0 collective-permute-done.refs_0_
  9.3 0.4 %collective-permute-done.3.refs_1_ = bf16[128,512]{1,0:T(8,128)(2,1)S(1)} collective-permute-done((bf16[128,512]{1,0:T(8,128)(2,1)S(1)}, bf16[128,512]{1,0:T(8,128)(2,1)S(1)}, u32[]{:S(2)}, u32[]{:S(2)}) %collective-permute-start.3) | collective-permute-done | bytes 131104 | tf_op jit(solution)/shard_map/ppermute | solution.py:336
  9.6 0.0 slice-done
  9.6 0.0 slice-done.1
  9.6 1.1 %shard_map.59 = (bf16[128,1024]{1,0:T(8,128)(2,1)S(1)}, bf16[128,512]{1,0:T(8,128)(2,1)S(1)}) custom-call(bf16[128,1024]{1,0:T(8,128)(2,1)S(1)} %copy-done, bf16[128,512]{1,0:T(8,128)(2,1)S(1)} %collective-permute-done.refs_0_, bf16[128,512]{1,0:T(8,128)(2,1)S(1)} %collective-permute-done.3.refs_1_, f32[1,512]{1,0:T(1,128)S(1)} %get-tuple-element.38.refs_2_, ...), custom_call_target="tpu_custom_call" | custom-call | flops 1000000000 | bytes 2000000 | tf_op jit(solution)/shard_map/pallas_call | solution.py:211
  10.8 1.6 %collective-permute-start.5 = (bf16[128,512]{1,0:T(8,128)(2,1)S(1)}, bf16[128,512]{1,0:T(8,128)(2,1)S(1)}, u32[]{:S(2)}, u32[]{:S(2)}) collective-permute-start(bf16[128,512]{1,0:T(8,128)(2,1)S(1)} %get-tuple-element.33), channel_id=1, source_target_pairs={{0,1},{1,0},{2,3},{3,2},{4,5},{5,4},{6,7},{7,6},{8,9},{9,8},{10,11... | collective-permute-start | bytes 393224 | tf_op jit(solution)/shard_map/ppermute | solution.py:35
  12.4 0.6 %shard_map.61 = (bf16[128,1024]{1,0:T(8,128)(2,1)S(1)}, bf16[128,512]{1,0:T(8,128)(2,1)S(1)}) custom-call(bf16[128,1024]{1,0:T(8,128)(2,1)S(1)} %get-tuple-element.28.a_ref, bf16[1024,4096]{1,0:T(8,128)(2,1)S(1)} %bitcast.9), custom_call_target="tpu_custom_call" | custom-call | flops 4000000000 | tf_op jit(solution)/shard_map/pallas_call | solution.py:238
  13.0 0.6 %collective-permute-start.6 = (bf16[128,512]{1,0:T(8,128)(2,1)S(1)}, bf16[128,512]{1,0:T(8,128)(2,1)S(1)}, u32[]{:S(2)}, u32[]{:S(2)}) collective-permute-start(bf16[128,512]{1,0:T(8,128)(2,1)S(1)} %get-tuple-element.34), channel_id=1, source_target_pairs={{0,1},{1,0},{2,3},{3,2},{4,5},{5,4},{6,7},{7,6},{8,9},{9,8},{10,11... | collective-permute-start | bytes 393224 | tf_op jit(solution)/shard_map/ppermute | solution.py:35
  13.5 1.5 %collective-permute-start.4 = (bf16[128,1024]{1,0:T(8,128)(2,1)S(1)}, bf16[128,1024]{1,0:T(8,128)(2,1)S(1)}, u32[]{:S(2)}, u32[]{:S(2)}) collective-permute-start(bf16[128,1024]{1,0:T(8,128)(2,1)S(1)} %get-tuple-element.30), channel_id=1, source_target_pairs={{0,1},{1,0},{2,3},{3,2},{4,5},{5,4},{6,7},{7,6},{8,9},{9,8},{10,11... | collective-permute-start | bytes 786440 | tf_op jit(solution)/shard_map/ppermute | solution.py:35
  15.1 0.7 %shard_map.60 = (bf16[128,512]{1,0:T(8,128)(2,1)S(1)}, bf16[128,1024]{1,0:T(8,128)(2,1)S(1)}, bf16[128,512]{1,0:T(8,128)(2,1)S(1)}) custom-call(bf16[128,1024]{1,0:T(8,128)(2,1)S(1)} %get-tuple-element.28.a_ref, bf16[1024,4096]{1,0:T(8,128)(2,1)S(1)} %bitcast.9), custom_call_target="tpu_custom_call" | custom-call | flops 4000000000 | tf_op jit(solution)/shard_map/pallas_call | solution.py:238
  15.8 1.4 %collective-permute-done.5.refs_2_ = bf16[128,512]{1,0:T(8,128)(2,1)S(1)} collective-permute-done((bf16[128,512]{1,0:T(8,128)(2,1)S(1)}, bf16[128,512]{1,0:T(8,128)(2,1)S(1)}, u32[]{:S(2)}, u32[]{:S(2)}) %collective-permute-start.5) | collective-permute-done | bytes 131104 | tf_op jit(solution)/shard_map/ppermute | solution.py:35
  17.2 2.8 %collective-permute-done.6.refs_3_ = bf16[128,512]{1,0:T(8,128)(2,1)S(1)} collective-permute-done((bf16[128,512]{1,0:T(8,128)(2,1)S(1)}, bf16[128,512]{1,0:T(8,128)(2,1)S(1)}, u32[]{:S(2)}, u32[]{:S(2)}) %collective-permute-start.6) | collective-permute-done | bytes 131104 | tf_op jit(solution)/shard_map/ppermute | solution.py:35
  20.0 0.7 %shard_map.62.refs_2_ = bf16[128,2048]{1,0:T(8,128)(2,1)} custom-call(bf16[128,512]{1,0:T(8,128)(2,1)S(1)} %get-tuple-element.31.refs_0_, bf16[128,512]{1,0:T(8,128)(2,1)S(1)} %get-tuple-element.32.refs_1_, bf16[128,512]{1,0:T(8,128)(2,1)S(1)} %collective-permute-done.5.refs_2_, bf16[128,512]{1,0:T(8,128)(2,1)S(1)} %collective-permute-done.6.refs_3_), custom_call_target="tpu_custom_call" | custom-call | flops 1000000 | bytes 1000000 | tf_op jit(solution)/shard_map/pallas_call | solution.py:274
  20.7 4.1 %collective-permute-done.4.refs_1_ = bf16[128,1024]{1,0:T(8,128)(2,1)S(1)} collective-permute-done((bf16[128,1024]{1,0:T(8,128)(2,1)S(1)}, bf16[128,1024]{1,0:T(8,128)(2,1)S(1)}, u32[]{:S(2)}, u32[]{:S(2)}) %collective-permute-start.4) | collective-permute-done | bytes 262176 | tf_op jit(solution)/shard_map/ppermute | solution.py:35
  24.8 0.8 %shard_map.63 = bf16[128,2048]{1,0:T(8,128)(2,1)} custom-call(bf16[128,1024]{1,0:T(8,128)(2,1)S(1)} %get-tuple-element.29.refs_0_, bf16[128,1024]{1,0:T(8,128)(2,1)S(1)} %collective-permute-done.4.refs_1_, bf16[128,2048]{1,0:T(8,128)(2,1)} %shard_map.62.refs_2_), custom_call_target="tpu_custom_call", output_to_operand_aliasing={{}: (2, {})} | custom-call | flops 1000000 | bytes 1000000 | tf_op jit(solution)/shard_map/pallas_call | solution.py:274
  (4 shorter events, 0.0 us)
Async XLA Ops:
  0.9 2.1 %copy-start = (bf16[128,1024]{1,0:T(8,128)(2,1)S(1)}, bf16[128,1024]{1,0:T(8,128)(2,1)}, u32[]{:S(2)}) copy-start(bf16[128,1024]{1,0:T(8,128)(2,1)} %q_ref.5) | copy-start | bytes 786436
  0.9 2.1 %copy-start.1 = (s32[16]{0:T(128)S(1)}, s32[16]{0:T(128)}, u32[]{:S(2)}) copy-start(s32[16]{0:T(128)} %docs_ref.1) | copy-start | bytes 196
  0.9 8.7 %slice-start = ((s8[8388608]{0:T(1024)(128)(4,1)}), s8[4194304]{0:T(1024)(128)(4,1)S(1)}, s32[]{:S(2)}) async-start(s8[8388608]{0:T(1024)(128)(4,1)} %bitcast.8), calls=%async_computation | async-start | bytes 8388608
  0.9 8.7 %slice-start.1 = ((s8[8388608]{0:T(1024)(128)(4,1)}), s8[4194304]{0:T(1024)(128)(4,1)S(1)}, s32[]{:S(2)}) async-start(s8[8388608]{0:T(1024)(128)(4,1)} %bitcast.8), calls=%async_computation.1 | async-start | bytes 8388608
  0.9 7.3 %collective-permute-start.2 = (bf16[128,512]{1,0:T(8,128)(2,1)S(1)}, bf16[128,512]{1,0:T(8,128)(2,1)S(1)}, u32[]{:S(2)}, u32[]{:S(2)}) collective-permute-start(bf16[128,512]{1,0:T(8,128)(2,1)S(1)} %shard_map.55.kv_ref), channel_id=1, source_target_pairs={{0,4},{2,6},{4,8},{6,0},{8,2},{10,16},{12,14},{14,18},{16,10},{18,... | collective-permute-start | bytes 393224 | tf_op jit(solution)/shard_map/ppermute | solution.py:330
  1.0 7.2 %collective-permute-start.1 = (bf16[128,512]{1,0:T(8,128)(2,1)S(1)}, bf16[128,512]{1,0:T(8,128)(2,1)S(1)}, u32[]{:S(2)}, u32[]{:S(2)}) collective-permute-start(bf16[128,512]{1,0:T(8,128)(2,1)S(1)} %shard_map.55.kv_ref), channel_id=1, source_target_pairs={{0,2},{2,0},{4,6},{6,10},{8,12},{10,14},{12,16},{14,4},{16,20},{18... | collective-permute-start | bytes 393224 | tf_op jit(solution)/shard_map/ppermute | solution.py:330
  4.0 5.2 %collective-permute-start = (bf16[128,512]{1,0:T(8,128)(2,1)S(1)}, bf16[128,512]{1,0:T(8,128)(2,1)S(1)}, u32[]{:S(2)}, u32[]{:S(2)}) collective-permute-start(bf16[128,512]{1,0:T(8,128)(2,1)S(1)} %get-tuple-element.20), channel_id=1, source_target_pairs={{0,2},{2,8},{4,6},{6,12},{8,10},{10,0},{12,4},{14,20},{16,18},{18,... | collective-permute-start | bytes 393224 | tf_op jit(solution)/shard_map/ppermute | solution.py:334
  8.2 1.4 %collective-permute-start.3 = (bf16[128,512]{1,0:T(8,128)(2,1)S(1)}, bf16[128,512]{1,0:T(8,128)(2,1)S(1)}, u32[]{:S(2)}, u32[]{:S(2)}) collective-permute-start(bf16[128,512]{1,0:T(8,128)(2,1)S(1)} %shard_map.57), channel_id=1, source_target_pairs={{0,2},{2,0},{4,6},{6,4},{8,10},{10,8},{12,14},{14,12},{16,18},{18,... | collective-permute-start | bytes 393224 | tf_op jit(solution)/shard_map/ppermute | solution.py:336
  10.8 6.4 %collective-permute-start.5 = (bf16[128,512]{1,0:T(8,128)(2,1)S(1)}, bf16[128,512]{1,0:T(8,128)(2,1)S(1)}, u32[]{:S(2)}, u32[]{:S(2)}) collective-permute-start(bf16[128,512]{1,0:T(8,128)(2,1)S(1)} %get-tuple-element.33), channel_id=1, source_target_pairs={{0,1},{1,0},{2,3},{3,2},{4,5},{5,4},{6,7},{7,6},{8,9},{9,8},{10,11... | collective-permute-start | bytes 393224 | tf_op jit(solution)/shard_map/ppermute | solution.py:35
  13.0 7.0 %collective-permute-start.6 = (bf16[128,512]{1,0:T(8,128)(2,1)S(1)}, bf16[128,512]{1,0:T(8,128)(2,1)S(1)}, u32[]{:S(2)}, u32[]{:S(2)}) collective-permute-start(bf16[128,512]{1,0:T(8,128)(2,1)S(1)} %get-tuple-element.34), channel_id=1, source_target_pairs={{0,1},{1,0},{2,3},{3,2},{4,5},{5,4},{6,7},{7,6},{8,9},{9,8},{10,11... | collective-permute-start | bytes 393224 | tf_op jit(solution)/shard_map/ppermute | solution.py:35
  13.5 11.3 %collective-permute-start.4 = (bf16[128,1024]{1,0:T(8,128)(2,1)S(1)}, bf16[128,1024]{1,0:T(8,128)(2,1)S(1)}, u32[]{:S(2)}, u32[]{:S(2)}) collective-permute-start(bf16[128,1024]{1,0:T(8,128)(2,1)S(1)} %get-tuple-element.30), channel_id=1, source_target_pairs={{0,1},{1,0},{2,3},{3,2},{4,5},{5,4},{6,7},{7,6},{8,9},{9,8},{10,11... | collective-permute-start | bytes 786440 | tf_op jit(solution)/shard_map/ppermute | solution.py:35

commit v6 on v4

--- a/solution.py
+++ b/solution.py
@@ -327,11 +327,12 @@
     kv = hold(side_by_side(key_states, value_states))
     if reach == 3 and count == len(RINGS[0]):
         packed, carrier = ring_table()
+        first_kv = kv
         arrived = [lax.ppermute(kv, "seq", list(enumerate(ring))) for ring in RINGS[1:]]
         gaps = [functools.partial(pick, word) for word in packed]
         gaps.append(lambda position: 1 + 2 * (position & 1))
         state, bias, kv = opening(block_docs, query_states, kv, out_weight, gaps, *sizes)
-        arrived = [lax.ppermute(kv, "seq", list(enumerate(RINGS[0])))] + arrived
+        arrived = [lax.ppermute(first_kv, "seq", list(enumerate(RINGS[0])))] + arrived
         second = choose(carrier, arrived[1:], state[0])
         late = lax.ppermute(second, "seq", [(i, i ^ 1) for i in range(count)])
         biases = [bias[at] for at in range(len(gaps))]

time: 25.7 us -> 25.7 us (level)
  Pallas kernels: 5.84 us -> 6.4 us
  waiting for transfers between devices: 12.2 us -> 11.7 us
    pallas_call x1, Pallas kernels: 1.05 us -> 1.61 us  [opening(): pl.pallas_call(functools.partial(opening_kernel, gaps, kv_local, group_si...]
    ppermute x2, waiting for transfers between devices: 4.13 us -> 3.64 us  [local(): lax.ppermute(kv, 'seq', list(enumerate(ring)))]
  transfers between devices with their start and end apart: 8 -> 8, of which waited for: 6 -> 6; matrix products, arithmetic and copies ran while one was open for 0% -> 0% of each run, Pallas kernels for 16% -> 18%
where the time goes in v6:
time: 25.7 us; the launch traced here: 25.5 us
  waiting for transfers between devices  11.7 us (46%)
  Pallas kernels  6.4 us (25%)
  starting transfers between devices  6.35 us (25%)
  other arithmetic  0.88 us (3%)
    ppermute x4, waiting for transfers between devices, turned(): lax.ppermute(value, axis, [(source, (source + steps) % count) for source...  7.7 us
    ppermute x4, starting transfers between devices, turned(): lax.ppermute(value, axis, [(source, (source + steps) % count) for source...  4.18 us
    ppermute x2, waiting for transfers between devices, local(): lax.ppermute(kv, 'seq', list(enumerate(ring)))  3.64 us
    ppermute x2, starting transfers between devices, local(): lax.ppermute(kv, 'seq', list(enumerate(ring)))  1.99 us
    pallas_call x2, Pallas kernels, attend(): pl.pallas_call(functools.partial(attend_kernel, blocks, len(biases) < blo...  1.95 us
    pallas_call x1, Pallas kernels, opening(): pl.pallas_call(functools.partial(opening_kernel, gaps, kv_local, group_si...  1.61 us
    pallas_call x2, Pallas kernels, close(): pl.pallas_call(functools.partial(close_kernel, [parts[at] for at in chose...  1.49 us
    pallas_call x2, Pallas kernels, project(): pl.pallas_call(functools.partial(project_kernel, step, parts), out_shape=...  1.33 us
  transfers between devices with their start and end apart: 8, of which 6 were waited for; matrix products, arithmetic and copies ran while one was open for 0% of the time, Pallas kernels for 18%

profile of v6, /device:TPU:24, one launch (start us, length us, event | category | flops | bytes accessed | tf_op | source)
XLA Modules:
  0.0 25.5 jit_solution(16446114627679916638)
XLA Ops:
  0.0 0.9 %pad_maximum_fusion.kv_in = bf16[128,512]{1,0:T(8,128)(2,1)S(1)} fusion(bf16[128,256]{1,0:T(8,128)(2,1)} %param.7, bf16[128,256]{1,0:T(8,128)(2,1)} %param.6), kind=kLoop, calls=%fused_computation | loop fusion | flops 262144 | bytes 262144 | tf_op jit(solution)/shard_map/max | solution.py:311
  0.9 0.0 copy-start
  0.9 0.0 copy-start.1
  0.9 0.0 slice-start
  0.9 0.0 slice-start.1
  0.9 0.1 collective-permute-start.2
  1.0 1.9 %collective-permute-start.1 = (bf16[128,512]{1,0:T(8,128)(2,1)S(1)}, bf16[128,512]{1,0:T(8,128)(2,1)S(1)}, u32[]{:S(2)}, u32[]{:S(2)}) collective-permute-start(bf16[128,512]{1,0:T(8,128)(2,1)S(1)} %shard_map.55.kv_ref), channel_id=1, source_target_pairs={{0,2},{2,0},{4,6},{6,10},{8,12},{10,14},{12,16},{14,4},{16,20},{18... | collective-permute-start | bytes 393224 | tf_op jit(solution)/shard_map/ppermute | solution.py:331
  2.9 0.0 collective-permute-start
  2.9 0.0 copy-done
  3.0 0.0 copy-done.1
  3.0 1.6 %shard_map.56 = (f32[2,1,512]{2,1,0:T(1,128)S(1)}, f32[2,1,512]{2,1,0:T(1,128)S(1)}, f32[2,128,512]{2,1,0:T(8,128)S(1)}, f32[4,1,512]{2,1,0:T(1,128)S(1)}, bf16[128,512]{1,0:T(8,128)(2,1)}) custom-call(s32[16]{0:T(128)S(1)} %copy-done.1, bf16[128,1024]{1,0:T(8,128)(2,1)S(1)} %copy-done, bf16[128,512]{1,0:T(8,128)(2,1)S(1)} %shard_map.55.kv_ref), custom_call_target="tpu_custom_call" | custom-call | flops 20000000000 | tf_op jit(solution)/shard_map/pallas_call | solution.py:112
  4.6 3.6 %collective-permute-done.2.refs_1_ = bf16[128,512]{1,0:T(8,128)(2,1)S(1)} collective-permute-done((bf16[128,512]{1,0:T(8,128)(2,1)S(1)}, bf16[128,512]{1,0:T(8,128)(2,1)S(1)}, u32[]{:S(2)}, u32[]{:S(2)}) %collective-permute-start.2) | collective-permute-done | bytes 131104 | tf_op jit(solution)/shard_map/ppermute | solution.py:331
  8.2 0.0 collective-permute-done.1.refs_0_
  8.2 0.2 collective-permute-start.3
  8.4 0.8 %shard_map.58 = (f32[2,1,512]{2,1,0:T(1,128)S(1)}, f32[2,1,512]{2,1,0:T(1,128)S(1)}, f32[2,128,512]{2,1,0:T(8,128)S(1)}) custom-call(bf16[128,1024]{1,0:T(8,128)(2,1)S(1)} %copy-done, bf16[128,512]{1,0:T(8,128)(2,1)S(1)} %collective-permute-done.1.refs_0_, bf16[128,512]{1,0:T(8,128)(2,1)S(1)} %collective-permute-done.2.refs_1_, ...), custom_call_target="tpu_custom_call" | custom-call | flops 1000000000 | bytes 2000000 | tf_op jit(solution)/shard_map/pallas_call | solution.py:211
  9.3 0.0 collective-permute-done.refs_0_
  9.3 0.4 %collective-permute-done.3.refs_1_ = bf16[128,512]{1,0:T(8,128)(2,1)S(1)} collective-permute-done((bf16[128,512]{1,0:T(8,128)(2,1)S(1)}, bf16[128,512]{1,0:T(8,128)(2,1)S(1)}, u32[]{:S(2)}, u32[]{:S(2)}) %collective-permute-start.3) | collective-permute-done | bytes 131104 | tf_op jit(solution)/shard_map/ppermute | solution.py:337
  9.6 0.0 slice-done
  9.6 0.0 slice-done.1
  9.6 1.1 %shard_map.59 = (bf16[128,1024]{1,0:T(8,128)(2,1)S(1)}, bf16[128,512]{1,0:T(8,128)(2,1)S(1)}) custom-call(bf16[128,1024]{1,0:T(8,128)(2,1)S(1)} %copy-done, bf16[128,512]{1,0:T(8,128)(2,1)S(1)} %collective-permute-done.refs_0_, bf16[128,512]{1,0:T(8,128)(2,1)S(1)} %collective-permute-done.3.refs_1_, f32[1,512]{1,0:T(1,128)S(1)} %get-tuple-element.40.refs_2_, ...), custom_call_target="tpu_custom_call" | custom-call | flops 1000000000 | bytes 2000000 | tf_op jit(solution)/shard_map/pallas_call | solution.py:211
  10.8 1.6 %collective-permute-start.7 = (bf16[128,512]{1,0:T(8,128)(2,1)S(1)}, bf16[128,512]{1,0:T(8,128)(2,1)S(1)}, u32[]{:S(2)}, u32[]{:S(2)}) collective-permute-start(bf16[128,512]{1,0:T(8,128)(2,1)S(1)} %get-tuple-element.36), channel_id=1, source_target_pairs={{0,1},{1,0},{2,3},{3,2},{4,5},{5,4},{6,7},{7,6},{8,9},{9,8},{10,11... | collective-permute-start | bytes 393224 | tf_op jit(solution)/shard_map/ppermute | solution.py:35
  12.3 0.6 %shard_map.61 = (bf16[128,512]{1,0:T(8,128)(2,1)S(1)}, bf16[128,512]{1,0:T(8,128)(2,1)S(1)}, bf16[128,512]{1,0:T(8,128)(2,1)S(1)}) custom-call(bf16[128,1024]{1,0:T(8,128)(2,1)S(1)} %get-tuple-element.28.a_ref, bf16[1024,4096]{1,0:T(8,128)(2,1)S(1)} %bitcast.9), custom_call_target="tpu_custom_call" | custom-call | flops 402653184 | bytes 1000000 | tf_op jit(solution)/shard_map/pallas_call | solution.py:238
  13.0 0.6 %collective-permute-start.5 = (bf16[128,512]{1,0:T(8,128)(2,1)S(1)}, bf16[128,512]{1,0:T(8,128)(2,1)S(1)}, u32[]{:S(2)}, u32[]{:S(2)}) collective-permute-start(bf16[128,512]{1,0:T(8,128)(2,1)S(1)} %get-tuple-element.34), channel_id=1, source_target_pairs={{0,1},{1,0},{2,3},{3,2},{4,5},{5,4},{6,7},{7,6},{8,9},{9,8},{10,11... | collective-permute-start | bytes 393224 | tf_op jit(solution)/shard_map/ppermute | solution.py:35
  13.5 1.5 %collective-permute-start.6 = (bf16[128,512]{1,0:T(8,128)(2,1)S(1)}, bf16[128,512]{1,0:T(8,128)(2,1)S(1)}, u32[]{:S(2)}, u32[]{:S(2)}) collective-permute-start(bf16[128,512]{1,0:T(8,128)(2,1)S(1)} %get-tuple-element.35), channel_id=1, source_target_pairs={{0,1},{1,0},{2,3},{3,2},{4,5},{5,4},{6,7},{7,6},{8,9},{9,8},{10,11... | collective-permute-start | bytes 393224 | tf_op jit(solution)/shard_map/ppermute | solution.py:35
  15.0 0.5 %collective-permute-start.4 = (bf16[128,512]{1,0:T(8,128)(2,1)S(1)}, bf16[128,512]{1,0:T(8,128)(2,1)S(1)}, u32[]{:S(2)}, u32[]{:S(2)}) collective-permute-start(bf16[128,512]{1,0:T(8,128)(2,1)S(1)} %get-tuple-element.30), channel_id=1, source_target_pairs={{0,1},{1,0},{2,3},{3,2},{4,5},{5,4},{6,7},{7,6},{8,9},{9,8},{10,11... | collective-permute-start | bytes 393224 | tf_op jit(solution)/shard_map/ppermute | solution.py:35
  15.6 0.7 %shard_map.60 = (bf16[128,512]{1,0:T(8,128)(2,1)S(1)}, bf16[128,512]{1,0:T(8,128)(2,1)S(1)}, bf16[128,512]{1,0:T(8,128)(2,1)S(1)}, bf16[128,512]{1,0:T(8,128)(2,1)S(1)}) custom-call(bf16[128,1024]{1,0:T(8,128)(2,1)S(1)} %get-tuple-element.28.a_ref, bf16[1024,4096]{1,0:T(8,128)(2,1)S(1)} %bitcast.9), custom_call_target="tpu_custom_call" | custom-call | flops 536870912 | bytes 1000000 | tf_op jit(solution)/shard_map/pallas_call | solution.py:238
  16.3 0.9 %collective-permute-done.7.refs_5_ = bf16[128,512]{1,0:T(8,128)(2,1)S(1)} collective-permute-done((bf16[128,512]{1,0:T(8,128)(2,1)S(1)}, bf16[128,512]{1,0:T(8,128)(2,1)S(1)}, u32[]{:S(2)}, u32[]{:S(2)}) %collective-permute-start.7) | collective-permute-done | bytes 131104 | tf_op jit(solution)/shard_map/ppermute | solution.py:35
  17.2 2.8 %collective-permute-done.5.refs_3_ = bf16[128,512]{1,0:T(8,128)(2,1)S(1)} collective-permute-done((bf16[128,512]{1,0:T(8,128)(2,1)S(1)}, bf16[128,512]{1,0:T(8,128)(2,1)S(1)}, u32[]{:S(2)}, u32[]{:S(2)}) %collective-permute-start.5) | collective-permute-done | bytes 131104 | tf_op jit(solution)/shard_map/ppermute | solution.py:35
  20.0 2.8 %collective-permute-done.6.refs_4_ = bf16[128,512]{1,0:T(8,128)(2,1)S(1)} collective-permute-done((bf16[128,512]{1,0:T(8,128)(2,1)S(1)}, bf16[128,512]{1,0:T(8,128)(2,1)S(1)}, u32[]{:S(2)}, u32[]{:S(2)}) %collective-permute-start.6) | collective-permute-done | bytes 131104 | tf_op jit(solution)/shard_map/ppermute | solution.py:35
  22.8 0.8 %shard_map.62.refs_2_ = bf16[128,2048]{1,0:T(8,128)(2,1)} custom-call(bf16[128,512]{1,0:T(8,128)(2,1)S(1)} %get-tuple-element.31.refs_0_, bf16[128,512]{1,0:T(8,128)(2,1)S(1)} %get-tuple-element.32.refs_1_, bf16[128,512]{1,0:T(8,128)(2,1)S(1)} %get-tuple-element.33.refs_2_, bf16[128,512]{1,0:T(8,128)(2,1)S(1)} %collective-permute-done.5.refs_3_, ...), custom_call_target="tpu_custom_call" | custom-call | flops 1000000 | bytes 1000000 | tf_op jit(solution)/shard_map/pallas_call | solution.py:274
  23.6 1.2 %collective-permute-done.4.refs_1_ = bf16[128,512]{1,0:T(8,128)(2,1)S(1)} collective-permute-done((bf16[128,512]{1,0:T(8,128)(2,1)S(1)}, bf16[128,512]{1,0:T(8,128)(2,1)S(1)}, u32[]{:S(2)}, u32[]{:S(2)}) %collective-permute-start.4) | collective-permute-done | bytes 131104 | tf_op jit(solution)/shard_map/ppermute | solution.py:35
  24.8 0.7 %shard_map.63 = bf16[128,2048]{1,0:T(8,128)(2,1)} custom-call(bf16[128,512]{1,0:T(8,128)(2,1)S(1)} %get-tuple-element.29.refs_0_, bf16[128,512]{1,0:T(8,128)(2,1)S(1)} %collective-permute-done.4.refs_1_, bf16[128,2048]{1,0:T(8,128)(2,1)} %shard_map.62.refs_2_), custom_call_target="tpu_custom_call", output_to_operand_aliasing={{}: (2, {})} | custom-call | flops 1000000 | bytes 1000000 | tf_op jit(solution)/shard_map/pallas_call | solution.py:274
  (4 shorter events, 0.0 us)
Async XLA Ops:
  0.9 2.1 %copy-start = (bf16[128,1024]{1,0:T(8,128)(2,1)S(1)}, bf16[128,1024]{1,0:T(8,128)(2,1)}, u32[]{:S(2)}) copy-start(bf16[128,1024]{1,0:T(8,128)(2,1)} %q_ref.5) | copy-start | bytes 786436
  0.9 2.1 %copy-start.1 = (s32[16]{0:T(128)S(1)}, s32[16]{0:T(128)}, u32[]{:S(2)}) copy-start(s32[16]{0:T(128)} %docs_ref.1) | copy-start | bytes 196
  0.9 8.7 %slice-start = ((s8[8388608]{0:T(1024)(128)(4,1)}), s8[4194304]{0:T(1024)(128)(4,1)S(1)}, s32[]{:S(2)}) async-start(s8[8388608]{0:T(1024)(128)(4,1)} %bitcast.8), calls=%async_computation | async-start | bytes 8388608
  0.9 8.7 %slice-start.1 = ((s8[8388608]{0:T(1024)(128)(4,1)}), s8[4194304]{0:T(1024)(128)(4,1)S(1)}, s32[]{:S(2)}) async-start(s8[8388608]{0:T(1024)(128)(4,1)} %bitcast.8), calls=%async_computation.1 | async-start | bytes 8388608
  0.9 7.3 %collective-permute-start.2 = (bf16[128,512]{1,0:T(8,128)(2,1)S(1)}, bf16[128,512]{1,0:T(8,128)(2,1)S(1)}, u32[]{:S(2)}, u32[]{:S(2)}) collective-permute-start(bf16[128,512]{1,0:T(8,128)(2,1)S(1)} %shard_map.55.kv_ref), channel_id=1, source_target_pairs={{0,4},{2,6},{4,8},{6,0},{8,2},{10,16},{12,14},{14,18},{16,10},{18,... | collective-permute-start | bytes 393224 | tf_op jit(solution)/shard_map/ppermute | solution.py:331
  1.0 7.2 %collective-permute-start.1 = (bf16[128,512]{1,0:T(8,128)(2,1)S(1)}, bf16[128,512]{1,0:T(8,128)(2,1)S(1)}, u32[]{:S(2)}, u32[]{:S(2)}) collective-permute-start(bf16[128,512]{1,0:T(8,128)(2,1)S(1)} %shard_map.55.kv_ref), channel_id=1, source_target_pairs={{0,2},{2,0},{4,6},{6,10},{8,12},{10,14},{12,16},{14,4},{16,20},{18... | collective-permute-start | bytes 393224 | tf_op jit(solution)/shard_map/ppermute | solution.py:331
  2.9 6.3 %collective-permute-start = (bf16[128,512]{1,0:T(8,128)(2,1)S(1)}, bf16[128,512]{1,0:T(8,128)(2,1)S(1)}, u32[]{:S(2)}, u32[]{:S(2)}) collective-permute-start(bf16[128,512]{1,0:T(8,128)(2,1)S(1)} %shard_map.55.kv_ref), channel_id=1, source_target_pairs={{0,2},{2,8},{4,6},{6,12},{8,10},{10,0},{12,4},{14,20},{16,18},{18,... | collective-permute-start | bytes 393224 | tf_op jit(solution)/shard_map/ppermute | solution.py:335
  8.2 1.4 %collective-permute-start.3 = (bf16[128,512]{1,0:T(8,128)(2,1)S(1)}, bf16[128,512]{1,0:T(8,128)(2,1)S(1)}, u32[]{:S(2)}, u32[]{:S(2)}) collective-permute-start(bf16[128,512]{1,0:T(8,128)(2,1)S(1)} %shard_map.57), channel_id=1, source_target_pairs={{0,2},{2,0},{4,6},{6,4},{8,10},{10,8},{12,14},{14,12},{16,18},{18,... | collective-permute-start | bytes 393224 | tf_op jit(solution)/shard_map/ppermute | solution.py:337
  10.8 6.4 %collective-permute-start.7 = (bf16[128,512]{1,0:T(8,128)(2,1)S(1)}, bf16[128,512]{1,0:T(8,128)(2,1)S(1)}, u32[]{:S(2)}, u32[]{:S(2)}) collective-permute-start(bf16[128,512]{1,0:T(8,128)(2,1)S(1)} %get-tuple-element.36), channel_id=1, source_target_pairs={{0,1},{1,0},{2,3},{3,2},{4,5},{5,4},{6,7},{7,6},{8,9},{9,8},{10,11... | collective-permute-start | bytes 393224 | tf_op jit(solution)/shard_map/ppermute | solution.py:35
  13.0 7.0 %collective-permute-start.5 = (bf16[128,512]{1,0:T(8,128)(2,1)S(1)}, bf16[128,512]{1,0:T(8,128)(2,1)S(1)}, u32[]{:S(2)}, u32[]{:S(2)}) collective-permute-start(bf16[128,512]{1,0:T(8,128)(2,1)S(1)} %get-tuple-element.34), channel_id=1, source_target_pairs={{0,1},{1,0},{2,3},{3,2},{4,5},{5,4},{6,7},{7,6},{8,9},{9,8},{10,11... | collective-permute-start | bytes 393224 | tf_op jit(solution)/shard_map/ppermute | solution.py:35
  13.5 9.3 %collective-permute-start.6 = (bf16[128,512]{1,0:T(8,128)(2,1)S(1)}, bf16[128,512]{1,0:T(8,128)(2,1)S(1)}, u32[]{:S(2)}, u32[]{:S(2)}) collective-permute-start(bf16[128,512]{1,0:T(8,128)(2,1)S(1)} %get-tuple-element.35), channel_id=1, source_target_pairs={{0,1},{1,0},{2,3},{3,2},{4,5},{5,4},{6,7},{7,6},{8,9},{9,8},{10,11... | collective-permute-start | bytes 393224 | tf_op jit(solution)/shard_map/ppermute | solution.py:35
  15.0 9.8 %collective-permute-start.4 = (bf16[128,512]{1,0:T(8,128)(2,1)S(1)}, bf16[128,512]{1,0:T(8,128)(2,1)S(1)}, u32[]{:S(2)}, u32[]{:S(2)}) collective-permute-start(bf16[128,512]{1,0:T(8,128)(2,1)S(1)} %get-tuple-element.30), channel_id=1, source_target_pairs={{0,1},{1,0},{2,3},{3,2},{4,5},{5,4},{6,7},{7,6},{8,9},{9,8},{10,11... | collective-permute-start | bytes 393224 | tf_op jit(solution)/shard_map/ppermute | solution.py:35

commit v7 on v6

--- a/solution.py
+++ b/solution.py
@@ -102,7 +102,7 @@
         source = jnp.maximum(position - gap, 0)
         near = (docs_ref[source] == doc) & (position >= gap) & (gap > 0)
         bias_ref[at] = jnp.full(bias_ref.shape[1:], jnp.where(near, 0.0, FAR), jnp.float32)
-    attend_kernel(1, True, kv_local, group_size, False, False, q_ref, kv_ref, *state_refs)
+    attend_kernel(1, True, (), kv_local, group_size, False, False, q_ref, kv_ref, bias_ref, *state_refs)
 
 
 def opening(docs, queries, kv, weights, gaps, kv_local, group_size):
@@ -124,10 +124,11 @@
     return range(kv_head * group_size, (kv_head + 1) * group_size)
 
 
-def attend_kernel(blocks, own, kv_local, group_size, resume, finish, q_ref, *refs):
+def attend_kernel(blocks, own, rows_of_bias, kv_local, group_size, resume, finish, q_ref, *refs):
     refs = list(refs)
     kv_refs = [refs.pop(0) for _ in range(blocks)]
-    bias_refs = [refs.pop(0) for _ in range(blocks - own)]
+    bias_ref = refs.pop(0)
+    bias_refs = [bias_ref.at[at] for at in rows_of_bias]
     state_in = [refs.pop(0) for _ in range(3)] if resume else None
     w_ref = refs.pop(0) if finish else None
     width = kv_local * HD
@@ -200,17 +201,17 @@
     return pl.multiple_of(target * (columns // groups), 128)
 
 
-def attend(queries, kv_blocks, biases, kv_local, group_size, state, weights=None, part=None):
+def attend(queries, kv_blocks, bias, rows_of_bias, kv_local, group_size, state, weights=None, part=None):
     rows = group_size * BLK
     if part:
         out_shape = [jax.ShapeDtypeStruct(queries.shape, jnp.bfloat16), part_shape(part)]
     else:
         out_shape = [jax.ShapeDtypeStruct((kv_local, n, rows), jnp.float32) for n in (1, 1, HD)]
-    operands = [queries, *kv_blocks, *biases, *state] + ([weights] if part else [])
+    operands = [queries, *kv_blocks, bias, *state] + ([weights] if part else [])
     blocks = len(kv_blocks)
     return pl.pallas_call(
         functools.partial(
-            attend_kernel, blocks, len(biases) < blocks, kv_local, group_size, bool(state), part
+            attend_kernel, blocks, len(rows_of_bias) < blocks, rows_of_bias, kv_local, group_size, bool(state), part
         ),
         out_shape=out_shape,
         in_specs=[VMEM] * len(operands),
@@ -335,10 +336,9 @@
         arrived = [lax.ppermute(first_kv, "seq", list(enumerate(RINGS[0])))] + arrived
         second = choose(carrier, arrived[1:], state[0])
         late = lax.ppermute(second, "seq", [(i, i ^ 1) for i in range(count)])
-        biases = [bias[at] for at in range(len(gaps))]
-        state = attend(query_states, arrived[1:], biases[1:3], *sizes, state)
+        state = attend(query_states, arrived[1:], bias, (1, 2), *sizes, state)
         attended, last = attend(
-            query_states, [arrived[0], late], [biases[0], biases[3]], *sizes, state, out_weight, parts[-1]
+            query_states, [arrived[0], late], bias, (0, 3), *sizes, state, out_weight, parts[-1]
         )
     else:
         blocks = [kv]
@@ -348,8 +348,7 @@
             passed = turned(jnp.stack(blocks[:send]), "seq", have)
             blocks = blocks + [passed[i] for i in range(send)]
         bias = mask(block_docs, reach, group_size * BLK)
-        biases = [bias[at] for at in range(reach)]
-        attended, last = attend(query_states, blocks, biases, *sizes, (), out_weight, parts[-1])
+        attended, last = attend(query_states, blocks, bias, tuple(range(reach)), *sizes, (), out_weight, parts[-1])
 
     received = []
     for step in range(1, groups):

time: 25.7 us -> 25.7 us (level)
  no operation moved by 1% of the time
where the time goes in v7:
time: 25.7 us; the launch traced here: 25.5 us
  waiting for transfers between devices  11.7 us (46%)
  Pallas kernels  6.4 us (25%)
  starting transfers between devices  6.35 us (25%)
  other arithmetic  0.88 us (3%)
    ppermute x4, waiting for transfers between devices, turned(): lax.ppermute(value, axis, [(source, (source + steps) % count) for source...  7.7 us
    ppermute x4, starting transfers between devices, turned(): lax.ppermute(value, axis, [(source, (source + steps) % count) for source...  4.18 us
    ppermute x2, waiting for transfers between devices, local(): lax.ppermute(kv, 'seq', list(enumerate(ring)))  3.64 us
    ppermute x2, starting transfers between devices, local(): lax.ppermute(kv, 'seq', list(enumerate(ring)))  1.99 us
    pallas_call x2, Pallas kernels, attend(): pl.pallas_call(functools.partial(attend_kernel, blocks, len(rows_of_bias)...  1.96 us
    pallas_call x1, Pallas kernels, opening(): pl.pallas_call(functools.partial(opening_kernel, gaps, kv_local, group_si...  1.61 us
    pallas_call x2, Pallas kernels, close(): pl.pallas_call(functools.partial(close_kernel, [parts[at] for at in chose...  1.49 us
    pallas_call x2, Pallas kernels, project(): pl.pallas_call(functools.partial(project_kernel, step, parts), out_shape=...  1.33 us
  transfers between devices with their start and end apart: 8, of which 6 were waited for; matrix products, arithmetic and copies ran while one was open for 0% of the time, Pallas kernels for 18%

profile of v7, /device:TPU:24, one launch (start us, length us, event | category | flops | bytes accessed | tf_op | source)
XLA Modules:
  0.0 25.5 jit_solution(13304356682885239134)
XLA Ops:
  0.0 0.9 %pad_maximum_fusion.kv_in = bf16[128,512]{1,0:T(8,128)(2,1)S(1)} fusion(bf16[128,256]{1,0:T(8,128)(2,1)} %param.7, bf16[128,256]{1,0:T(8,128)(2,1)} %param.6), kind=kLoop, calls=%fused_computation | loop fusion | flops 262144 | bytes 262144 | tf_op jit(solution)/shard_map/max | solution.py:312
  0.9 0.0 copy-start
  0.9 0.0 copy-start.1
  0.9 0.0 slice-start
  0.9 0.0 slice-start.1
  0.9 0.1 collective-permute-start.2
  1.0 1.9 %collective-permute-start.1 = (bf16[128,512]{1,0:T(8,128)(2,1)S(1)}, bf16[128,512]{1,0:T(8,128)(2,1)S(1)}, u32[]{:S(2)}, u32[]{:S(2)}) collective-permute-start(bf16[128,512]{1,0:T(8,128)(2,1)S(1)} %shard_map.55.kv_ref), channel_id=1, source_target_pairs={{0,2},{2,0},{4,6},{6,10},{8,12},{10,14},{12,16},{14,4},{16,20},{18... | collective-permute-start | bytes 393224 | tf_op jit(solution)/shard_map/ppermute | solution.py:332
  2.9 0.0 collective-permute-start
  2.9 0.0 copy-done
  3.0 0.0 copy-done.1
  3.0 1.6 %shard_map.56 = (f32[2,1,512]{2,1,0:T(1,128)S(1)}, f32[2,1,512]{2,1,0:T(1,128)S(1)}, f32[2,128,512]{2,1,0:T(8,128)S(1)}, f32[4,1,512]{2,1,0:T(1,128)S(1)}, bf16[128,512]{1,0:T(8,128)(2,1)}) custom-call(s32[16]{0:T(128)S(1)} %copy-done.1, bf16[128,1024]{1,0:T(8,128)(2,1)S(1)} %copy-done, bf16[128,512]{1,0:T(8,128)(2,1)S(1)} %shard_map.55.kv_ref), custom_call_target="tpu_custom_call" | custom-call | flops 20000000000 | tf_op jit(solution)/shard_map/pallas_call | solution.py:112
  4.6 3.6 %collective-permute-done.2.refs_1_ = bf16[128,512]{1,0:T(8,128)(2,1)S(1)} collective-permute-done((bf16[128,512]{1,0:T(8,128)(2,1)S(1)}, bf16[128,512]{1,0:T(8,128)(2,1)S(1)}, u32[]{:S(2)}, u32[]{:S(2)}) %collective-permute-start.2) | collective-permute-done | bytes 131104 | tf_op jit(solution)/shard_map/ppermute | solution.py:332
  8.2 0.0 collective-permute-done.1.refs_0_
  8.2 0.2 collective-permute-start.3
  8.4 0.8 %shard_map.58 = (f32[2,1,512]{2,1,0:T(1,128)S(1)}, f32[2,1,512]{2,1,0:T(1,128)S(1)}, f32[2,128,512]{2,1,0:T(8,128)S(1)}) custom-call(bf16[128,1024]{1,0:T(8,128)(2,1)S(1)} %copy-done, bf16[128,512]{1,0:T(8,128)(2,1)S(1)} %collective-permute-done.1.refs_0_, bf16[128,512]{1,0:T(8,128)(2,1)S(1)} %collective-permute-done.2.refs_1_, ...), custom_call_target="tpu_custom_call" | custom-call | flops 1000000000 | bytes 2000000 | tf_op jit(solution)/shard_map/pallas_call | solution.py:212
  9.3 0.0 collective-permute-done.refs_0_
  9.3 0.4 %collective-permute-done.3.refs_1_ = bf16[128,512]{1,0:T(8,128)(2,1)S(1)} collective-permute-done((bf16[128,512]{1,0:T(8,128)(2,1)S(1)}, bf16[128,512]{1,0:T(8,128)(2,1)S(1)}, u32[]{:S(2)}, u32[]{:S(2)}) %collective-permute-start.3) | collective-permute-done | bytes 131104 | tf_op jit(solution)/shard_map/ppermute | solution.py:338
  9.6 0.0 slice-done
  9.6 0.0 slice-done.1
  9.6 1.1 %shard_map.59 = (bf16[128,1024]{1,0:T(8,128)(2,1)S(1)}, bf16[128,512]{1,0:T(8,128)(2,1)S(1)}) custom-call(bf16[128,1024]{1,0:T(8,128)(2,1)S(1)} %copy-done, bf16[128,512]{1,0:T(8,128)(2,1)S(1)} %collective-permute-done.refs_0_, bf16[128,512]{1,0:T(8,128)(2,1)S(1)} %collective-permute-done.3.refs_1_, f32[4,1,512]{2,1,0:T(1,128)S(1)} %get-tuple-element.22.refs_2_, ...), custom_call_target="tpu_custom_call" | custom-call | flops 1000000000 | bytes 2000000 | tf_op jit(solution)/shard_map/pallas_call | solution.py:212
  10.8 1.6 %collective-permute-start.7 = (bf16[128,512]{1,0:T(8,128)(2,1)S(1)}, bf16[128,512]{1,0:T(8,128)(2,1)S(1)}, u32[]{:S(2)}, u32[]{:S(2)}) collective-permute-start(bf16[128,512]{1,0:T(8,128)(2,1)S(1)} %get-tuple-element.36), channel_id=1, source_target_pairs={{0,1},{1,0},{2,3},{3,2},{4,5},{5,4},{6,7},{7,6},{8,9},{9,8},{10,11... | collective-permute-start | bytes 393224 | tf_op jit(solution)/shard_map/ppermute | solution.py:35
  12.3 0.6 %shard_map.61 = (bf16[128,512]{1,0:T(8,128)(2,1)S(1)}, bf16[128,512]{1,0:T(8,128)(2,1)S(1)}, bf16[128,512]{1,0:T(8,128)(2,1)S(1)}) custom-call(bf16[128,1024]{1,0:T(8,128)(2,1)S(1)} %get-tuple-element.28.a_ref, bf16[1024,4096]{1,0:T(8,128)(2,1)S(1)} %bitcast.1), custom_call_target="tpu_custom_call" | custom-call | flops 402653184 | bytes 1000000 | tf_op jit(solution)/shard_map/pallas_call | solution.py:239
  13.0 0.6 %collective-permute-start.5 = (bf16[128,512]{1,0:T(8,128)(2,1)S(1)}, bf16[128,512]{1,0:T(8,128)(2,1)S(1)}, u32[]{:S(2)}, u32[]{:S(2)}) collective-permute-start(bf16[128,512]{1,0:T(8,128)(2,1)S(1)} %get-tuple-element.34), channel_id=1, source_target_pairs={{0,1},{1,0},{2,3},{3,2},{4,5},{5,4},{6,7},{7,6},{8,9},{9,8},{10,11... | collective-permute-start | bytes 393224 | tf_op jit(solution)/shard_map/ppermute | solution.py:35
  13.5 1.5 %collective-permute-start.6 = (bf16[128,512]{1,0:T(8,128)(2,1)S(1)}, bf16[128,512]{1,0:T(8,128)(2,1)S(1)}, u32[]{:S(2)}, u32[]{:S(2)}) collective-permute-start(bf16[128,512]{1,0:T(8,128)(2,1)S(1)} %get-tuple-element.35), channel_id=1, source_target_pairs={{0,1},{1,0},{2,3},{3,2},{4,5},{5,4},{6,7},{7,6},{8,9},{9,8},{10,11... | collective-permute-start | bytes 393224 | tf_op jit(solution)/shard_map/ppermute | solution.py:35
  15.0 0.5 %collective-permute-start.4 = (bf16[128,512]{1,0:T(8,128)(2,1)S(1)}, bf16[128,512]{1,0:T(8,128)(2,1)S(1)}, u32[]{:S(2)}, u32[]{:S(2)}) collective-permute-start(bf16[128,512]{1,0:T(8,128)(2,1)S(1)} %get-tuple-element.30), channel_id=1, source_target_pairs={{0,1},{1,0},{2,3},{3,2},{4,5},{5,4},{6,7},{7,6},{8,9},{9,8},{10,11... | collective-permute-start | bytes 393224 | tf_op jit(solution)/shard_map/ppermute | solution.py:35
  15.6 0.7 %shard_map.60 = (bf16[128,512]{1,0:T(8,128)(2,1)S(1)}, bf16[128,512]{1,0:T(8,128)(2,1)S(1)}, bf16[128,512]{1,0:T(8,128)(2,1)S(1)}, bf16[128,512]{1,0:T(8,128)(2,1)S(1)}) custom-call(bf16[128,1024]{1,0:T(8,128)(2,1)S(1)} %get-tuple-element.28.a_ref, bf16[1024,4096]{1,0:T(8,128)(2,1)S(1)} %bitcast.1), custom_call_target="tpu_custom_call" | custom-call | flops 536870912 | bytes 1000000 | tf_op jit(solution)/shard_map/pallas_call | solution.py:239
  16.3 0.9 %collective-permute-done.7.refs_5_ = bf16[128,512]{1,0:T(8,128)(2,1)S(1)} collective-permute-done((bf16[128,512]{1,0:T(8,128)(2,1)S(1)}, bf16[128,512]{1,0:T(8,128)(2,1)S(1)}, u32[]{:S(2)}, u32[]{:S(2)}) %collective-permute-start.7) | collective-permute-done | bytes 131104 | tf_op jit(solution)/shard_map/ppermute | solution.py:35
  17.2 2.8 %collective-permute-done.5.refs_3_ = bf16[128,512]{1,0:T(8,128)(2,1)S(1)} collective-permute-done((bf16[128,512]{1,0:T(8,128)(2,1)S(1)}, bf16[128,512]{1,0:T(8,128)(2,1)S(1)}, u32[]{:S(2)}, u32[]{:S(2)}) %collective-permute-start.5) | collective-permute-done | bytes 131104 | tf_op jit(solution)/shard_map/ppermute | solution.py:35
  20.0 2.8 %collective-permute-done.6.refs_4_ = bf16[128,512]{1,0:T(8,128)(2,1)S(1)} collective-permute-done((bf16[128,512]{1,0:T(8,128)(2,1)S(1)}, bf16[128,512]{1,0:T(8,128)(2,1)S(1)}, u32[]{:S(2)}, u32[]{:S(2)}) %collective-permute-start.6) | collective-permute-done | bytes 131104 | tf_op jit(solution)/shard_map/ppermute | solution.py:35
  22.8 0.8 %shard_map.62.refs_2_ = bf16[128,2048]{1,0:T(8,128)(2,1)} custom-call(bf16[128,512]{1,0:T(8,128)(2,1)S(1)} %get-tuple-element.31.refs_0_, bf16[128,512]{1,0:T(8,128)(2,1)S(1)} %get-tuple-element.32.refs_1_, bf16[128,512]{1,0:T(8,128)(2,1)S(1)} %get-tuple-element.33.refs_2_, bf16[128,512]{1,0:T(8,128)(2,1)S(1)} %collective-permute-done.5.refs_3_, ...), custom_call_target="tpu_custom_call" | custom-call | flops 1000000 | bytes 1000000 | tf_op jit(solution)/shard_map/pallas_call | solution.py:275
  23.6 1.2 %collective-permute-done.4.refs_1_ = bf16[128,512]{1,0:T(8,128)(2,1)S(1)} collective-permute-done((bf16[128,512]{1,0:T(8,128)(2,1)S(1)}, bf16[128,512]{1,0:T(8,128)(2,1)S(1)}, u32[]{:S(2)}, u32[]{:S(2)}) %collective-permute-start.4) | collective-permute-done | bytes 131104 | tf_op jit(solution)/shard_map/ppermute | solution.py:35
  24.8 0.7 %shard_map.63 = bf16[128,2048]{1,0:T(8,128)(2,1)} custom-call(bf16[128,512]{1,0:T(8,128)(2,1)S(1)} %get-tuple-element.29.refs_0_, bf16[128,512]{1,0:T(8,128)(2,1)S(1)} %collective-permute-done.4.refs_1_, bf16[128,2048]{1,0:T(8,128)(2,1)} %shard_map.62.refs_2_), custom_call_target="tpu_custom_call", output_to_operand_aliasing={{}: (2, {})} | custom-call | flops 1000000 | bytes 1000000 | tf_op jit(solution)/shard_map/pallas_call | solution.py:275
  (3 shorter events, 0.0 us)
Async XLA Ops:
  0.9 2.1 %copy-start = (bf16[128,1024]{1,0:T(8,128)(2,1)S(1)}, bf16[128,1024]{1,0:T(8,128)(2,1)}, u32[]{:S(2)}) copy-start(bf16[128,1024]{1,0:T(8,128)(2,1)} %q_ref.5) | copy-start | bytes 786436
  0.9 2.1 %copy-start.1 = (s32[16]{0:T(128)S(1)}, s32[16]{0:T(128)}, u32[]{:S(2)}) copy-start(s32[16]{0:T(128)} %docs_ref.1) | copy-start | bytes 196
  0.9 8.7 %slice-start = ((s8[8388608]{0:T(1024)(128)(4,1)}), s8[4194304]{0:T(1024)(128)(4,1)S(1)}, s32[]{:S(2)}) async-start(s8[8388608]{0:T(1024)(128)(4,1)} %bitcast), calls=%async_computation | async-start | bytes 8388608
  0.9 8.7 %slice-start.1 = ((s8[8388608]{0:T(1024)(128)(4,1)}), s8[4194304]{0:T(1024)(128)(4,1)S(1)}, s32[]{:S(2)}) async-start(s8[8388608]{0:T(1024)(128)(4,1)} %bitcast), calls=%async_computation.1 | async-start | bytes 8388608
  0.9 7.3 %collective-permute-start.2 = (bf16[128,512]{1,0:T(8,128)(2,1)S(1)}, bf16[128,512]{1,0:T(8,128)(2,1)S(1)}, u32[]{:S(2)}, u32[]{:S(2)}) collective-permute-start(bf16[128,512]{1,0:T(8,128)(2,1)S(1)} %shard_map.55.kv_ref), channel_id=1, source_target_pairs={{0,4},{2,6},{4,8},{6,0},{8,2},{10,16},{12,14},{14,18},{16,10},{18,... | collective-permute-start | bytes 393224 | tf_op jit(solution)/shard_map/ppermute | solution.py:332
  1.0 7.2 %collective-permute-start.1 = (bf16[128,512]{1,0:T(8,128)(2,1)S(1)}, bf16[128,512]{1,0:T(8,128)(2,1)S(1)}, u32[]{:S(2)}, u32[]{:S(2)}) collective-permute-start(bf16[128,512]{1,0:T(8,128)(2,1)S(1)} %shard_map.55.kv_ref), channel_id=1, source_target_pairs={{0,2},{2,0},{4,6},{6,10},{8,12},{10,14},{12,16},{14,4},{16,20},{18... | collective-permute-start | bytes 393224 | tf_op jit(solution)/shard_map/ppermute | solution.py:332
  2.9 6.3 %collective-permute-start = (bf16[128,512]{1,0:T(8,128)(2,1)S(1)}, bf16[128,512]{1,0:T(8,128)(2,1)S(1)}, u32[]{:S(2)}, u32[]{:S(2)}) collective-permute-start(bf16[128,512]{1,0:T(8,128)(2,1)S(1)} %shard_map.55.kv_ref), channel_id=1, source_target_pairs={{0,2},{2,8},{4,6},{6,12},{8,10},{10,0},{12,4},{14,20},{16,18},{18,... | collective-permute-start | bytes 393224 | tf_op jit(solution)/shard_map/ppermute | solution.py:336
  8.2 1.4 %collective-permute-start.3 = (bf16[128,512]{1,0:T(8,128)(2,1)S(1)}, bf16[128,512]{1,0:T(8,128)(2,1)S(1)}, u32[]{:S(2)}, u32[]{:S(2)}) collective-permute-start(bf16[128,512]{1,0:T(8,128)(2,1)S(1)} %shard_map.57), channel_id=1, source_target_pairs={{0,2},{2,0},{4,6},{6,4},{8,10},{10,8},{12,14},{14,12},{16,18},{18,... | collective-permute-start | bytes 393224 | tf_op jit(solution)/shard_map/ppermute | solution.py:338
  10.8 6.4 %collective-permute-start.7 = (bf16[128,512]{1,0:T(8,128)(2,1)S(1)}, bf16[128,512]{1,0:T(8,128)(2,1)S(1)}, u32[]{:S(2)}, u32[]{:S(2)}) collective-permute-start(bf16[128,512]{1,0:T(8,128)(2,1)S(1)} %get-tuple-element.36), channel_id=1, source_target_pairs={{0,1},{1,0},{2,3},{3,2},{4,5},{5,4},{6,7},{7,6},{8,9},{9,8},{10,11... | collective-permute-start | bytes 393224 | tf_op jit(solution)/shard_map/ppermute | solution.py:35
  13.0 7.0 %collective-permute-start.5 = (bf16[128,512]{1,0:T(8,128)(2,1)S(1)}, bf16[128,512]{1,0:T(8,128)(2,1)S(1)}, u32[]{:S(2)}, u32[]{:S(2)}) collective-permute-start(bf16[128,512]{1,0:T(8,128)(2,1)S(1)} %get-tuple-element.34), channel_id=1, source_target_pairs={{0,1},{1,0},{2,3},{3,2},{4,5},{5,4},{6,7},{7,6},{8,9},{9,8},{10,11... | collective-permute-start | bytes 393224 | tf_op jit(solution)/shard_map/ppermute | solution.py:35
  13.5 9.3 %collective-permute-start.6 = (bf16[128,512]{1,0:T(8,128)(2,1)S(1)}, bf16[128,512]{1,0:T(8,128)(2,1)S(1)}, u32[]{:S(2)}, u32[]{:S(2)}) collective-permute-start(bf16[128,512]{1,0:T(8,128)(2,1)S(1)} %get-tuple-element.35), channel_id=1, source_target_pairs={{0,1},{1,0},{2,3},{3,2},{4,5},{5,4},{6,7},{7,6},{8,9},{9,8},{10,11... | collective-permute-start | bytes 393224 | tf_op jit(solution)/shard_map/ppermute | solution.py:35
  15.0 9.8 %collective-permute-start.4 = (bf16[128,512]{1,0:T(8,128)(2,1)S(1)}, bf16[128,512]{1,0:T(8,128)(2,1)S(1)}, u32[]{:S(2)}, u32[]{:S(2)}) collective-permute-start(bf16[128,512]{1,0:T(8,128)(2,1)S(1)} %get-tuple-element.30), channel_id=1, source_target_pairs={{0,1},{1,0},{2,3},{3,2},{4,5},{5,4},{6,7},{7,6},{8,9},{9,8},{10,11... | collective-permute-start | bytes 393224 | tf_op jit(solution)/shard_map/ppermute | solution.py:35
